TPU v7x, 32 devices: a whole 2x2x4 slice. The times are simulated.
32 devices in a mesh: batch: 8 (over z, x), tensor: 4 (over y, core).
Axes of the slice: x: 2, y: 2, z: 4, core: 2. Of those that a mesh axis runs over, the one named last changes fastest.
Arguments:
- hidden_in: bfloat16 [4096, 8192], P('batch', 'tensor'), may hold values from -1600 to 1600, as said below
- norm_gain: bfloat16 [8192], P('tensor'), may hold values from 0.099609375 to 1.8984375
- q_weight: bfloat16 [8192, 4096], P(('batch', 'tensor')), may hold values from -0.4087961 to 0.4087961, as said below
- k_weight: bfloat16 [8192, 512], P(('batch', 'tensor')), may hold values from -0.044194174 to 0.044194174, as said below
- v_weight: bfloat16 [8192, 512], P(('batch', 'tensor')), may hold values from -0.0625 to 0.0625
Outputs:
- head_out: bfloat16 [4096, 4096], P('batch', 'tensor')
Inputs may be any that keep to these rules, and one draw needn't show every extreme that they name: `hidden_in`: activations with independent scales over rows and over features. `q_weight`: A dense matrix. `k_weight`: A dense matrix.
All inputs are finite; a program needn't handle non-finite values.
Results may differ from a plain program's by a relative error of at most 0.008.
Values may be sent and summed in bfloat16 or wider, within the bound.
No kernel may reach another device: no remote copies, remote signals or barrier semaphores. Data moves between devices by JAX's collectives and lax.ppermute only.
A program may use at most 128 MiB of HBM per device.

v0:
```python
import jax
import jax.numpy as jnp
from jax import lax
from jax.sharding import PartitionSpec as P

HD = 128


def rotate_heads(field, head_size):
    seq_len = field.shape[0]
    heads = field.shape[1] // head_size
    shaped = field.reshape(seq_len, heads, head_size)
    half = head_size // 2
    position = jnp.arange(seq_len, dtype=jnp.float32)
    freqs = 500000.0 ** (-(jnp.arange(half, dtype=jnp.float32) * 2.0) / head_size)
    angles = position[:, None] * freqs[None, :]
    cosine = jnp.cos(angles)[:, None, :]
    sine = jnp.sin(angles)[:, None, :]
    first = shaped[..., :half]
    second = shaped[..., half:]
    turned = jnp.concatenate(
        [first * cosine - second * sine, second * cosine + first * sine], axis=-1
    )
    return turned.astype(jnp.bfloat16)


def on_device(hidden_in, norm_gain, q_weight, k_weight, v_weight):
    tensor_count = lax.axis_size("tensor")
    whole_rows, whole_gain = (
        lax.all_gather(hidden_in, "tensor", axis=1, tiled=True),
        lax.all_gather(norm_gain, "tensor", axis=0, tiled=True),
    )
    values = whole_rows.astype(jnp.float32)
    meansq = jnp.mean(values * values, axis=-1, keepdims=True)
    normed = (values * lax.rsqrt(meansq + 1e-05) * whole_gain.astype(jnp.float32)).astype(
        jnp.bfloat16
    )
    own_rows = q_weight.shape[0]
    kv_heads = k_weight.shape[1] // HD
    repeat_count = tensor_count // kv_heads
    q_send = q_weight.reshape(own_rows, tensor_count, -1)
    k_send = jnp.repeat(k_weight.reshape(own_rows, kv_heads, HD), repeat_count, axis=1)
    v_send = jnp.repeat(v_weight.reshape(own_rows, kv_heads, HD), repeat_count, axis=1)
    q_recv, k_recv, v_recv = (
        lax.all_to_all(q_send, "tensor", split_axis=1, concat_axis=0, tiled=True),
        lax.all_to_all(k_send, "tensor", split_axis=1, concat_axis=0, tiled=True),
        lax.all_to_all(v_send, "tensor", split_axis=1, concat_axis=0, tiled=True),
    )
    q_block = q_recv.reshape(q_recv.shape[0], q_recv.shape[2])
    k_block = k_recv.reshape(k_recv.shape[0], k_recv.shape[2])
    v_block = v_recv.reshape(v_recv.shape[0], v_recv.shape[2])
    seq_len = normed.shape[0]
    q_full, k_full, v_full = (
        lax.all_gather(q_block, "batch", axis=0, tiled=True),
        lax.all_gather(k_block, "batch", axis=0, tiled=True),
        lax.all_gather(v_block, "batch", axis=0, tiled=True),
    )
    q_lin = jnp.dot(normed, q_full, preferred_element_type=jnp.float32)
    k_lin = jnp.dot(normed, k_full, preferred_element_type=jnp.float32)
    v_lin = jnp.dot(normed, v_full, preferred_element_type=jnp.float32)
    q_rot = rotate_heads(q_lin, HD)
    k_rot = rotate_heads(k_lin, HD)[:, 0, :]
    v_val = v_lin.astype(jnp.bfloat16)
    scores = jnp.einsum("shd,td->hst", q_rot, k_rot, preferred_element_type=jnp.float32) / jnp.sqrt(
        jnp.float32(HD)
    )
    causal = jnp.tril(jnp.ones((seq_len, seq_len), dtype=bool))
    scores = jnp.where(causal[None], scores, jnp.float32(-1e30))
    top = jnp.max(scores, axis=-1, keepdims=True)
    expo = jnp.exp(scores - top)
    probs = (expo / jnp.sum(expo, axis=-1, keepdims=True)).astype(jnp.bfloat16)
    result = jnp.einsum("hst,td->shd", probs, v_val, preferred_element_type=jnp.float32)
    return result.astype(jnp.bfloat16).reshape(seq_len, -1)


def solution(mesh):
    placed = (
        P("batch", "tensor"),
        P("tensor"),
        P(("batch", "tensor"), None),
        P(("batch", "tensor"), None),
        P(("batch", "tensor"), None),
    )
    return jax.shard_map(
        on_device, mesh=mesh, in_specs=placed, out_specs=P("batch", "tensor"), check_vma=False
    )
```

profile of v0, /device:TPU:1, one launch (start us, length us, event | category | flops | bytes accessed | tf_op | source)
XLA Modules:
  0.0 441.2 jit_solution(16623019637303173179)
XLA Ops:
  6.5 0.0 all-gather.5.cloned.1.call-start
  6.5 0.7 all-gather.5.cloned.1.call-update
  7.3 0.0 copy-start
  7.3 0.0 all-gather.9.cloned.1.call-start
  7.3 1.1 copy.30
  8.4 9.1 %all_to_all.45 = bf16[256,4,128]{0,2,1:T(8,128)(2,1)S(1)} all-to-all(bf16[256,4,128]{0,2,1:T(8,128)(2,1)S(1)} %bitcast.57), channel_id=1, replica_groups=mesh['batch'=8,'tensor'=4] {'tensor'}, dimensions={1} | all-to-all | bytes 524288 | tf_op jit(solution)/shard_map/all_to_all | solution.py:46
  17.5 0.0 copy-start.1
  17.5 0.8 copy.31
  18.4 0.0 all-gather.9.cloned.1.call-update
  18.4 0.0 all-gather.11.cloned.1.call-start
  18.4 4.3 copy.32
  22.8 52.2 %all_to_all.46 = bf16[256,4,1024]{0,2,1:T(8,128)(2,1)S(1)} all-to-all(bf16[256,4,1024]{0,2,1:T(8,128)(2,1)} %bitcast.51), channel_id=1, replica_groups=mesh['batch'=8,'tensor'=4] {'tensor'}, dimensions={1} | all-to-all | bytes 4194304 | tf_op jit(solution)/shard_map/all_to_all | solution.py:45
  75.0 2.5 copy.33
  77.5 0.0 all-gather.11.cloned.1.call-update
  77.6 0.0 copy-done
  77.6 0.9 copy.28
  78.4 4.2 all-to-all-start
  82.6 0.0 all-gather.7.cloned.1.call-start
  82.6 0.0 copy-done.1
  82.6 10.0 %all_gather.16 = bf16[8192]{0:T(1024)(128)(2,1)S(1)} all-gather(bf16[2048]{0:T(1024)(128)(2,1)S(1)} %copy-done.1), channel_id=1, replica_groups=mesh['batch'=8,'tensor'=4] {'tensor'}, dimensions={0}, use_global_device_ids=true | all-gather | bytes 20480 | tf_op jit(solution)/shard_map/all_gather | solution.py:31
  92.7 0.1 iota_compare_fusion
  92.8 1.0 fusion.16
  93.7 0.0 all-to-all-done
  93.7 0.9 copy.29
  94.6 0.0 all-gather.7.cloned.1.call-update
  94.6 0.5 all-gather.5.cloned.1.call-done
  95.1 5.1 %fusion.1 = f32[512]{0:T(512)S(1)} fusion(bf16[512,8192]{1,0:T(8,128)(2,1)} %all-gather.5.cloned.1.call-done), kind=kLoop, calls=%fused_computation.3 | loop fusion | flops 12582400 | bytes 8390656 | tf_op jit(solution)/shard_map/reduce_sum | solution.py:34
  100.2 44.8 %all-gather.9.cloned.1.call-done = bf16[8192,128]{1,0:T(8,128)(2,1)} async-done(((bf16[1024,128]{1,0:T(8,128)(2,1)}), bf16[8192,128]{1,0:T(8,128)(2,1)}) %all-gather.9.cloned.1.call-update) | async-done | bytes 2097168 | tf_op jit(solution)/shard_map/all_gather | solution.py:55
  145.0 6.5 %convolution_bitcast_fusion.1 = f32[512,1,128]{0,2,1:T(8,128)S(1)} fusion(bf16[8192,128]{1,0:T(8,128)(2,1)} %all-gather.9.cloned.1.call-done, bf16[512,8192]{1,0:T(8,128)(2,1)} %all-gather.5.cloned.1.call-done, f32[8192]{0:T(1024)S(1)} %convert_element_type.27, f32[512]{0:T(512)S(1)} %add_rsqrt_fusion), kind=kOutput, calls=%fused_computation.18 | convolution fusion | flops 1090519040 | bytes 10782720 | tf_op jit(solution)/shard_map/dot_general | solution.py:59
  151.5 0.6 fusion.21
  152.1 222.0 %all-gather.11.cloned.1.call-done = bf16[8192,1024]{1,0:T(8,128)(2,1)} async-done(((bf16[1024,1024]{1,0:T(8,128)(2,1)}), bf16[8192,1024]{1,0:T(8,128)(2,1)}) %all-gather.11.cloned.1.call-update) | async-done | bytes 16777232 | tf_op jit(solution)/shard_map/all_gather | solution.py:54
  374.1 14.5 %convolution_bitcast_fusion = f32[64,8,8,128]{3,1,2,0:T(8,128)S(1)} fusion(bf16[8192,1024]{1,0:T(8,128)(2,1)} %all-gather.11.cloned.1.call-done, bf16[512,8192]{1,0:T(8,128)(2,1)} %all-gather.5.cloned.1.call-done, f32[8192]{0:T(1024)S(1)} %convert_element_type.27, f32[512]{0:T(512)S(1)} %add_rsqrt_fusion), kind=kOutput, calls=%fused_computation.16 | convolution fusion | flops 8606711808 | bytes 27297792 | tf_op jit(solution)/shard_map/dot_general | solution.py:58
  388.5 0.5 copy.47
  389.0 0.7 fusion.30
  389.7 0.8 subtract_convert_fusion
  390.5 1.3 fusion.11
  391.8 5.7 %fusion.31 = (f32[8,512]{1,0:T(8,128)S(1)}, f32[8,512,512]{1,2,0:T(8,128)}) fusion(f32[512,512,8]{1,0,2:T(8,128)S(1)} %fusion.11, pred[512,512]{0,1:T(8,128)(4,1)S(1)} %iota_compare_fusion), kind=kOutput, calls=%fused_computation.45 | output fusion | flops 12583423 | bytes 17055744 | tf_op jit(solution)/shard_map/sub | solution.py:70
  397.5 25.3 %all-gather.7.cloned.1.call-done = bf16[8192,128]{1,0:T(8,128)(2,1)} async-done(((bf16[1024,128]{1,0:T(8,128)(2,1)}), bf16[8192,128]{1,0:T(8,128)(2,1)}) %all-gather.7.cloned.1.call-update) | async-done | bytes 2097168 | tf_op jit(solution)/shard_map/all_gather | solution.py:56
  422.8 10.5 %fusion.9 = bf16[128,8,512]{2,0,1:T(8,128)(2,1)S(1)} fusion(f32[8,512,512]{1,2,0:T(8,128)} %get-tuple-element.14, f32[8,512]{1,0:T(8,128)S(1)} %get-tuple-element.13, bf16[8192,128]{1,0:T(8,128)(2,1)} %all-gather.7.cloned.1.call-done, bf16[512,8192]{1,0:T(8,128)(2,1)} %all-gather.5.cloned.1.call-done, f32[8192]{0:T(1024)S(1)} %convert_element_type.27, ...), kind=kOutput, calls=%fused_computation.17 | convolution fusion | flops 1632174080 | bytes 19974144 | tf_op jit(solution)/shard_map/hst,td->shd/dot_general | solution.py:72
  433.3 1.3 copy.39
  (3 shorter events, 0.0 us)
Async XLA Ops:
  6.5 88.6 %all-gather.5.cloned.1.call-start = ((), (), s32[]{:S(2)}) async-start(), calls=%async_computation.3 | async-start | bytes 10485760 | tf_op jit(solution)/shard_map/all_gather | solution.py:30
  7.3 70.3 %copy-start = (bf16[256,512]{1,0:T(8,128)(2,1)S(1)}, bf16[256,512]{1,0:T(8,128)(2,1)}, u32[]{:S(2)}) copy-start(bf16[256,512]{1,0:T(8,128)(2,1)} %param.9) | copy-start | bytes 786436
  7.3 137.8 %all-gather.9.cloned.1.call-start = ((), (), s32[]{:S(2)}) async-start(), calls=%async_computation.5 | async-start | bytes 2359296 | tf_op jit(solution)/shard_map/all_gather | solution.py:55
  17.5 65.1 %copy-start.1 = (bf16[2048]{0:T(1024)(128)(2,1)S(1)}, bf16[2048]{0:T(1024)(128)(2,1)}, u32[]{:S(2)}) copy-start(bf16[2048]{0:T(1024)(128)(2,1)} %param.6) | copy-start | bytes 12292
  18.4 355.7 %all-gather.11.cloned.1.call-start = ((), (), s32[]{:S(2)}) async-start(), calls=%async_computation.6 | async-start | bytes 18874368 | tf_op jit(solution)/shard_map/all_gather | solution.py:54
  78.4 15.3 %all-to-all-start = ((bf16[256,4,128]{0,2,1:T(8,128)(2,1)}), bf16[256,4,128]{0,2,1:T(8,128)(2,1)S(1)}, u32[]{:S(2)}, u32[]{:S(2)}) async-start(bf16[256,4,128]{0,2,1:T(8,128)(2,1)} %bitcast), calls=%async_computation | async-start | bytes 524288 | tf_op jit(solution)/shard_map/all_to_all | solution.py:47
  82.6 340.2 %all-gather.7.cloned.1.call-start = ((), (), s32[]{:S(2)}) async-start(), calls=%async_computation.4 | async-start | bytes 2359296 | tf_op jit(solution)/shard_map/all_gather | solution.py:56
Sparse Core Ops, SparseCore 0:
  8.9 86.1 all-gather.4
  97.2 47.7 all-gather.8
  147.2 226.8 all-gather.10
  376.0 46.7 all-gather.6
where the time goes:
time: 443 us; the launch traced here: 441 us
  waiting for transfers between devices  293 us (66%)
  blocking collectives  71.4 us (16%)
  matrix products  32.8 us (7%)
  other arithmetic  13.3 us (3%)
  between operations  13.2 us (3%)
  local copies, waits for them, and re-layouts  13 us (3%)
    all_gather x1, waiting for transfers between devices, on_device(): lax.all_gather(q_block, 'batch', axis=0, tiled=True)  222 us
    all_to_all x1, blocking collectives, on_device(): lax.all_to_all(q_send, 'tensor', split_axis=1, concat_axis=0, tiled=True)  52.2 us
    all_gather x1, waiting for transfers between devices, on_device(): lax.all_gather(k_block, 'batch', axis=0, tiled=True)  44.8 us
    all_gather x1, waiting for transfers between devices, on_device(): lax.all_gather(v_block, 'batch', axis=0, tiled=True)  25.3 us
    dot_general x1, matrix products, on_device(): q_lin = jnp.dot(normed, q_full, preferred_element_type=jnp.float32)  14.5 us
    dot_general x1, matrix products, on_device(): jnp.einsum('hst,td->shd', probs, v_val, preferred_element_type=jnp.float32)  10.5 us
    all_gather x1, blocking collectives, on_device(): lax.all_gather(norm_gain, 'tensor', axis=0, tiled=True)  10 us
    all_to_all x1, blocking collectives, on_device(): lax.all_to_all(k_send, 'tensor', split_axis=1, concat_axis=0, tiled=True)  9.09 us
  transfers between devices with their start and end apart: 5, of which 4 were waited for; matrix products, arithmetic and copies ran while one was open for 11% of the time, Pallas kernels for 0%

commit v1 on v0

v1 whole, which is shorter than its diff:
```python
import jax
import jax.numpy as jnp
from jax import lax
from jax.sharding import PartitionSpec as P

HD = 128
AXES = ("batch", "tensor")


def rotary_tables(seq_len, head_size):
    half = head_size // 2
    position = jnp.arange(seq_len, dtype=jnp.float32)
    freqs = 500000.0 ** (-(jnp.arange(half, dtype=jnp.float32) * 2.0) / head_size)
    angles = position[:, None] * freqs[None, :]
    return jnp.cos(angles), jnp.sin(angles)


def rotate_heads(field, tables):
    seq_len = field.shape[0]
    shaped = field.reshape(seq_len, -1, HD)
    half = HD // 2
    cosine = tables[0][:, None, :]
    sine = tables[1][:, None, :]
    first = shaped[..., :half]
    second = shaped[..., half:]
    turned = jnp.concatenate(
        [first * cosine - second * sine, second * cosine + first * sine], axis=-1
    )
    return turned.astype(jnp.bfloat16)


def attend(q_rot, k_rot, v_val):
    seq_len = q_rot.shape[0]
    scores = jnp.einsum("shd,td->hst", q_rot, k_rot, preferred_element_type=jnp.float32) / jnp.sqrt(
        jnp.float32(HD)
    )
    causal = jnp.tril(jnp.ones((seq_len, seq_len), dtype=bool))
    scores = jnp.where(causal[None], scores, jnp.float32(-1e30))
    top = jnp.max(scores, axis=-1, keepdims=True)
    expo = jnp.exp(scores - top)
    probs = (expo / jnp.sum(expo, axis=-1, keepdims=True)).astype(jnp.bfloat16)
    result = jnp.einsum("hst,td->shd", probs, v_val, preferred_element_type=jnp.float32)
    return result.astype(jnp.bfloat16).reshape(seq_len, -1)


def gathered_plan(hidden_in, norm_gain, q_weight, k_weight, v_weight):
    tensor_count = lax.axis_size("tensor")
    whole_rows, whole_gain = (
        lax.all_gather(hidden_in, "tensor", axis=1, tiled=True),
        lax.all_gather(norm_gain, "tensor", axis=0, tiled=True),
    )
    values = whole_rows.astype(jnp.float32)
    meansq = jnp.mean(values * values, axis=-1, keepdims=True)
    normed = (values * lax.rsqrt(meansq + 1e-05) * whole_gain.astype(jnp.float32)).astype(
        jnp.bfloat16
    )
    own_rows = q_weight.shape[0]
    kv_heads = k_weight.shape[1] // HD
    repeat_count = tensor_count // kv_heads
    q_send = q_weight.reshape(own_rows, tensor_count, -1)
    k_send = jnp.repeat(k_weight.reshape(own_rows, kv_heads, HD), repeat_count, axis=1)
    v_send = jnp.repeat(v_weight.reshape(own_rows, kv_heads, HD), repeat_count, axis=1)
    sends = jnp.concatenate([k_send, v_send, q_send], axis=2)
    recv = lax.all_to_all(sends, "tensor", split_axis=1, concat_axis=0, tiled=True)
    full = lax.all_gather(recv.reshape(-1, recv.shape[2]), "batch", axis=0, tiled=True)
    lin = jnp.dot(normed, full, preferred_element_type=jnp.float32)
    tables = rotary_tables(normed.shape[0], HD)
    k_rot = rotate_heads(lin[:, :HD], tables)[:, 0, :]
    v_val = lin[:, HD : 2 * HD].astype(jnp.bfloat16)
    return attend(rotate_heads(lin[:, 2 * HD :], tables), k_rot, v_val)


def move(value, route):
    pairs = []
    for flat in range(32):
        to = route(flat >> 3, flat >> 2 & 1, flat >> 1 & 1, flat & 1)
        if to is not None:
            pairs.append((flat, ((to[0] * 2 + to[1]) * 2 + to[2]) * 2 + to[3]))
    return lax.ppermute(value, AXES, pairs)


def swap_x(z, x, y, c):
    return z, 1 - x, y, c


def swap_y(z, x, y, c):
    return z, x, 1 - y, c


def swap_xy(z, x, y, c):
    return z, 1 - x, 1 - y, c


def swap_c(z, x, y, c):
    return z, x, y, 1 - c


def swap_near(z, x, y, c):
    return z ^ 1, x, y, c


def swap_far(z, x, y, c):
    return z ^ 2, x, y, c


def pick(pair, index):
    return lax.dynamic_index_in_dim(pair, index, 0, keepdims=False)


CHUNKS = ((0, 2), (2, 4), (4, 6), (6, 8))


def split_plan(hidden_in, norm_gain, q_weight, k_weight, v_weight):
    flat = lax.axis_index(AXES)
    z, x, y, c = flat >> 3, flat >> 2 & 1, flat >> 1 & 1, flat & 1
    odd = z & 1
    home = c == odd
    rows = hidden_in.shape[0]
    own = q_weight.shape[0]
    q_cols = q_weight.shape[1] // 4

    def columns(group, lo, hi):
        take = lax.dynamic_slice_in_dim
        q_part = take(q_weight, group * q_cols + lo * HD, (hi - lo) * HD, 1)
        if lo > 0:
            return q_part
        return jnp.concatenate(
            [take(k_weight, group * HD, HD, 1), take(v_weight, group * HD, HD, 1), q_part], axis=1
        )

    near, far = [], []
    for lo, hi in CHUNKS:
        mine = columns(2 * y + x, lo, hi)
        from_x = move(columns(2 * y + 1 - x, lo, hi), swap_x)
        from_y = move(columns(2 * (1 - y) + x, lo, hi), swap_y)
        from_xy = move(columns(2 * (1 - y) + 1 - x, lo, hi), swap_xy)
        block = jnp.zeros((4,) + mine.shape, mine.dtype)
        for piece, px, py in (
            (mine, x, y), (from_x, 1 - x, y), (from_y, x, 1 - y), (from_xy, 1 - x, 1 - y)
        ):
            block = lax.dynamic_update_index_in_dim(block, piece, 2 * px + py, 0)
        block = block.reshape(4 * own, -1)
        near.append(block)
        far.append(move(block, swap_far))

    values = hidden_in.astype(jnp.float32)
    total = jnp.sum(values * values, axis=-1)
    total = total + move(total, swap_c)
    total = total + move(total, swap_y)
    scale = lax.rsqrt(total / (4 * hidden_in.shape[1]) + 1e-05)
    normed = (values * scale[:, None] * norm_gain.astype(jnp.float32)[None, :]).astype(jnp.bfloat16)

    halves = normed.reshape(rows, 4, 2, own).transpose(2, 0, 1, 3).reshape(2, rows, 4 * own)
    half_same, half_other = pick(halves, odd), pick(halves, 1 - odd)

    def to_same_parity(z, x, y, c):
        return (z, x, y, 1 - c) if c == z & 1 else (z ^ 1, x, y, c)

    def to_other_plane(z, x, y, c):
        return None if c == z & 1 else (z ^ 1, x, y, 1 - c)

    got_one = move(half_other, to_same_parity)
    got_two = move(half_same, to_other_plane)
    here = jnp.stack(
        [jnp.where(home, half_same, got_one), jnp.where(home, got_one, got_two)]
    )
    here_x = move(here, swap_x)
    here_y = move(here, swap_y)
    here_xy = jnp.stack([move(here_x[0], swap_y), move(here_y[1], swap_x)])
    by_y = (jnp.stack([here, here_x]), jnp.stack([here_y, here_xy]))
    straight = y == z >> 1
    x_near = jnp.where(straight, by_y[0], by_y[1]).reshape(4 * rows, -1)
    x_far = jnp.where(straight, by_y[1], by_y[0]).reshape(4 * rows, -1)

    tables = rotary_tables(rows, HD)
    keep = c ^ x
    results = []
    k_rot = v_val = None
    for j, (lo, hi) in enumerate(CHUNKS):
        part = jnp.dot(x_near, near[j], preferred_element_type=jnp.float32)
        part = part + jnp.dot(x_far, far[j], preferred_element_type=jnp.float32)
        part = part.reshape(2, 2, rows, -1)
        both = pick(part, keep) + move(pick(part, 1 - keep), swap_c)
        sent = both[1] if lo == 0 else both[1].astype(jnp.float16)
        lin = both[0] + move(sent, swap_near).astype(jnp.float32)
        if lo == 0:
            k_rot = rotate_heads(lin[:, :HD], tables)[:, 0, :]
            v_val = lin[:, HD : 2 * HD].astype(jnp.bfloat16)
            lin = lin[:, 2 * HD :]
        out = attend(rotate_heads(lin, tables), k_rot, v_val)

        def to_owner(z, x, y, c):
            return None if x == c else (z, c, y, x)

        results.append(jnp.where(x == c, out, move(out, to_owner)))
    return jnp.concatenate(results, axis=1)


def solution(mesh):
    placed = (
        P("batch", "tensor"),
        P("tensor"),
        P(("batch", "tensor"), None),
        P(("batch", "tensor"), None),
        P(("batch", "tensor"), None),
    )
    plan = split_plan if dict(mesh.shape) == {"batch": 8, "tensor": 4} else gathered_plan
    return jax.shard_map(
        plan, mesh=mesh, in_specs=placed, out_specs=P("batch", "tensor"), check_vma=False
    )
```

time: 443 us -> 335 us (0.76)
  waiting for transfers between devices: 293 us -> 174 us
  blocking collectives: 71.4 us -> 0 us
  starting transfers between devices: 4.28 us -> 48.1 us
  local copies, waits for them, and re-layouts: 13 us -> 51.5 us
  other arithmetic: 13.3 us -> 29.2 us
  between operations: 13.2 us -> 0.91 us
    all_gather x4 -> x0, waiting for transfers between devices: 293 us -> none  [the longest x1 222 us: on_device(): lax.all_gather(q_block, 'batch', axis=0, tiled=True)]
    ppermute x0 -> x36, waiting for transfers between devices: none -> 174 us  [move(): return lax.ppermute(value, AXES, pairs)]
    all_to_all x2 -> x0, blocking collectives: 61.3 us -> none  [the longest x1 52.2 us: on_device(): lax.all_to_all(q_send, 'tensor', split_axis=1, concat_axis=0, tiled=True)]
    ppermute x0 -> x36, starting transfers between devices: none -> 48.1 us  [move(): return lax.ppermute(value, AXES, pairs)]
    dynamic_slice x0 -> x13, local copies, waits for them, and re-layouts: none -> 16.5 us  [the longest x11 12.2 us: pick(): return lax.dynamic_index_in_dim(pair, index, 0, keepdims=False)]
    dynamic_update_slice x0 -> x15, local copies, waits for them, and re-layouts: none -> 10.5 us  [split_plan(): block = lax.dynamic_update_index_in_dim(block, piece, 2 * px + py, 0)]
    all_gather x1 -> x0, blocking collectives: 10 us -> none  [on_device(): lax.all_gather(norm_gain, 'tensor', axis=0, tiled=True)]
    add x0 -> x9, other arithmetic: none -> 9.88 us  [the longest x4 6.45 us: split_plan(): both = pick(part, keep) + move(pick(part, 1 - keep), swap_c)]
  transfers between devices with their start and end apart: 5 -> 36, of which waited for: 4 -> 13; matrix products, arithmetic and copies ran while one was open for 11% -> 28% of each run, Pallas kernels for 0% -> 0%
where the time goes in v1:
time: 335 us; the launch traced here: 334 us
  waiting for transfers between devices  174 us (52%)
  local copies, waits for them, and re-layouts  51.5 us (15%)
  starting transfers between devices  48.1 us (14%)
  matrix products  30.4 us (9%)
  other arithmetic  29.2 us (9%)
    ppermute x36, waiting for transfers between devices, move(): return lax.ppermute(value, AXES, pairs)  174 us
    ppermute x36, starting transfers between devices, move(): return lax.ppermute(value, AXES, pairs)  48.1 us
    unnamed x81, local copies, waits for them, and re-layouts  13.8 us
    dynamic_slice x11, local copies, waits for them, and re-layouts, pick(): return lax.dynamic_index_in_dim(pair, index, 0, keepdims=False)  12.2 us
    dynamic_update_slice x15, local copies, waits for them, and re-layouts, split_plan(): block = lax.dynamic_update_index_in_dim(block, piece, 2 * px + py, 0)  10.5 us
    dot_general x4, matrix products, split_plan(): part = part + jnp.dot(x_far, far[j], preferred_element_type=jnp.float32)  9.8 us
    dot_general x4, matrix products, split_plan(): part = jnp.dot(x_near, near[j], preferred_element_type=jnp.float32)  8.61 us
  transfers between devices with their start and end apart: 36, of which 13 were waited for; matrix products, arithmetic and copies ran while one was open for 28% of the time, Pallas kernels for 0%

profile of v1, /device:TPU:1, one launch (start us, length us, event | category | flops | bytes accessed | tf_op | source)
XLA Modules:
  0.0 333.8 jit_solution(16124168435884496094)
XLA Ops:
  0.0 2.9 copy.86
  4.6 2.4 collective-permute-start.1
  9.4 4.8 %collective-permute-start.3 = (bf16[512,1024]{1,0:T(8,128)(2,1)S(1)}, bf16[512,1024]{1,0:T(8,128)(2,1)}, u32[]{:S(2)}, u32[]{:S(2)}) collective-permute-start(bf16[512,1024]{1,0:T(8,128)(2,1)S(1)} %bitcast.220), channel_id=1, source_target_pairs={{1,8},{3,10},{5,12},{7,14},{8,1},{10,3},{12,5},{14,7},{17,24},{19,... | collective-permute-start | bytes 3145736 | tf_op jit(solution)/shard_map/ppermute | solution.py:79
  14.8 2.6 constant_dynamic-slice_fusion.12
  23.1 1.8 constant_dynamic-slice_fusion.16
  27.1 10.0 %collective-permute-done.2 = bf16[512,1024]{1,0:T(8,128)(2,1)S(1)} collective-permute-done((bf16[512,1024]{1,0:T(8,128)(2,1)S(1)}, bf16[512,1024]{1,0:T(8,128)(2,1)S(1)}, u32[]{:S(2)}, u32[]{:S(2)}) %collective-permute-start.2) | collective-permute-done | bytes 1048608 | tf_op jit(solution)/shard_map/ppermute | solution.py:79
  38.5 1.6 fusion.146
  41.5 1.7 fusion.48
  45.3 1.6 bitcast_dynamic-update-slice_fusion.14
  49.9 40.5 %collective-permute-done.22 = bf16[256,256]{1,0:T(8,128)(2,1)S(1)} collective-permute-done((bf16[256,256]{1,0:T(8,128)(2,1)}, bf16[256,256]{1,0:T(8,128)(2,1)S(1)}, u32[]{:S(2)}, u32[]{:S(2)}) %collective-permute-start.22) | collective-permute-done | bytes 131104 | tf_op jit(solution)/shard_map/ppermute | solution.py:79
  93.7 1.8 collective-permute-done.23
  96.5 3.7 %collective-permute-start.16 = (bf16[256,256]{1,0:T(8,128)(2,1)S(1)}, bf16[256,256]{1,0:T(8,128)(2,1)S(1)}, u32[]{:S(2)}, u32[]{:S(2)}) collective-permute-start(bf16[256,256]{1,0:T(8,128)(2,1)S(1)} %copy-done.32), channel_id=1, source_target_pairs={{0,2},{1,3},{2,0},{3,1},{4,6},{5,7},{6,4},{7,5},{8,10},{9,11},{10,... | collective-permute-start | bytes 393224 | tf_op jit(solution)/shard_map/ppermute | solution.py:79
  103.2 1.5 collective-permute-start.9
  108.5 2.2 collective-permute-start.10
  111.4 2.3 collective-permute-start.32
  115.2 23.3 %collective-permute-done.10 = bf16[256,512]{1,0:T(8,128)(2,1)S(1)} collective-permute-done((bf16[256,512]{1,0:T(8,128)(2,1)S(1)}, bf16[256,512]{1,0:T(8,128)(2,1)S(1)}, u32[]{:S(2)}, u32[]{:S(2)}) %collective-permute-start.10) | collective-permute-done | bytes 262176 | tf_op jit(solution)/shard_map/ppermute | solution.py:79
  138.5 2.0 collective-permute-start.18
  141.8 2.8 broadcast_select_fusion.1
  144.6 37.0 %collective-permute-done.32 = bf16[1024,256]{1,0:T(8,128)(2,1)S(1)} collective-permute-done((bf16[1024,256]{1,0:T(8,128)(2,1)S(1)}, bf16[1024,256]{1,0:T(8,128)(2,1)S(1)}, u32[]{:S(2)}, u32[]{:S(2)}) %collective-permute-start.32) | collective-permute-done | bytes 524320 | tf_op jit(solution)/shard_map/ppermute | solution.py:79
  184.2 8.6 %collective-permute-done.25 = bf16[1024,256]{1,0:T(8,128)(2,1)S(1)} collective-permute-done((bf16[1024,256]{1,0:T(8,128)(2,1)S(1)}, bf16[1024,256]{1,0:T(8,128)(2,1)S(1)}, u32[]{:S(2)}, u32[]{:S(2)}) %collective-permute-start.25) | collective-permute-done | bytes 524320 | tf_op jit(solution)/shard_map/ppermute | solution.py:79
  198.3 2.0 collective-permute-start.33
  201.6 25.0 %collective-permute-done.11 = bf16[1024,512]{1,0:T(8,128)(2,1)} collective-permute-done((bf16[1024,512]{1,0:T(8,128)(2,1)}, bf16[1024,512]{1,0:T(8,128)(2,1)}, u32[]{:S(2)}, u32[]{:S(2)}) %collective-permute-start.11) | collective-permute-done | bytes 1048608 | tf_op jit(solution)/shard_map/ppermute | solution.py:79
  226.7 4.9 %fusion.167 = f32[2048,512]{1,0:T(8,128)S(1)} fusion(bf16[2048,1024]{1,0:T(8,128)(2,1)} %bitcast.216, bf16[1024,512]{1,0:T(8,128)(2,1)} %collective-permute-done.11), kind=kOutput, calls=%fused_computation.211 | convolution fusion | flops 2147483648 | bytes 9437184 | tf_op jit(solution)/shard_map/dot_general | solution.py:181
  231.6 3.6 %convolution_add_fusion = f32[2048,512]{1,0:T(8,128)S(1)} fusion(f32[2048,512]{1,0:T(8,128)S(1)} %fusion.167, bf16[2048,1024]{1,0:T(8,128)(2,1)S(1)} %bitcast.207, bf16[1024,512]{1,0:T(8,128)(2,1)} %bitcast.20), kind=kOutput, calls=%fused_computation.13 | convolution fusion | flops 2148532224 | bytes 13631488 | tf_op jit(solution)/shard_map/dot_general | solution.py:180
  235.2 1.6 dynamic-slice_bitcast_fusion
  236.8 1.5 copy-done.4
  239.6 2.3 fusion.168
  241.9 2.4 convolution_add_fusion.3
  244.2 2.8 copy.113
  252.5 1.5 bitcast_add_fusion.1
  254.2 1.4 bitcast_add_fusion.2
  257.1 1.4 bitcast_add_fusion.3
  259.6 2.2 collective-permute-done.34
  261.9 2.1 bitcast_add_fusion
  265.2 2.3 collective-permute-done.27
  269.0 2.0 copy.139
  272.0 1.8 fusion.149
  273.8 2.0 copy.137
  279.9 15.7 %collective-permute-done.13 = f32[512,512]{1,0:T(8,128)} collective-permute-done((f32[512,512]{1,0:T(8,128)}, f32[512,512]{1,0:T(8,128)}, u32[]{:S(2)}, u32[]{:S(2)}) %collective-permute-start.13) | collective-permute-done | bytes 1048608 | tf_op jit(solution)/shard_map/ppermute | solution.py:79
  299.9 3.4 %subtract_convert_fusion.3 = (bf16[512,2,64]{2,0,1:T(8,128)(2,1)S(1)}, bf16[512,2,64]{2,0,1:T(8,128)(2,1)}, bf16[512,2,64]{2,0,1:T(8,128)(2,1)}, bf16[512,2,64]{...) fusion(f32[512,2,64]{2,0,1:T(8,128)} %copy.134, ...), kind=kLoop, calls=%fused_computation.81 | loop fusion | flops 2097152 | bytes 3407872 | tf_op jit(solution)/shard_map/convert.9
  303.3 2.0 fusion.160
  306.7 3.2 collective-permute-start.14
  312.4 2.6 collective-permute-start.21
  317.4 3.2 collective-permute-start.28
  320.7 2.0 fusion.151
  322.7 2.2 convolution_convert_fusion
  325.0 2.4 collective-permute-start.35
  327.5 5.2 %collective-permute-done.35 = bf16[512,256]{1,0:T(8,128)(2,1)S(1)} collective-permute-done((bf16[512,256]{1,0:T(8,128)(2,1)S(1)}, bf16[512,256]{1,0:T(8,128)(2,1)S(1)}, u32[]{:S(2)}, u32[]{:S(2)}) %collective-permute-start.35) | collective-permute-done | bytes 262176 | tf_op jit(solution)/shard_map/ppermute | solution.py:79
  (204 shorter events, 73.2 us)
Async XLA Ops:
  3.4 1.2 collective-permute-start
  4.6 3.4 %collective-permute-start.1 = (f32[512]{0:T(512)S(1)}, f32[512]{0:T(512)S(1)}, u32[]{:S(2)}, u32[]{:S(2)}) collective-permute-start(f32[512]{0:T(512)S(1)} %add.288), channel_id=1, source_target_pairs={{0,2},{1,3},{2,0},{3,1},{4,6},{5,7},{6,4},{7,5},{8,10},{9,11},{10,... | collective-permute-start | bytes 6152 | tf_op jit(solution)/shard_map/ppermute | solution.py:79
  9.4 17.8 %collective-permute-start.3 = (bf16[512,1024]{1,0:T(8,128)(2,1)S(1)}, bf16[512,1024]{1,0:T(8,128)(2,1)}, u32[]{:S(2)}, u32[]{:S(2)}) collective-permute-start(bf16[512,1024]{1,0:T(8,128)(2,1)S(1)} %bitcast.220), channel_id=1, source_target_pairs={{1,8},{3,10},{5,12},{7,14},{8,1},{10,3},{12,5},{14,7},{17,24},{19,... | collective-permute-start | bytes 3145736 | tf_op jit(solution)/shard_map/ppermute | solution.py:79
  14.7 22.4 %collective-permute-start.2 = (bf16[512,1024]{1,0:T(8,128)(2,1)S(1)}, bf16[512,1024]{1,0:T(8,128)(2,1)S(1)}, u32[]{:S(2)}, u32[]{:S(2)}) collective-permute-start(bf16[512,1024]{1,0:T(8,128)(2,1)S(1)} %bitcast.229), channel_id=1, source_target_pairs={{0,1},{1,9},{2,3},{3,11},{4,5},{5,13},{6,7},{7,15},{8,0},{9,8},{10... | collective-permute-start | bytes 3145736 | tf_op jit(solution)/shard_map/ppermute | solution.py:79
  17.4 31.3 %collective-permute-start.29 = (bf16[256,256]{1,0:T(8,128)(2,1)}, bf16[256,256]{1,0:T(8,128)(2,1)}, u32[]{:S(2)}, u32[]{:S(2)}) collective-permute-start(bf16[256,256]{1,0:T(8,128)(2,1)} %get-tuple-element.10), channel_id=1, source_target_pairs={{0,4},{1,5},{2,6},{3,7},{4,0},{5,1},{6,2},{7,3},{8,12},{9,13},{10,... | collective-permute-start | bytes 393224 | tf_op jit(solution)/shard_map/ppermute | solution.py:79
  18.6 73.0 %collective-permute-start.30 = (bf16[256,256]{1,0:T(8,128)(2,1)}, bf16[256,256]{1,0:T(8,128)(2,1)}, u32[]{:S(2)}, u32[]{:S(2)}) collective-permute-start(bf16[256,256]{1,0:T(8,128)(2,1)} %get-tuple-element.21), channel_id=1, source_target_pairs={{0,2},{1,3},{2,0},{3,1},{4,6},{5,7},{6,4},{7,5},{8,10},{9,11},{10,... | collective-permute-start | bytes 393224 | tf_op jit(solution)/shard_map/ppermute | solution.py:79
  19.9 76.6 %collective-permute-start.31 = (bf16[256,256]{1,0:T(8,128)(2,1)}, bf16[256,256]{1,0:T(8,128)(2,1)}, u32[]{:S(2)}, u32[]{:S(2)}) collective-permute-start(bf16[256,256]{1,0:T(8,128)(2,1)} %get-tuple-element.20), channel_id=1, source_target_pairs={{0,6},{1,7},{2,4},{3,5},{4,2},{5,3},{6,0},{7,1},{8,14},{9,15},{10,... | collective-permute-start | bytes 393224 | tf_op jit(solution)/shard_map/ppermute | solution.py:79
  40.2 7.8 %copy-start.18 = (bf16[256,128]{1,0:T(8,128)(2,1)S(1)}, bf16[256,128]{1,0:T(8,128)(2,1)}, u32[]{:S(2)}) copy-start(bf16[256,128]{1,0:T(8,128)(2,1)} %get-tuple-element.67) | copy-start | bytes 196612
  40.2 8.8 %copy-start.12 = (bf16[4,256,256]{2,1,0:T(8,128)(2,1)S(1)}, bf16[4,256,256]{2,1,0:T(8,128)(2,1)}, u32[]{:S(2)}) copy-start(bf16[4,256,256]{2,1,0:T(8,128)(2,1)} %copy-done.11) | copy-start | bytes 1572868
  40.2 51.5 %copy-start.14 = (bf16[4,256,256]{2,1,0:T(8,128)(2,1)S(1)}, bf16[4,256,256]{2,1,0:T(8,128)(2,1)}, u32[]{:S(2)}) copy-start(bf16[4,256,256]{2,1,0:T(8,128)(2,1)} %copy-done.13) | copy-start | bytes 1572868
  40.2 63.0 %collective-permute-start.4 = (bf16[2,512,1024]{2,1,0:T(8,128)(2,1)}, bf16[2,512,1024]{2,1,0:T(8,128)(2,1)}, u32[]{:S(2)}, u32[]{:S(2)}) collective-permute-start(bf16[2,512,1024]{2,1,0:T(8,128)(2,1)} %get-tuple-element.27), channel_id=1, source_target_pairs={{0,4},{1,5},{2,6},{3,7},{4,0},{5,1},{6,2},{7,3},{8,12},{9,13},{10,... | collective-permute-start | bytes 6291464 | tf_op jit(solution)/shard_map/ppermute | solution.py:79
  41.5 59.7 %copy-start.31 = (bf16[256,256]{1,0:T(8,128)(2,1)S(1)}, bf16[256,256]{1,0:T(8,128)(2,1)}, u32[]{:S(2)}) copy-start(bf16[256,256]{1,0:T(8,128)(2,1)} %get-tuple-element.9) | copy-start | bytes 393220
  43.2 62.8 %collective-permute-start.5 = (bf16[2,512,1024]{2,1,0:T(8,128)(2,1)}, bf16[2,512,1024]{2,1,0:T(8,128)(2,1)}, u32[]{:S(2)}, u32[]{:S(2)}) collective-permute-start(bf16[2,512,1024]{2,1,0:T(8,128)(2,1)} %get-tuple-element.27), channel_id=1, source_target_pairs={{0,2},{1,3},{2,0},{3,1},{4,6},{5,7},{6,4},{7,5},{8,10},{9,11},{10,... | collective-permute-start | bytes 6291464 | tf_op jit(solution)/shard_map/ppermute | solution.py:79
  46.9 44.8 %copy-start.34 = (bf16[256,256]{1,0:T(8,128)(2,1)S(1)}, bf16[256,256]{1,0:T(8,128)(2,1)}, u32[]{:S(2)}) copy-start(bf16[256,256]{1,0:T(8,128)(2,1)} %get-tuple-element.11) | copy-start | bytes 393220
  46.9 48.6 %copy-start.33 = (bf16[256,256]{1,0:T(8,128)(2,1)S(1)}, bf16[256,256]{1,0:T(8,128)(2,1)}, u32[]{:S(2)}) copy-start(bf16[256,256]{1,0:T(8,128)(2,1)} %get-tuple-element.15) | copy-start | bytes 393220
  46.9 49.6 %copy-start.32 = (bf16[256,256]{1,0:T(8,128)(2,1)S(1)}, bf16[256,256]{1,0:T(8,128)(2,1)}, u32[]{:S(2)}) copy-start(bf16[256,256]{1,0:T(8,128)(2,1)} %get-tuple-element.14) | copy-start | bytes 393220
  46.9 54.5 %copy-start.22 = (bf16[256,512]{1,0:T(8,128)(2,1)S(1)}, bf16[256,512]{1,0:T(8,128)(2,1)}, u32[]{:S(2)}) copy-start(bf16[256,512]{1,0:T(8,128)(2,1)} %pad_maximum_fusion.4) | copy-start | bytes 786436
  46.9 56.3 %copy-start.21 = (bf16[256,512]{1,0:T(8,128)(2,1)S(1)}, bf16[256,512]{1,0:T(8,128)(2,1)}, u32[]{:S(2)}) copy-start(bf16[256,512]{1,0:T(8,128)(2,1)} %pad_maximum_fusion.5) | copy-start | bytes 786436
  48.7 41.7 %collective-permute-start.22 = (bf16[256,256]{1,0:T(8,128)(2,1)}, bf16[256,256]{1,0:T(8,128)(2,1)S(1)}, u32[]{:S(2)}, u32[]{:S(2)}) collective-permute-start(bf16[256,256]{1,0:T(8,128)(2,1)} %get-tuple-element.13), channel_id=1, source_target_pairs={{0,4},{1,5},{2,6},{3,7},{4,0},{5,1},{6,2},{7,3},{8,12},{9,13},{10,... | collective-permute-start | bytes 393224 | tf_op jit(solution)/shard_map/ppermute | solution.py:79
  90.4 5.1 %collective-permute-start.23 = (bf16[256,256]{1,0:T(8,128)(2,1)}, bf16[256,256]{1,0:T(8,128)(2,1)S(1)}, u32[]{:S(2)}, u32[]{:S(2)}) collective-permute-start(bf16[256,256]{1,0:T(8,128)(2,1)} %get-tuple-element.12), channel_id=1, source_target_pairs={{0,2},{1,3},{2,0},{3,1},{4,6},{5,7},{6,4},{7,5},{8,10},{9,11},{10,... | collective-permute-start | bytes 393224 | tf_op jit(solution)/shard_map/ppermute | solution.py:79
  91.7 9.4 %collective-permute-start.24 = (bf16[256,256]{1,0:T(8,128)(2,1)S(1)}, bf16[256,256]{1,0:T(8,128)(2,1)S(1)}, u32[]{:S(2)}, u32[]{:S(2)}) collective-permute-start(bf16[256,256]{1,0:T(8,128)(2,1)S(1)} %copy-done.34), channel_id=1, source_target_pairs={{0,6},{1,7},{2,4},{3,5},{4,2},{5,3},{6,0},{7,1},{8,14},{9,15},{10,... | collective-permute-start | bytes 393224 | tf_op jit(solution)/shard_map/ppermute | solution.py:79
  95.5 5.8 %collective-permute-start.15 = (bf16[256,256]{1,0:T(8,128)(2,1)S(1)}, bf16[256,256]{1,0:T(8,128)(2,1)S(1)}, u32[]{:S(2)}, u32[]{:S(2)}) collective-permute-start(bf16[256,256]{1,0:T(8,128)(2,1)S(1)} %copy-done.33), channel_id=1, source_target_pairs={{0,4},{1,5},{2,6},{3,7},{4,0},{5,1},{6,2},{7,3},{8,12},{9,13},{10,... | collective-permute-start | bytes 393224 | tf_op jit(solution)/shard_map/ppermute | solution.py:79
  96.5 10.9 %collective-permute-start.16 = (bf16[256,256]{1,0:T(8,128)(2,1)S(1)}, bf16[256,256]{1,0:T(8,128)(2,1)S(1)}, u32[]{:S(2)}, u32[]{:S(2)}) collective-permute-start(bf16[256,256]{1,0:T(8,128)(2,1)S(1)} %copy-done.32), channel_id=1, source_target_pairs={{0,2},{1,3},{2,0},{3,1},{4,6},{5,7},{6,4},{7,5},{8,10},{9,11},{10,... | collective-permute-start | bytes 393224 | tf_op jit(solution)/shard_map/ppermute | solution.py:79
  101.1 7.4 %collective-permute-start.17 = (bf16[256,256]{1,0:T(8,128)(2,1)S(1)}, bf16[256,256]{1,0:T(8,128)(2,1)S(1)}, u32[]{:S(2)}, u32[]{:S(2)}) collective-permute-start(bf16[256,256]{1,0:T(8,128)(2,1)S(1)} %copy-done.31), channel_id=1, source_target_pairs={{0,6},{1,7},{2,4},{3,5},{4,2},{5,3},{6,0},{7,1},{8,14},{9,15},{10,... | collective-permute-start | bytes 393224 | tf_op jit(solution)/shard_map/ppermute | solution.py:79
  101.4 10.1 %collective-permute-start.8 = (bf16[256,512]{1,0:T(8,128)(2,1)S(1)}, bf16[256,512]{1,0:T(8,128)(2,1)S(1)}, u32[]{:S(2)}, u32[]{:S(2)}) collective-permute-start(bf16[256,512]{1,0:T(8,128)(2,1)S(1)} %copy-done.22), channel_id=1, source_target_pairs={{0,4},{1,5},{2,6},{3,7},{4,0},{5,1},{6,2},{7,3},{8,12},{9,13},{10,... | collective-permute-start | bytes 786440 | tf_op jit(solution)/shard_map/ppermute | solution.py:79
  103.2 11.3 %collective-permute-start.9 = (bf16[256,512]{1,0:T(8,128)(2,1)S(1)}, bf16[256,512]{1,0:T(8,128)(2,1)S(1)}, u32[]{:S(2)}, u32[]{:S(2)}) collective-permute-start(bf16[256,512]{1,0:T(8,128)(2,1)S(1)} %copy-done.21), channel_id=1, source_target_pairs={{0,2},{1,3},{2,0},{3,1},{4,6},{5,7},{6,4},{7,5},{8,10},{9,11},{10,... | collective-permute-start | bytes 786440 | tf_op jit(solution)/shard_map/ppermute | solution.py:79
  106.0 35.3 %collective-permute-start.6 = (bf16[512,1024]{1,0:T(8,128)(2,1)S(1)}, bf16[512,1024]{1,0:T(8,128)(2,1)S(1)}, u32[]{:S(2)}, u32[]{:S(2)}) collective-permute-start(bf16[512,1024]{1,0:T(8,128)(2,1)S(1)} %slice_bitcast_fusion.3), channel_id=1, source_target_pairs={{0,2},{1,3},{2,0},{3,1},{4,6},{5,7},{6,4},{7,5},{8,10},{9,11},{10,... | collective-permute-start | bytes 3145736 | tf_op jit(solution)/shard_map/ppermute | solution.py:79
  107.4 34.2 %collective-permute-start.7 = (bf16[512,1024]{1,0:T(8,128)(2,1)S(1)}, bf16[512,1024]{1,0:T(8,128)(2,1)S(1)}, u32[]{:S(2)}, u32[]{:S(2)}) collective-permute-start(bf16[512,1024]{1,0:T(8,128)(2,1)S(1)} %slice_bitcast_fusion.2), channel_id=1, source_target_pairs={{0,4},{1,5},{2,6},{3,7},{4,0},{5,1},{6,2},{7,3},{8,12},{9,13},{10,... | collective-permute-start | bytes 3145736 | tf_op jit(solution)/shard_map/ppermute | solution.py:79
  108.5 30.0 %collective-permute-start.10 = (bf16[256,512]{1,0:T(8,128)(2,1)S(1)}, bf16[256,512]{1,0:T(8,128)(2,1)S(1)}, u32[]{:S(2)}, u32[]{:S(2)}) collective-permute-start(bf16[256,512]{1,0:T(8,128)(2,1)S(1)} %copy-done.20), channel_id=1, source_target_pairs={{0,6},{1,7},{2,4},{3,5},{4,2},{5,3},{6,0},{7,1},{8,14},{9,15},{10,... | collective-permute-start | bytes 786440 | tf_op jit(solution)/shard_map/ppermute | solution.py:79
  111.4 70.2 %collective-permute-start.32 = (bf16[1024,256]{1,0:T(8,128)(2,1)S(1)}, bf16[1024,256]{1,0:T(8,128)(2,1)S(1)}, u32[]{:S(2)}, u32[]{:S(2)}) collective-permute-start(bf16[1024,256]{1,0:T(8,128)(2,1)S(1)} %bitcast.225), channel_id=1, source_target_pairs={{0,16},{1,17},{2,18},{3,19},{4,20},{5,21},{6,22},{7,23},{8,24},{9,... | collective-permute-start | bytes 1572872 | tf_op jit(solution)/shard_map/ppermute | solution.py:79
  114.4 78.4 %collective-permute-start.25 = (bf16[1024,256]{1,0:T(8,128)(2,1)S(1)}, bf16[1024,256]{1,0:T(8,128)(2,1)S(1)}, u32[]{:S(2)}, u32[]{:S(2)}) collective-permute-start(bf16[1024,256]{1,0:T(8,128)(2,1)S(1)} %bitcast.227), channel_id=1, source_target_pairs={{0,16},{1,17},{2,18},{3,19},{4,20},{5,21},{6,22},{7,23},{8,24},{9,... | collective-permute-start | bytes 1572872 | tf_op jit(solution)/shard_map/ppermute | solution.py:79
  138.5 101.0 %collective-permute-start.18 = (bf16[1024,256]{1,0:T(8,128)(2,1)}, bf16[1024,256]{1,0:T(8,128)(2,1)}, u32[]{:S(2)}, u32[]{:S(2)}) collective-permute-start(bf16[1024,256]{1,0:T(8,128)(2,1)} %bitcast.42), channel_id=1, source_target_pairs={{0,16},{1,17},{2,18},{3,19},{4,20},{5,21},{6,22},{7,23},{8,24},{9,... | collective-permute-start | bytes 1572872 | tf_op jit(solution)/shard_map/ppermute | solution.py:79
  141.3 85.4 %collective-permute-start.11 = (bf16[1024,512]{1,0:T(8,128)(2,1)}, bf16[1024,512]{1,0:T(8,128)(2,1)}, u32[]{:S(2)}, u32[]{:S(2)}) collective-permute-start(bf16[1024,512]{1,0:T(8,128)(2,1)} %bitcast.20), channel_id=1, source_target_pairs={{0,16},{1,17},{2,18},{3,19},{4,20},{5,21},{6,22},{7,23},{8,24},{9,... | collective-permute-start | bytes 3145736 | tf_op jit(solution)/shard_map/ppermute | solution.py:79
  144.6 48.2 %copy-start.2 = (bf16[2,2,512,1024]{3,2,1,0:T(8,128)(2,1)}, bf16[2,2,512,1024]{3,2,1,0:T(8,128)(2,1)S(1)}, u32[]{:S(2)}) copy-start(bf16[2,2,512,1024]{3,2,1,0:T(8,128)(2,1)S(1)} %get-tuple-element.6) | copy-start | bytes 12582916
  144.6 49.6 %copy-start = (bf16[2,2,512,1024]{3,2,1,0:T(8,128)(2,1)}, bf16[2,2,512,1024]{3,2,1,0:T(8,128)(2,1)S(1)}, u32[]{:S(2)}) copy-start(bf16[2,2,512,1024]{3,2,1,0:T(8,128)(2,1)S(1)} %get-tuple-element.5) | copy-start | bytes 12582916
  198.3 54.1 %collective-permute-start.33 = (f32[2,512,256]{1,2,0:T(8,128)}, f32[2,512,256]{1,2,0:T(8,128)}, u32[]{:S(2)}, u32[]{:S(2)}) collective-permute-start(f32[2,512,256]{1,2,0:T(8,128)} %bitcast.230), channel_id=1, source_target_pairs={{0,1},{1,0},{2,3},{3,2},{4,5},{5,4},{6,7},{7,6},{8,9},{9,8},{10,11... | collective-permute-start | bytes 3145736 | tf_op jit(solution)/shard_map/ppermute | solution.py:79
  201.6 29.9 %copy-start.1 = (bf16[2,2,512,1024]{3,2,1,0:T(8,128)(2,1)S(1)}, bf16[2,2,512,1024]{3,2,1,0:T(8,128)(2,1)}, u32[]{:S(2)}) copy-start(bf16[2,2,512,1024]{3,2,1,0:T(8,128)(2,1)} %copy-done) | copy-start | bytes 12582916
  201.6 52.6 %collective-permute-start.26 = (f32[2,512,256]{1,2,0:T(8,128)}, f32[2,512,256]{1,2,0:T(8,128)}, u32[]{:S(2)}, u32[]{:S(2)}) collective-permute-start(f32[2,512,256]{1,2,0:T(8,128)} %bitcast.61), channel_id=1, source_target_pairs={{0,1},{1,0},{2,3},{3,2},{4,5},{5,4},{6,7},{7,6},{8,9},{9,8},{10,11... | collective-permute-start | bytes 3145736 | tf_op jit(solution)/shard_map/ppermute | solution.py:79
  238.3 23.6 %collective-permute-start.12 = (f32[2,512,512]{2,1,0:T(8,128)}, f32[2,512,512]{2,1,0:T(8,128)}, u32[]{:S(2)}, u32[]{:S(2)}) collective-permute-start(f32[2,512,512]{2,1,0:T(8,128)} %dynamic-slice_bitcast_fusion), channel_id=1, source_target_pairs={{0,1},{1,0},{2,3},{3,2},{4,5},{5,4},{6,7},{7,6},{8,9},{9,8},{10,11... | collective-permute-start | bytes 6291464 | tf_op jit(solution)/shard_map/ppermute | solution.py:79
  250.9 6.3 %collective-permute-start.19 = (f32[2,512,256]{1,2,0:T(8,128)}, f32[2,512,256]{1,2,0:T(8,128)}, u32[]{:S(2)}, u32[]{:S(2)}) collective-permute-start(f32[2,512,256]{1,2,0:T(8,128)} %bitcast.231), channel_id=1, source_target_pairs={{0,1},{1,0},{2,3},{3,2},{4,5},{5,4},{6,7},{7,6},{8,9},{9,8},{10,11... | collective-permute-start | bytes 3145736 | tf_op jit(solution)/shard_map/ppermute | solution.py:79
  254.0 7.8 %collective-permute-start.34 = (f16[512,256]{0,1:T(8,128)(2,1)S(1)}, f16[512,256]{0,1:T(8,128)(2,1)S(1)}, u32[]{:S(2)}, u32[]{:S(2)}) collective-permute-start(f16[512,256]{0,1:T(8,128)(2,1)S(1)} %fusion.29), channel_id=1, source_target_pairs={{0,8},{1,9},{2,10},{3,11},{4,12},{5,13},{6,14},{7,15},{8,0},{9,1},... | collective-permute-start | bytes 786440 | tf_op jit(solution)/shard_map/ppermute | solution.py:79
  255.7 11.7 %collective-permute-start.27 = (f16[512,256]{0,1:T(8,128)(2,1)S(1)}, f16[512,256]{0,1:T(8,128)(2,1)S(1)}, u32[]{:S(2)}, u32[]{:S(2)}) collective-permute-start(f16[512,256]{0,1:T(8,128)(2,1)S(1)} %fusion.28), channel_id=1, source_target_pairs={{0,8},{1,9},{2,10},{3,11},{4,12},{5,13},{6,14},{7,15},{8,0},{9,1},... | collective-permute-start | bytes 786440 | tf_op jit(solution)/shard_map/ppermute | solution.py:79
  259.3 17.5 %collective-permute-start.20 = (f16[512,256]{0,1:T(8,128)(2,1)}, f16[512,256]{0,1:T(8,128)(2,1)}, u32[]{:S(2)}, u32[]{:S(2)}) collective-permute-start(f16[512,256]{0,1:T(8,128)(2,1)} %fusion.27), channel_id=1, source_target_pairs={{0,8},{1,9},{2,10},{3,11},{4,12},{5,13},{6,14},{7,15},{8,0},{9,1},... | collective-permute-start | bytes 786440 | tf_op jit(solution)/shard_map/ppermute | solution.py:79
  265.0 30.6 %collective-permute-start.13 = (f32[512,512]{1,0:T(8,128)}, f32[512,512]{1,0:T(8,128)}, u32[]{:S(2)}, u32[]{:S(2)}) collective-permute-start(f32[512,512]{1,0:T(8,128)} %slice_bitcast_fusion), channel_id=1, source_target_pairs={{0,8},{1,9},{2,10},{3,11},{4,12},{5,13},{6,14},{7,15},{8,0},{9,1},... | collective-permute-start | bytes 3145736 | tf_op jit(solution)/shard_map/ppermute | solution.py:79
  306.7 20.7 %collective-permute-start.14 = (bf16[512,256]{1,0:T(8,128)(2,1)S(1)}, bf16[512,256]{1,0:T(8,128)(2,1)S(1)}, u32[]{:S(2)}, u32[]{:S(2)}) collective-permute-start(bf16[512,256]{1,0:T(8,128)(2,1)S(1)} %copy.96), channel_id=1, source_target_pairs={{1,4},{3,6},{4,1},{6,3},{9,12},{11,14},{12,9},{14,11},{17,20},{19,... | collective-permute-start | bytes 786440 | tf_op jit(solution)/shard_map/ppermute | solution.py:79
  312.4 15.1 %collective-permute-start.21 = (bf16[512,256]{1,0:T(8,128)(2,1)S(1)}, bf16[512,256]{1,0:T(8,128)(2,1)S(1)}, u32[]{:S(2)}, u32[]{:S(2)}) collective-permute-start(bf16[512,256]{1,0:T(8,128)(2,1)S(1)} %copy.104), channel_id=1, source_target_pairs={{1,4},{3,6},{4,1},{6,3},{9,12},{11,14},{12,9},{14,11},{17,20},{19,... | collective-permute-start | bytes 786440 | tf_op jit(solution)/shard_map/ppermute | solution.py:79
  317.4 10.0 %collective-permute-start.28 = (bf16[512,256]{1,0:T(8,128)(2,1)S(1)}, bf16[512,256]{1,0:T(8,128)(2,1)S(1)}, u32[]{:S(2)}, u32[]{:S(2)}) collective-permute-start(bf16[512,256]{1,0:T(8,128)(2,1)S(1)} %copy.112), channel_id=1, source_target_pairs={{1,4},{3,6},{4,1},{6,3},{9,12},{11,14},{12,9},{14,11},{17,20},{19,... | collective-permute-start | bytes 786440 | tf_op jit(solution)/shard_map/ppermute | solution.py:79
  325.0 7.7 %collective-permute-start.35 = (bf16[512,256]{1,0:T(8,128)(2,1)S(1)}, bf16[512,256]{1,0:T(8,128)(2,1)S(1)}, u32[]{:S(2)}, u32[]{:S(2)}) collective-permute-start(bf16[512,256]{1,0:T(8,128)(2,1)S(1)} %copy.120), channel_id=1, source_target_pairs={{1,4},{3,6},{4,1},{6,3},{9,12},{11,14},{12,9},{14,11},{17,20},{19,... | collective-permute-start | bytes 786440 | tf_op jit(solution)/shard_map/ppermute | solution.py:79
  (24 other events, 91.8 us)

commit v2 on v1

v2 whole, which is shorter than its diff:
```python
import jax
import jax.numpy as jnp
from jax import lax
from jax.experimental import pallas as pl
from jax.experimental.pallas import tpu as pltpu
from jax.sharding import PartitionSpec as P

HD = 128
AXES = ("batch", "tensor")


def rotary_tables(seq_len, head_size):
    half = head_size // 2
    position = jnp.arange(seq_len, dtype=jnp.float32)
    freqs = 500000.0 ** (-(jnp.arange(half, dtype=jnp.float32) * 2.0) / head_size)
    angles = position[:, None] * freqs[None, :]
    return jnp.cos(angles), jnp.sin(angles)


def rotate_heads(field, tables):
    seq_len = field.shape[0]
    shaped = field.reshape(seq_len, -1, HD)
    half = HD // 2
    cosine = tables[0][:, None, :]
    sine = tables[1][:, None, :]
    first = shaped[..., :half]
    second = shaped[..., half:]
    turned = jnp.concatenate(
        [first * cosine - second * sine, second * cosine + first * sine], axis=-1
    )
    return turned.astype(jnp.bfloat16)


def attend(q_rot, k_rot, v_val):
    seq_len = q_rot.shape[0]
    scores = jnp.einsum("shd,td->hst", q_rot, k_rot, preferred_element_type=jnp.float32) / jnp.sqrt(
        jnp.float32(HD)
    )
    causal = jnp.tril(jnp.ones((seq_len, seq_len), dtype=bool))
    scores = jnp.where(causal[None], scores, jnp.float32(-1e30))
    top = jnp.max(scores, axis=-1, keepdims=True)
    expo = jnp.exp(scores - top)
    probs = (expo / jnp.sum(expo, axis=-1, keepdims=True)).astype(jnp.bfloat16)
    result = jnp.einsum("hst,td->shd", probs, v_val, preferred_element_type=jnp.float32)
    return result.astype(jnp.bfloat16).reshape(seq_len, -1)


def gathered_plan(hidden_in, norm_gain, q_weight, k_weight, v_weight):
    tensor_count = lax.axis_size("tensor")
    whole_rows, whole_gain = (
        lax.all_gather(hidden_in, "tensor", axis=1, tiled=True),
        lax.all_gather(norm_gain, "tensor", axis=0, tiled=True),
    )
    values = whole_rows.astype(jnp.float32)
    meansq = jnp.mean(values * values, axis=-1, keepdims=True)
    normed = (values * lax.rsqrt(meansq + 1e-05) * whole_gain.astype(jnp.float32)).astype(
        jnp.bfloat16
    )
    own_rows = q_weight.shape[0]
    kv_heads = k_weight.shape[1] // HD
    repeat_count = tensor_count // kv_heads
    q_send = q_weight.reshape(own_rows, tensor_count, -1)
    k_send = jnp.repeat(k_weight.reshape(own_rows, kv_heads, HD), repeat_count, axis=1)
    v_send = jnp.repeat(v_weight.reshape(own_rows, kv_heads, HD), repeat_count, axis=1)
    sends = jnp.concatenate([k_send, v_send, q_send], axis=2)
    recv = lax.all_to_all(sends, "tensor", split_axis=1, concat_axis=0, tiled=True)
    full = lax.all_gather(recv.reshape(-1, recv.shape[2]), "batch", axis=0, tiled=True)
    lin = jnp.dot(normed, full, preferred_element_type=jnp.float32)
    tables = rotary_tables(normed.shape[0], HD)
    k_rot = rotate_heads(lin[:, :HD], tables)[:, 0, :]
    v_val = lin[:, HD : 2 * HD].astype(jnp.bfloat16)
    return attend(rotate_heads(lin[:, 2 * HD :], tables), k_rot, v_val)


def move(value, route):
    pairs = []
    for flat in range(32):
        to = route(flat >> 3, flat >> 2 & 1, flat >> 1 & 1, flat & 1)
        if to is not None:
            pairs.append((flat, ((to[0] * 2 + to[1]) * 2 + to[2]) * 2 + to[3]))
    return lax.ppermute(value, AXES, pairs)


def swap_x(z, x, y, c):
    return z, 1 - x, y, c


def swap_y(z, x, y, c):
    return z, x, 1 - y, c


def swap_xy(z, x, y, c):
    return z, 1 - x, 1 - y, c


def swap_c(z, x, y, c):
    return z, x, y, 1 - c


def swap_near(z, x, y, c):
    return z ^ 1, x, y, c


def swap_far(z, x, y, c):
    return z ^ 2, x, y, c


CHUNKS = ((0, 5), (5, 8), (8, 10))
VMEM = 16 * 2**20


def place():
    batch, tensor = lax.axis_index("batch"), lax.axis_index("tensor")
    return batch >> 1, batch & 1, tensor >> 1, tensor & 1


def pick(pair, index):
    return lax.dynamic_index_in_dim(pair, index, 0, keepdims=False)


def call(kernel, out_shape, scratch=(), flops=0, name=None):
    shapes = out_shape if isinstance(out_shape, (list, tuple)) else (out_shape,)
    size = sum(2 * s.size * s.dtype.itemsize for s in shapes)
    return pl.pallas_call(
        kernel,
        out_shape=out_shape,
        scratch_shapes=scratch,
        compiler_params=pltpu.CompilerParams(vmem_limit_bytes=VMEM),
        cost_estimate=pl.CostEstimate(flops=flops, bytes_accessed=size, transcendentals=0),
        name=name,
    )


def pack_kernel(q_ref, k_ref, v_ref, *outs):
    _, x, y, _ = place()
    q_cols = outs[0].shape[1] - 2 * HD
    for out, px, py in zip(outs, (x, 1 - x, x, 1 - x), (y, y, 1 - y, 1 - y)):
        group = 2 * py + px
        out[:, :HD] = k_ref[:, pl.ds(pl.multiple_of(group * HD, HD), HD)]
        out[:, HD : 2 * HD] = v_ref[:, pl.ds(pl.multiple_of(group * HD, HD), HD)]
        out[:, 2 * HD :] = q_ref[:, pl.ds(pl.multiple_of(group * q_cols, HD), q_cols)]


def rest_kernel(own_ref, a_ref, b_ref, c_ref, all_ref, *outs):
    own = a_ref.shape[0]
    for i, ref in enumerate((own_ref, a_ref, b_ref, c_ref)):
        all_ref[i * own : (i + 1) * own, :] = ref[...]
        for out, (lo, hi) in zip(outs, CHUNKS):
            if i > 0:
                out[(i - 1) * own : i * own, :] = ref[:, lo * HD : hi * HD]


def squares_kernel(rows_ref, out):
    value = rows_ref[...].astype(jnp.float32)
    total = jnp.sum(value * value, axis=1, keepdims=True)
    out[...] = jnp.transpose(jnp.broadcast_to(total, (total.shape[0], HD)))[: out.shape[0], :]


def stamp_kernel(rows_ref, gain_ref, own_ref, got_ref, out):
    rows, feats = rows_ref.shape
    out[:rows, :] = rows_ref[...]
    left = own_ref[...] + got_ref[...]
    parts = []
    for _ in range(3):
        part = left.astype(jnp.bfloat16).astype(jnp.float32)
        parts.append(part)
        left = left - part
    parts.append(jnp.zeros((left.shape[0], feats - 3 * rows), jnp.float32))
    tile = jnp.concatenate(parts, axis=1)
    at = lax.broadcasted_iota(jnp.int32, tile.shape, 0)
    tile = jnp.where(at == 0, gain_ref[...].astype(jnp.float32), tile)
    out[rows:, :] = jnp.concatenate([tile, tile], axis=0).astype(jnp.bfloat16)


def scale_kernel(here, by_x, by_y, by_xy, out):
    z, x, y, c = place()
    rows, feats = out.shape[0], here.shape[1]
    at = jnp.where(y == z >> 1, 0, feats)

    def fill(same, other):
        tiles = [ref[rows:, :].astype(jnp.float32) for ref in (same, other)]
        total = sum(tile[1:2, i * rows : (i + 1) * rows] for tile in tiles for i in range(3))
        scale = lax.rsqrt(total / (4 * feats) + 1e-05)
        scale = jnp.transpose(jnp.broadcast_to(scale, (HD, rows)))[:, :1]
        for ref, tile, to in ((same, tiles[0], at), (other, tiles[1], feats - at)):
            value = ref[:rows, :].astype(jnp.float32) * scale * tile[:1, :]
            out[:, pl.ds(pl.multiple_of(to, feats), feats)] = value.astype(jnp.bfloat16)

    @pl.when(c == x)
    def _():
        fill(here, by_y)

    @pl.when(c != x)
    def _():
        fill(by_x, by_xy)


def product_kernel(lo, hi, lhs, near_both, mine_both, rest, rest_core, out, near, far):
    _, x, y, c = place()
    own = mine_both.shape[1]
    depth = near.shape[0]
    span = slice(lo * HD, hi * HD)
    for core, others in ((c, rest), (1 - c, rest_core)):
        for i in range(4):
            px = x if i % 2 == 0 else 1 - x
            py = y if i < 2 else 1 - y
            at = pl.ds(pl.multiple_of((4 * px + 2 * py + core) * own, own), own)
            near[at, :] = near_both[core, i * own : (i + 1) * own, span]
            far[at, :] = mine_both[core, :, span] if i == 0 else others[(i - 1) * own : i * own, :]
    out[...] = jnp.dot(lhs[:, :depth], near[...], preferred_element_type=jnp.float32) + jnp.dot(
        lhs[:, depth:], far[...], preferred_element_type=jnp.float32
    )


def turn(value, cosine, sine):
    return (value * cosine + pltpu.roll(value, HD // 2, 1) * sine).astype(jnp.bfloat16)


def attend_kernel(with_kv, *refs):
    if with_kv:
        near_ref, got_ref, cos_ref, sin_ref, out_ref, k_ref, v_ref = refs
    else:
        near_ref, got_ref, cos_ref, sin_ref, k_ref, v_ref, out_ref = refs
    rows = near_ref.shape[0]
    cosine, sine = cos_ref[...], sin_ref[...]

    def head(h):
        return near_ref[:, h * HD : (h + 1) * HD] + got_ref[:, h * HD : (h + 1) * HD]

    if with_kv:
        k_ref[...] = turn(head(0), cosine, sine)
        v_ref[...] = head(1).astype(jnp.bfloat16)
    skip = 2 if with_kv else 0
    half = rows // 2
    scale = 1.0 / (HD**0.5)
    above = lax.broadcasted_iota(jnp.int32, (half, half), 1) > lax.broadcasted_iota(
        jnp.int32, (half, half), 0
    )
    for h in range(out_ref.shape[1] // HD):
        q = turn(head(h + skip), cosine, sine)
        for block in range(2):
            mine = q[block * half : (block + 1) * half]
            parts = []
            for other in range(block + 1):
                keys = k_ref[other * half : (other + 1) * half, :]
                s = lax.dot_general(
                    mine, keys, (((1,), (1,)), ((), ())), preferred_element_type=jnp.float32
                )
                s = s * scale
                parts.append(jnp.where(above, -1e30, s) if other == block else s)
            s = parts[0] if block == 0 else jnp.concatenate(parts, axis=1)
            expo = jnp.exp(s - jnp.max(s, axis=1, keepdims=True))
            probs = (expo / jnp.sum(expo, axis=1, keepdims=True)).astype(jnp.bfloat16)
            got = jnp.dot(
                probs, v_ref[: (block + 1) * half, :], preferred_element_type=jnp.float32
            )
            out_ref[block * half : (block + 1) * half, h * HD : (h + 1) * HD] = got.astype(
                jnp.bfloat16
            )


def split_plan(hidden_in, norm_gain, q_weight, k_weight, v_weight):
    z, x, y, c = place()
    home = c == z & 1
    direct = c == x
    rows, feats = hidden_in.shape
    own = q_weight.shape[0]
    cols = (q_weight.shape[1] + k_weight.shape[1] + v_weight.shape[1]) // 4
    bf16 = jnp.bfloat16

    mine, for_x, for_y, for_xy = call(
        pack_kernel, [jax.ShapeDtypeStruct((own, cols), bf16)] * 4, name="pack"
    )(q_weight, k_weight, v_weight)
    def to_other_plane(z, x, y, c):
        return None if c == z & 1 else (z ^ 1, x, y, x)

    def to_core(z, x, y, c):
        return (z, x, y, x) if c == z & 1 and c != x else None

    squares = call(squares_kernel, jax.ShapeDtypeStruct((8, rows), jnp.float32), name="squares")(
        hidden_in
    )
    stamped = call(stamp_kernel, jax.ShapeDtypeStruct((rows + 16, feats), bf16), name="stamp")(
        hidden_in, norm_gain[None, :], squares, move(squares, swap_c)
    )
    here_far = move(stamped, to_other_plane)
    far_mine = move(mine, swap_far)
    pieces = (move(for_x, swap_x), move(for_y, swap_y), move(for_xy, swap_xy))
    mine, far_mine, pieces, here_far, later = lax.optimization_barrier(
        (mine, far_mine, pieces, here_far, stamped)
    )

    widths = [(hi - lo) * HD for lo, hi in CHUNKS]
    near_all, *rest = call(
        rest_kernel,
        [jax.ShapeDtypeStruct((4 * own, cols), bf16)]
        + [jax.ShapeDtypeStruct((3 * own, n), bf16) for n in widths],
        name="rest",
    )(mine, *pieces)

    def give(dx, dy):
        return lambda z, x, y, c: (z, x ^ dx, y ^ dy, c) if c == x else None

    def spread(block):
        return (block, move(block, give(1, 0)), move(block, give(0, 1)), move(block, give(1, 1)))

    far_rest = [move(rest[0], swap_far)]
    far_rows = spread(here_far)
    here_near = jnp.where(home, later, move(later, to_core))

    def normed(blocks):
        shape = jax.ShapeDtypeStruct((rows, 2 * feats), bf16)
        return call(scale_kernel, shape, name="scale_rows")(*blocks)

    far_rows, here_near, far_rest[0], rest[1] = lax.optimization_barrier(
        (far_rows, here_near, far_rest[0], rest[1])
    )
    far_rest.append(move(rest[1], swap_far))
    near_rows = spread(here_near)
    rest[2], far_rest[1], far_rows = lax.optimization_barrier((rest[2], far_rest[1], far_rows))
    far_rest.append(move(rest[2], swap_far))
    far_rows = normed(far_rows)
    near_rows = normed(near_rows)

    cores = [[0, 1], [2, 3]]
    near_both = lax.all_gather(near_all, "tensor", axis_index_groups=cores)
    far_mine_both = lax.all_gather(far_mine, "tensor", axis_index_groups=cores)

    cosine, sine = rotary_tables(rows, HD)
    cosine = jnp.concatenate([cosine, cosine], axis=1)
    sine = jnp.concatenate([-sine, sine], axis=1)

    weights = [
        (near_both, far_mine_both, far_rest[j], move(far_rest[j], swap_c))
        for j in range(len(CHUNKS))
    ]

    def product(block, j):
        lo, hi = CHUNKS[j]
        n = (hi - lo) * HD
        return call(
            lambda *refs: product_kernel(lo, hi, *refs),
            jax.ShapeDtypeStruct((rows, n), jnp.float32),
            scratch=[pltpu.VMEM((feats, n), bf16)] * 2,
            name="product",
        )(block, *weights[j])

    def to_owner(z, x, y, c):
        return None if x == c else (z, c, y, x)

    sums = []
    for j, (lo, hi) in enumerate(CHUNKS):
        sent = product(far_rows, j)
        if lo == 0:
            v_got = move(sent[:, HD : 2 * HD], swap_near)
            sent = jnp.concatenate([sent[:, :HD], sent[:, 2 * HD :]], axis=1)
        got = move(sent.astype(jnp.float16), swap_near).astype(jnp.float32)
        if lo == 0:
            got = jnp.concatenate([got[:, :HD], v_got, got[:, HD:]], axis=1)
        sums.append(got)

    results = []
    k_rot = v_val = None
    for j, (lo, hi) in enumerate(CHUNKS):
        args = (product(near_rows, j), sums[j], cosine, sine)
        if lo == 0:
            out, k_rot, v_val = call(
                lambda *refs: attend_kernel(True, *refs),
                [jax.ShapeDtypeStruct((rows, (hi - lo - 2) * HD), bf16)]
                + [jax.ShapeDtypeStruct((rows, HD), bf16)] * 2,
                name="attend_first",
            )(*args)
        else:
            out = call(
                lambda *refs: attend_kernel(False, *refs),
                jax.ShapeDtypeStruct((rows, (hi - lo) * HD), bf16),
                name="attend",
            )(*args, k_rot, v_val)
        results.append(jnp.where(direct, out, move(out, to_owner)))
    return jnp.concatenate(results, axis=1)


def solution(mesh):
    placed = (
        P("batch", "tensor"),
        P("tensor"),
        P(("batch", "tensor"), None),
        P(("batch", "tensor"), None),
        P(("batch", "tensor"), None),
    )
    plan = split_plan if dict(mesh.shape) == {"batch": 8, "tensor": 4} else gathered_plan
    return jax.shard_map(
        plan, mesh=mesh, in_specs=placed, out_specs=P("batch", "tensor"), check_vma=False
    )
```

time: 335 us -> 255 us (0.76)
  waiting for transfers between devices: 174 us -> 97.2 us
  Pallas kernels: 0 us -> 39.2 us
  matrix products: 30.4 us -> 0 us
  local copies, waits for them, and re-layouts: 51.5 us -> 25.9 us
  starting transfers between devices: 48.1 us -> 68.8 us
  other arithmetic: 29.2 us -> 8.69 us
  between operations: 0.91 us -> 14 us
    ppermute x36 -> x26, waiting for transfers between devices: 174 us -> 97.2 us  [move(): return lax.ppermute(value, AXES, pairs)]
    pallas_call x0 -> x15, Pallas kernels: none -> 39.2 us  [the longest x6 21.6 us: product(): call(lambda *refs: product_kernel(lo, hi, *refs), jax.ShapeDtypeStruct((r...]
    dot_general x12 -> x0, matrix products: 24.4 us -> none  [the longest x4 9.8 us: split_plan(): part = part + jnp.dot(x_far, far[j], preferred_element_type=jnp.float32)]
    ppermute x36 -> x26, starting transfers between devices: 48.1 us -> 68.8 us  [move(): return lax.ppermute(value, AXES, pairs)]
    dynamic_slice x13 -> x0, local copies, waits for them, and re-layouts: 16.5 us -> none  [the longest x11 12.2 us: pick(): return lax.dynamic_index_in_dim(pair, index, 0, keepdims=False)]
    unnamed x81 -> x74, local copies, waits for them, and re-layouts: 13.8 us -> 24.8 us
    dynamic_update_slice x15 -> x0, local copies, waits for them, and re-layouts: 10.5 us -> none  [split_plan(): block = lax.dynamic_update_index_in_dim(block, piece, 2 * px + py, 0)]
    add x9 -> x0, other arithmetic: 9.88 us -> none  [the longest x4 6.45 us: split_plan(): both = pick(part, keep) + move(pick(part, 1 - keep), swap_c)]
  transfers between devices with their start and end apart: 36 -> 28, of which waited for: 13 -> 9; matrix products, arithmetic and copies ran while one was open for 28% -> 3% of each run, Pallas kernels for 0% -> 15%
where the time goes in v2:
time: 255 us; the launch traced here: 254 us
  waiting for transfers between devices  97.2 us (38%)
  starting transfers between devices  68.8 us (27%)
  Pallas kernels  39.2 us (15%)
  local copies, waits for them, and re-layouts  25.9 us (10%)
  between operations  14 us (5%)
  other arithmetic  8.69 us (3%)
    ppermute x26, waiting for transfers between devices, move(): return lax.ppermute(value, AXES, pairs)  97.2 us
    ppermute x26, starting transfers between devices, move(): return lax.ppermute(value, AXES, pairs)  68.8 us
    unnamed x74, local copies, waits for them, and re-layouts  24.8 us
    pallas_call x6, Pallas kernels, product(): call(lambda *refs: product_kernel(lo, hi, *refs), jax.ShapeDtypeStruct((r...  21.6 us
    pallas_call x2, Pallas kernels, normed(): return call(scale_kernel, shape, name='scale_rows')(*blocks)  8.98 us
  transfers between devices with their start and end apart: 28, of which 9 were waited for; matrix products, arithmetic and copies ran while one was open for 3% of the time, Pallas kernels for 15%

profile of v2, /device:TPU:1, one launch (start us, length us, event | category | flops | bytes accessed | tf_op | source)
XLA Modules:
  0.0 253.9 jit_solution(2879677252172555067)
XLA Ops:
  6.5 1.6 copy-done.10
  10.1 6.1 %collective-permute-start.5 = (bf16[528,2048]{1,0:T(8,128)(2,1)S(1)}, bf16[528,2048]{1,0:T(8,128)(2,1)}, u32[]{:S(2)}, u32[]{:S(2)}) collective-permute-start(bf16[528,2048]{1,0:T(8,128)(2,1)S(1)} %stamp.1), channel_id=1, source_target_pairs={{1,8},{3,10},{5,13},{7,15},{8,0},{10,2},{12,5},{14,7},{17,24},{19,... | collective-permute-start | bytes 6488072 | tf_op jit(solution)/shard_map/ppermute | solution.py:81
  16.4 1.3 collective-permute-start.2
  17.8 1.3 collective-permute-start.3
  19.1 2.3 collective-permute-start
  21.4 12.0 %collective-permute-done.1.a_ref = bf16[256,1280]{1,0:T(8,128)(2,1)S(1)} collective-permute-done((bf16[256,1280]{1,0:T(8,128)(2,1)S(1)}, bf16[256,1280]{1,0:T(8,128)(2,1)S(1)}, u32[]{:S(2)}, u32[]{:S(2)}) %collective-permute-start.1) | collective-permute-done | bytes 655392 | tf_op jit(solution)/shard_map/ppermute | solution.py:81
  33.4 13.5 %collective-permute-done.2.b_ref = bf16[256,1280]{1,0:T(8,128)(2,1)S(1)} collective-permute-done((bf16[256,1280]{1,0:T(8,128)(2,1)S(1)}, bf16[256,1280]{1,0:T(8,128)(2,1)S(1)}, u32[]{:S(2)}, u32[]{:S(2)}) %collective-permute-start.2) | collective-permute-done | bytes 655392 | tf_op jit(solution)/shard_map/ppermute | solution.py:81
  48.6 3.8 %collective-permute-done = bf16[256,1280]{1,0:T(8,128)(2,1)} collective-permute-done((bf16[256,1280]{1,0:T(8,128)(2,1)S(1)}, bf16[256,1280]{1,0:T(8,128)(2,1)}, u32[]{:S(2)}, u32[]{:S(2)}) %collective-permute-start) | collective-permute-done | bytes 655392 | tf_op jit(solution)/shard_map/ppermute | solution.py:81
  55.0 1.5 copy-done.20
  59.1 2.0 collective-permute-start.9
  61.1 1.3 collective-permute-start.8
  62.4 2.0 collective-permute-start.7
  64.4 1.3 collective-permute-start.6
  65.7 3.0 %collective-permute-start.10 = (bf16[768,640]{1,0:T(8,128)(2,1)}, bf16[768,640]{1,0:T(8,128)(2,1)S(1)}, u32[]{:S(2)}, u32[]{:S(2)}) collective-permute-start(bf16[768,640]{1,0:T(8,128)(2,1)} %copy-done.30), channel_id=1, source_target_pairs={{0,16},{1,17},{2,18},{3,19},{4,20},{5,21},{6,22},{7,23},{8,24},{9,... | collective-permute-start | bytes 2949128 | tf_op jit(solution)/shard_map/ppermute | solution.py:81
  68.7 1.9 broadcast_select_fusion.here
  70.6 36.8 %collective-permute-done.10.refs_3_ = bf16[768,640]{1,0:T(8,128)(2,1)S(1)} collective-permute-done((bf16[768,640]{1,0:T(8,128)(2,1)}, bf16[768,640]{1,0:T(8,128)(2,1)S(1)}, u32[]{:S(2)}, u32[]{:S(2)}) %collective-permute-start.10) | collective-permute-done | bytes 983072 | tf_op jit(solution)/shard_map/ppermute | solution.py:81
  107.4 5.8 %collective-permute-done.6.by_x = bf16[528,2048]{1,0:T(8,128)(2,1)} collective-permute-done((bf16[528,2048]{1,0:T(8,128)(2,1)}, bf16[528,2048]{1,0:T(8,128)(2,1)}, u32[]{:S(2)}, u32[]{:S(2)}) %collective-permute-start.6) | collective-permute-done | bytes 2162720 | tf_op jit(solution)/shard_map/ppermute | solution.py:81
  113.2 1.3 collective-permute-start.13
  114.5 2.0 collective-permute-start.12
  117.8 3.0 %collective-permute-start.15 = (bf16[768,384]{1,0:T(8,128)(2,1)S(1)}, bf16[768,384]{1,0:T(8,128)(2,1)}, u32[]{:S(2)}, u32[]{:S(2)}) collective-permute-start(bf16[768,384]{1,0:T(8,128)(2,1)S(1)} %copy-done.32), channel_id=1, source_target_pairs={{0,16},{1,17},{2,18},{3,19},{4,20},{5,21},{6,22},{7,23},{8,24},{9,... | collective-permute-start | bytes 1769480 | tf_op jit(solution)/shard_map/ppermute | solution.py:81
  120.8 8.8 %collective-permute-start.14 = (bf16[768,640]{1,0:T(8,128)(2,1)S(1)}, bf16[768,640]{1,0:T(8,128)(2,1)S(1)}, u32[]{:S(2)}, u32[]{:S(2)}) collective-permute-start(bf16[768,640]{1,0:T(8,128)(2,1)S(1)} %collective-permute-done.10.refs_3_), channel_id=1, source_target_pairs={{0,1},{1,0},{2,3},{3,2},{4,5},{5,4},{6,7},{7,6},{8,9},{9,8},{10,11... | collective-permute-start | bytes 2949128 | tf_op jit(solution)/shard_map/ppermute | solution.py:81
  129.6 12.9 %collective-permute-done.15.refs_3_ = bf16[768,384]{1,0:T(8,128)(2,1)} collective-permute-done((bf16[768,384]{1,0:T(8,128)(2,1)S(1)}, bf16[768,384]{1,0:T(8,128)(2,1)}, u32[]{:S(2)}, u32[]{:S(2)}) %collective-permute-start.15) | collective-permute-done | bytes 589856 | tf_op jit(solution)/shard_map/ppermute | solution.py:81
  142.6 8.7 %collective-permute-done.22.refs_3_ = bf16[768,256]{1,0:T(8,128)(2,1)S(1)} collective-permute-done((bf16[768,256]{1,0:T(8,128)(2,1)S(1)}, bf16[768,256]{1,0:T(8,128)(2,1)S(1)}, u32[]{:S(2)}, u32[]{:S(2)}) %collective-permute-start.22) | collective-permute-done | bytes 393248 | tf_op jit(solution)/shard_map/ppermute | solution.py:81
  151.3 6.3 %collective-permute-start.23 = (bf16[768,256]{1,0:T(8,128)(2,1)S(1)}, bf16[768,256]{1,0:T(8,128)(2,1)}, u32[]{:S(2)}, u32[]{:S(2)}) collective-permute-start(bf16[768,256]{1,0:T(8,128)(2,1)S(1)} %collective-permute-done.22.refs_3_), channel_id=1, source_target_pairs={{0,1},{1,0},{2,3},{3,2},{4,5},{5,4},{6,7},{7,6},{8,9},{9,8},{10,11... | collective-permute-start | bytes 1179656 | tf_op jit(solution)/shard_map/ppermute | solution.py:81
  157.6 4.6 %scale_rows.3.refs_0_ = bf16[512,4096]{1,0:T(8,128)(2,1)S(1)} custom-call(bf16[528,2048]{1,0:T(8,128)(2,1)} %collective-permute-done.5.here, bf16[528,2048]{1,0:T(8,128)(2,1)} %collective-permute-done.6.by_x, bf16[528,2048]{1,0:T(8,128)(2,1)} %collective-permute-done.7.by_y, bf16[528,2048]{1,0:T(8,128)(2,1)} %collective-permute-done.8.by_xy), custom_call_target="tpu_custom_call" | custom-call | bytes 8388608 | tf_op jit(solution)/shard_map/scale_rows/pallas_call | solution.py:313
  162.3 2.0 copy-done.2
  165.4 2.5 copy-done
  167.9 2.2 copy-done.3
  170.1 1.3 copy-done.7
  172.6 3.8 %product.7 = f32[512,640]{1,0:T(8,128)S(1)} custom-call(bf16[512,4096]{1,0:T(8,128)(2,1)S(1)} %copy-done.3, bf16[2,1024,1280]{2,1,0:T(8,128)(2,1)S(1)} %bitcast.2, bf16[2,256,1280]{2,1,0:T(8,128)(2,1)S(1)} %bitcast.10, bf16[768,640]{1,0:T(8,128)(2,1)S(1)} %collective-permute-done.10.refs_3_, bf16[768,640]{1,0:T(8,128)(2,1)S(1)} %copy-done.18), custom_call_target="tpu_custom_call" | custom-call | bytes 2621440 | tf_op jit(solution)/shard_map/product/pallas_call | solution.py:341
  176.7 11.0 %collective-permute-start.16 = (f16[512,512]{1,0:T(8,128)(2,1)S(1)}, f16[512,512]{1,0:T(8,128)(2,1)S(1)}, u32[]{:S(2)}, u32[]{:S(2)}) collective-permute-start(f16[512,512]{1,0:T(8,128)(2,1)S(1)} %pad_maximum_fusion.2), channel_id=1, source_target_pairs={{0,8},{1,9},{2,10},{3,11},{4,12},{5,13},{6,14},{7,15},{8,0},{9,1},... | collective-permute-start | bytes 1572872 | tf_op jit(solution)/shard_map/ppermute | solution.py:81
  187.8 2.4 product.11
  190.3 1.8 collective-permute-start.24
  193.4 4.3 %scale_rows.2.refs_0_ = bf16[512,4096]{1,0:T(8,128)(2,1)S(1)} custom-call(bf16[528,2048]{1,0:T(8,128)(2,1)S(1)} %broadcast_select_fusion.here, bf16[528,2048]{1,0:T(8,128)(2,1)} %collective-permute-done.11.by_x, bf16[528,2048]{1,0:T(8,128)(2,1)} %collective-permute-done.12.by_y, bf16[528,2048]{1,0:T(8,128)(2,1)} %collective-permute-done.13.by_xy), custom_call_target="tpu_custom_call" | custom-call | bytes 8388608 | tf_op jit(solution)/shard_map/scale_rows/pallas_call | solution.py:313
  198.1 5.5 %product.9 = f32[512,384]{1,0:T(8,128)S(1)} custom-call(bf16[512,4096]{1,0:T(8,128)(2,1)S(1)} %copy-done.4, bf16[2,1024,1280]{2,1,0:T(8,128)(2,1)S(1)} %bitcast.6, bf16[2,256,1280]{2,1,0:T(8,128)(2,1)S(1)} %bitcast.12, bf16[768,384]{1,0:T(8,128)(2,1)} %collective-permute-done.15.refs_3_, bf16[768,384]{1,0:T(8,128)(2,1)} %collective-permute-done.19.refs_4_), custom_call_target="tpu_custom_call" | custom-call | bytes 1572864 | tf_op jit(solution)/shard_map/product/pallas_call | solution.py:341
  204.4 1.4 collective-permute-start.20
  205.8 3.8 %product.6.refs_0_ = f32[512,640]{1,0:T(8,128)S(1)} custom-call(bf16[512,4096]{1,0:T(8,128)(2,1)S(1)} %scale_rows.2.refs_0_, bf16[2,1024,1280]{2,1,0:T(8,128)(2,1)S(1)} %bitcast.7, bf16[2,256,1280]{2,1,0:T(8,128)(2,1)S(1)} %bitcast.13, bf16[768,640]{1,0:T(8,128)(2,1)S(1)} %copy-done.16, bf16[768,640]{1,0:T(8,128)(2,1)S(1)} %copy-done.19), custom_call_target="tpu_custom_call" | custom-call | bytes 2621440 | tf_op jit(solution)/shard_map/product/pallas_call | solution.py:341
  209.6 2.4 product.10.refs_0_
  212.4 2.8 %attend_first.1 = (bf16[512,384]{1,0:T(8,128)(2,1)S(1)}, bf16[512,128]{1,0:T(8,128)(2,1)S(1)}, bf16[512,128]{1,0:T(8,128)(2,1)S(1)}) custom-call(f32[512,640]{1,0:T(8,128)S(1)} %product.6.refs_0_, f32[512,640]{1,0:T(8,128)S(1)} %pad_maximum_fusion.refs_1_, f32[512,128]{1,0:T(8,128)S(1)} %get-tuple-element.70.refs_2_, f32[512,128]{1,0:T(8,128)S(1)} %get-tuple-element.71.refs_3_), custom_call_target="tpu_custom_call" | custom-call | bytes 1310720 | tf_op jit(solution)/shard_map/attend_first/pallas_call | solution.py:367
  215.3 1.9 attend.3
  217.1 5.1 %collective-permute-start.25 = (bf16[512,256]{1,0:T(8,128)(2,1)S(1)}, bf16[512,256]{1,0:T(8,128)(2,1)}, u32[]{:S(2)}, u32[]{:S(2)}) collective-permute-start(bf16[512,256]{1,0:T(8,128)(2,1)S(1)} %attend.3), channel_id=1, source_target_pairs={{1,4},{3,6},{4,1},{6,3},{9,12},{11,14},{12,9},{14,11},{17,20},{19,... | collective-permute-start | bytes 786440 | tf_op jit(solution)/shard_map/ppermute | solution.py:81
  222.3 2.1 collective-permute-start.18
  224.4 2.5 copy-done.1
  226.9 2.2 copy-done.6
  229.1 3.8 %product.8.refs_0_ = f32[512,384]{1,0:T(8,128)S(1)} custom-call(bf16[512,4096]{1,0:T(8,128)(2,1)S(1)} %copy-done.6, bf16[2,1024,1280]{2,1,0:T(8,128)(2,1)S(1)} %bitcast.9, bf16[2,256,1280]{2,1,0:T(8,128)(2,1)S(1)} %bitcast.15, bf16[768,384]{1,0:T(8,128)(2,1)} %collective-permute-done.15.refs_3_, bf16[768,384]{1,0:T(8,128)(2,1)} %collective-permute-done.19.refs_4_), custom_call_target="tpu_custom_call" | custom-call | bytes 1572864 | tf_op jit(solution)/shard_map/product/pallas_call | solution.py:341
  234.0 2.7 %attend.2 = bf16[512,384]{1,0:T(8,128)(2,1)S(1)} custom-call(f32[512,384]{1,0:T(8,128)S(1)} %product.8.refs_0_, f32[512,384]{1,0:T(8,128)S(1)} %convert_element_type.18.refs_1_, f32[512,128]{1,0:T(8,128)S(1)} %copy-done.12, f32[512,128]{1,0:T(8,128)S(1)} %copy-done.14, bf16[512,128]{1,0:T(8,128)(2,1)S(1)} %get-tuple-element.64.refs_4_, ...), custom_call_target="tpu_custom_call" | custom-call | bytes 786432 | tf_op jit(solution)/shard_map/attend/pallas_call | solution.py:374
  236.8 3.6 %collective-permute-start.21 = (bf16[512,384]{1,0:T(8,128)(2,1)S(1)}, bf16[512,384]{1,0:T(8,128)(2,1)S(1)}, u32[]{:S(2)}, u32[]{:S(2)}) collective-permute-start(bf16[512,384]{1,0:T(8,128)(2,1)S(1)} %attend.2), channel_id=1, source_target_pairs={{1,4},{3,6},{4,1},{6,3},{9,12},{11,14},{12,9},{14,11},{17,20},{19,... | collective-permute-start | bytes 1179656 | tf_op jit(solution)/shard_map/ppermute | solution.py:81
  242.5 3.4 %collective-permute-done.21 = bf16[512,384]{1,0:T(8,128)(2,1)S(1)} collective-permute-done((bf16[512,384]{1,0:T(8,128)(2,1)S(1)}, bf16[512,384]{1,0:T(8,128)(2,1)S(1)}, u32[]{:S(2)}, u32[]{:S(2)}) %collective-permute-start.21) | collective-permute-done | bytes 393248 | tf_op jit(solution)/shard_map/ppermute | solution.py:81
  (122 shorter events, 20.2 us)
Async XLA Ops:
  6.5 158.9 %all-gather.7.cloned.1.call-start = ((), (), s32[]{:S(2)}) async-start(), calls=%async_computation.1 | async-start | bytes 1966080 | tf_op jit(solution)/shard_map/all_gather | solution.py:327
  8.6 7.5 %copy-start.21 = (bf16[256,4096]{1,0:T(8,128)(2,1)S(1)}, bf16[256,4096]{1,0:T(8,128)(2,1)}, u32[]{:S(2)}) copy-start(bf16[256,4096]{1,0:T(8,128)(2,1)} %q_ref.1) | copy-start | bytes 6291460
  8.6 7.5 %copy-start.28 = (bf16[256,512]{1,0:T(8,128)(2,1)S(1)}, bf16[256,512]{1,0:T(8,128)(2,1)}, u32[]{:S(2)}) copy-start(bf16[256,512]{1,0:T(8,128)(2,1)} %k_ref.1) | copy-start | bytes 786436
  8.7 7.5 %copy-start.29 = (bf16[256,512]{1,0:T(8,128)(2,1)S(1)}, bf16[256,512]{1,0:T(8,128)(2,1)}, u32[]{:S(2)}) copy-start(bf16[256,512]{1,0:T(8,128)(2,1)} %v_ref.1) | copy-start | bytes 786436
  8.7 1.2 collective-permute-start.4
  10.1 49.0 %copy-start.9 = (bf16[528,2048]{1,0:T(8,128)(2,1)}, bf16[528,2048]{1,0:T(8,128)(2,1)S(1)}, u32[]{:S(2)}) copy-start(bf16[528,2048]{1,0:T(8,128)(2,1)S(1)} %stamp.1) | copy-start | bytes 6488068
  10.1 42.3 %collective-permute-start.5 = (bf16[528,2048]{1,0:T(8,128)(2,1)S(1)}, bf16[528,2048]{1,0:T(8,128)(2,1)}, u32[]{:S(2)}, u32[]{:S(2)}) collective-permute-start(bf16[528,2048]{1,0:T(8,128)(2,1)S(1)} %stamp.1), channel_id=1, source_target_pairs={{1,8},{3,10},{5,13},{7,15},{8,0},{10,2},{12,5},{14,7},{17,24},{19,... | collective-permute-start | bytes 6488072 | tf_op jit(solution)/shard_map/ppermute | solution.py:81
  16.4 17.0 %collective-permute-start.1 = (bf16[256,1280]{1,0:T(8,128)(2,1)S(1)}, bf16[256,1280]{1,0:T(8,128)(2,1)S(1)}, u32[]{:S(2)}, u32[]{:S(2)}) collective-permute-start(bf16[256,1280]{1,0:T(8,128)(2,1)S(1)} %get-tuple-element.37), channel_id=1, source_target_pairs={{0,4},{1,5},{2,6},{3,7},{4,0},{5,1},{6,2},{7,3},{8,12},{9,13},{10,... | collective-permute-start | bytes 1966088 | tf_op jit(solution)/shard_map/ppermute | solution.py:81
  16.4 30.4 %collective-permute-start.2 = (bf16[256,1280]{1,0:T(8,128)(2,1)S(1)}, bf16[256,1280]{1,0:T(8,128)(2,1)S(1)}, u32[]{:S(2)}, u32[]{:S(2)}) collective-permute-start(bf16[256,1280]{1,0:T(8,128)(2,1)S(1)} %get-tuple-element.38), channel_id=1, source_target_pairs={{0,2},{1,3},{2,0},{3,1},{4,6},{5,7},{6,4},{7,5},{8,10},{9,11},{10,... | collective-permute-start | bytes 1966088 | tf_op jit(solution)/shard_map/ppermute | solution.py:81
  17.8 29.9 %collective-permute-start.3 = (bf16[256,1280]{1,0:T(8,128)(2,1)S(1)}, bf16[256,1280]{1,0:T(8,128)(2,1)S(1)}, u32[]{:S(2)}, u32[]{:S(2)}) collective-permute-start(bf16[256,1280]{1,0:T(8,128)(2,1)S(1)} %get-tuple-element.39), channel_id=1, source_target_pairs={{0,6},{1,7},{2,4},{3,5},{4,2},{5,3},{6,0},{7,1},{8,14},{9,15},{10,... | collective-permute-start | bytes 1966088 | tf_op jit(solution)/shard_map/ppermute | solution.py:81
  19.1 33.3 %collective-permute-start = (bf16[256,1280]{1,0:T(8,128)(2,1)S(1)}, bf16[256,1280]{1,0:T(8,128)(2,1)}, u32[]{:S(2)}, u32[]{:S(2)}) collective-permute-start(bf16[256,1280]{1,0:T(8,128)(2,1)S(1)} %get-tuple-element.42.own_ref), channel_id=1, source_target_pairs={{0,16},{1,17},{2,18},{3,19},{4,20},{5,21},{6,22},{7,23},{8,24},{9,... | collective-permute-start | bytes 1966088 | tf_op jit(solution)/shard_map/ppermute | solution.py:81
  52.4 113.0 %all-gather.5.cloned.1.call-start = ((), (), s32[]{:S(2)}) async-start(), calls=%async_computation | async-start | bytes 7864320 | tf_op jit(solution)/shard_map/all_gather | solution.py:326
  59.1 9.6 %collective-permute-start.9 = (bf16[528,2048]{1,0:T(8,128)(2,1)S(1)}, bf16[528,2048]{1,0:T(8,128)(2,1)}, u32[]{:S(2)}, u32[]{:S(2)}) collective-permute-start(bf16[528,2048]{1,0:T(8,128)(2,1)S(1)} %stamp.1), channel_id=1, source_target_pairs={{4,5},{6,7},{9,8},{11,10},{20,21},{22,23},{25,24},{27,26}} | collective-permute-start | bytes 6488072 | tf_op jit(solution)/shard_map/ppermute | solution.py:81
  61.1 46.3 %collective-permute-start.8 = (bf16[528,2048]{1,0:T(8,128)(2,1)}, bf16[528,2048]{1,0:T(8,128)(2,1)}, u32[]{:S(2)}, u32[]{:S(2)}) collective-permute-start(bf16[528,2048]{1,0:T(8,128)(2,1)} %collective-permute-done.5.here), channel_id=1, source_target_pairs={{0,6},{2,4},{5,3},{7,1},{8,14},{10,12},{13,11},{15,9},{16,22},{18,... | collective-permute-start | bytes 6488072 | tf_op jit(solution)/shard_map/ppermute | solution.py:81
  62.4 45.0 %collective-permute-start.7 = (bf16[528,2048]{1,0:T(8,128)(2,1)}, bf16[528,2048]{1,0:T(8,128)(2,1)}, u32[]{:S(2)}, u32[]{:S(2)}) collective-permute-start(bf16[528,2048]{1,0:T(8,128)(2,1)} %collective-permute-done.5.here), channel_id=1, source_target_pairs={{0,2},{2,0},{5,7},{7,5},{8,10},{10,8},{13,15},{15,13},{16,18},{18,... | collective-permute-start | bytes 6488072 | tf_op jit(solution)/shard_map/ppermute | solution.py:81
  64.4 48.8 %collective-permute-start.6 = (bf16[528,2048]{1,0:T(8,128)(2,1)}, bf16[528,2048]{1,0:T(8,128)(2,1)}, u32[]{:S(2)}, u32[]{:S(2)}) collective-permute-start(bf16[528,2048]{1,0:T(8,128)(2,1)} %collective-permute-done.5.here), channel_id=1, source_target_pairs={{0,4},{2,6},{5,1},{7,3},{8,12},{10,14},{13,9},{15,11},{16,20},{18,... | collective-permute-start | bytes 6488072 | tf_op jit(solution)/shard_map/ppermute | solution.py:81
  65.7 41.7 %collective-permute-start.10 = (bf16[768,640]{1,0:T(8,128)(2,1)}, bf16[768,640]{1,0:T(8,128)(2,1)S(1)}, u32[]{:S(2)}, u32[]{:S(2)}) collective-permute-start(bf16[768,640]{1,0:T(8,128)(2,1)} %copy-done.30), channel_id=1, source_target_pairs={{0,16},{1,17},{2,18},{3,19},{4,20},{5,21},{6,22},{7,23},{8,24},{9,... | collective-permute-start | bytes 2949128 | tf_op jit(solution)/shard_map/ppermute | solution.py:81
  68.6 49.2 %copy-start.32 = (bf16[768,384]{1,0:T(8,128)(2,1)S(1)}, bf16[768,384]{1,0:T(8,128)(2,1)}, u32[]{:S(2)}) copy-start(bf16[768,384]{1,0:T(8,128)(2,1)} %copy-done.31) | copy-start | bytes 1769476
  68.7 73.9 %copy-start.34 = (bf16[768,256]{1,0:T(8,128)(2,1)S(1)}, bf16[768,256]{1,0:T(8,128)(2,1)}, u32[]{:S(2)}) copy-start(bf16[768,256]{1,0:T(8,128)(2,1)} %copy-done.33) | copy-start | bytes 1179652
  107.4 58.0 %copy-start.15 = (bf16[768,640]{1,0:T(8,128)(2,1)}, bf16[768,640]{1,0:T(8,128)(2,1)S(1)}, u32[]{:S(2)}) copy-start(bf16[768,640]{1,0:T(8,128)(2,1)S(1)} %collective-permute-done.10.refs_3_) | copy-start | bytes 2949124
  113.2 77.0 %collective-permute-start.13 = (bf16[528,2048]{1,0:T(8,128)(2,1)S(1)}, bf16[528,2048]{1,0:T(8,128)(2,1)}, u32[]{:S(2)}, u32[]{:S(2)}) collective-permute-start(bf16[528,2048]{1,0:T(8,128)(2,1)S(1)} %broadcast_select_fusion.here), channel_id=1, source_target_pairs={{0,6},{2,4},{5,3},{7,1},{8,14},{10,12},{13,11},{15,9},{16,22},{18,... | collective-permute-start | bytes 6488072 | tf_op jit(solution)/shard_map/ppermute | solution.py:81
  114.5 77.5 %collective-permute-start.12 = (bf16[528,2048]{1,0:T(8,128)(2,1)S(1)}, bf16[528,2048]{1,0:T(8,128)(2,1)}, u32[]{:S(2)}, u32[]{:S(2)}) collective-permute-start(bf16[528,2048]{1,0:T(8,128)(2,1)S(1)} %broadcast_select_fusion.here), channel_id=1, source_target_pairs={{0,2},{2,0},{5,7},{7,5},{8,10},{10,8},{13,15},{15,13},{16,18},{18,... | collective-permute-start | bytes 6488072 | tf_op jit(solution)/shard_map/ppermute | solution.py:81
  116.5 76.8 %collective-permute-start.11 = (bf16[528,2048]{1,0:T(8,128)(2,1)S(1)}, bf16[528,2048]{1,0:T(8,128)(2,1)}, u32[]{:S(2)}, u32[]{:S(2)}) collective-permute-start(bf16[528,2048]{1,0:T(8,128)(2,1)S(1)} %broadcast_select_fusion.here), channel_id=1, source_target_pairs={{0,4},{2,6},{5,1},{7,3},{8,12},{10,14},{13,9},{15,11},{16,20},{18,... | collective-permute-start | bytes 6488072 | tf_op jit(solution)/shard_map/ppermute | solution.py:81
  117.8 24.7 %collective-permute-start.15 = (bf16[768,384]{1,0:T(8,128)(2,1)S(1)}, bf16[768,384]{1,0:T(8,128)(2,1)}, u32[]{:S(2)}, u32[]{:S(2)}) collective-permute-start(bf16[768,384]{1,0:T(8,128)(2,1)S(1)} %copy-done.32), channel_id=1, source_target_pairs={{0,16},{1,17},{2,18},{3,19},{4,20},{5,21},{6,22},{7,23},{8,24},{9,... | collective-permute-start | bytes 1769480 | tf_op jit(solution)/shard_map/ppermute | solution.py:81
  120.8 43.4 %collective-permute-start.14 = (bf16[768,640]{1,0:T(8,128)(2,1)S(1)}, bf16[768,640]{1,0:T(8,128)(2,1)S(1)}, u32[]{:S(2)}, u32[]{:S(2)}) collective-permute-start(bf16[768,640]{1,0:T(8,128)(2,1)S(1)} %collective-permute-done.10.refs_3_), channel_id=1, source_target_pairs={{0,1},{1,0},{2,3},{3,2},{4,5},{5,4},{6,7},{7,6},{8,9},{9,8},{10,11... | collective-permute-start | bytes 2949128 | tf_op jit(solution)/shard_map/ppermute | solution.py:81
  142.6 8.7 %collective-permute-start.22 = (bf16[768,256]{1,0:T(8,128)(2,1)S(1)}, bf16[768,256]{1,0:T(8,128)(2,1)S(1)}, u32[]{:S(2)}, u32[]{:S(2)}) collective-permute-start(bf16[768,256]{1,0:T(8,128)(2,1)S(1)} %copy-done.34), channel_id=1, source_target_pairs={{0,16},{1,17},{2,18},{3,19},{4,20},{5,21},{6,22},{7,23},{8,24},{9,... | collective-permute-start | bytes 1179656 | tf_op jit(solution)/shard_map/ppermute | solution.py:81
  151.3 36.5 %copy-start.22 = (bf16[768,256]{1,0:T(8,128)(2,1)}, bf16[768,256]{1,0:T(8,128)(2,1)S(1)}, u32[]{:S(2)}) copy-start(bf16[768,256]{1,0:T(8,128)(2,1)S(1)} %collective-permute-done.22.refs_3_) | copy-start | bytes 1179652
  151.3 25.5 %collective-permute-start.23 = (bf16[768,256]{1,0:T(8,128)(2,1)S(1)}, bf16[768,256]{1,0:T(8,128)(2,1)}, u32[]{:S(2)}, u32[]{:S(2)}) collective-permute-start(bf16[768,256]{1,0:T(8,128)(2,1)S(1)} %collective-permute-done.22.refs_3_), channel_id=1, source_target_pairs={{0,1},{1,0},{2,3},{3,2},{4,5},{5,4},{6,7},{7,6},{8,9},{9,8},{10,11... | collective-permute-start | bytes 1179656 | tf_op jit(solution)/shard_map/ppermute | solution.py:81
  165.2 32.5 %collective-permute-start.19 = (bf16[768,384]{1,0:T(8,128)(2,1)}, bf16[768,384]{1,0:T(8,128)(2,1)}, u32[]{:S(2)}, u32[]{:S(2)}) collective-permute-start(bf16[768,384]{1,0:T(8,128)(2,1)} %collective-permute-done.15.refs_3_), channel_id=1, source_target_pairs={{0,1},{1,0},{2,3},{3,2},{4,5},{5,4},{6,7},{7,6},{8,9},{9,8},{10,11... | collective-permute-start | bytes 1769480 | tf_op jit(solution)/shard_map/ppermute | solution.py:81
  176.4 11.4 %copy-start.4 = (bf16[512,4096]{1,0:T(8,128)(2,1)S(1)}, bf16[512,4096]{1,0:T(8,128)(2,1)}, u32[]{:S(2)}) copy-start(bf16[512,4096]{1,0:T(8,128)(2,1)} %copy-done.2) | copy-start | bytes 12582916
  176.7 35.3 %collective-permute-start.16 = (f16[512,512]{1,0:T(8,128)(2,1)S(1)}, f16[512,512]{1,0:T(8,128)(2,1)S(1)}, u32[]{:S(2)}, u32[]{:S(2)}) collective-permute-start(f16[512,512]{1,0:T(8,128)(2,1)S(1)} %pad_maximum_fusion.2), channel_id=1, source_target_pairs={{0,8},{1,9},{2,10},{3,11},{4,12},{5,13},{6,14},{7,15},{8,0},{9,1},... | collective-permute-start | bytes 1572872 | tf_op jit(solution)/shard_map/ppermute | solution.py:81
  190.3 21.8 %collective-permute-start.24 = (f16[512,256]{1,0:T(8,128)(2,1)S(1)}, f16[512,256]{1,0:T(8,128)(2,1)S(1)}, u32[]{:S(2)}, u32[]{:S(2)}) collective-permute-start(f16[512,256]{1,0:T(8,128)(2,1)S(1)} %convert_element_type.19), channel_id=1, source_target_pairs={{0,8},{1,9},{2,10},{3,11},{4,12},{5,13},{6,14},{7,15},{8,0},{9,1},... | collective-permute-start | bytes 786440 | tf_op jit(solution)/shard_map/ppermute | solution.py:81
  192.0 20.3 %collective-permute-start.17 = (f32[512,128]{1,0:T(8,128)S(1)}, f32[512,128]{1,0:T(8,128)S(1)}, u32[]{:S(2)}, u32[]{:S(2)}) collective-permute-start(f32[512,128]{1,0:T(8,128)S(1)} %slice.25), channel_id=1, source_target_pairs={{0,8},{1,9},{2,10},{3,11},{4,12},{5,13},{6,14},{7,15},{8,0},{9,1},... | collective-permute-start | bytes 786440 | tf_op jit(solution)/shard_map/ppermute | solution.py:81
  193.1 4.7 %slice-start = ((s8[5242880]{0:T(1024)(128)(4,1)}), s8[4194304]{0:T(1024)(128)(4,1)S(1)}, s32[]{:S(2)}) async-start(s8[5242880]{0:T(1024)(128)(4,1)} %bitcast.4), calls=%async_computation.2 | async-start | bytes 8388608
  193.3 21.9 %copy-start.11 = (f32[512,128]{1,0:T(8,128)}, f32[512,128]{1,0:T(8,128)S(1)}, u32[]{:S(2)}) copy-start(f32[512,128]{1,0:T(8,128)S(1)} %get-tuple-element.70.refs_2_) | copy-start | bytes 786436
  193.3 21.9 %copy-start.13 = (f32[512,128]{1,0:T(8,128)}, f32[512,128]{1,0:T(8,128)S(1)}, u32[]{:S(2)}) copy-start(f32[512,128]{1,0:T(8,128)S(1)} %get-tuple-element.71.refs_3_) | copy-start | bytes 786436
  193.4 4.4 %slice-start.1 = ((s8[5242880]{0:T(1024)(128)(4,1)}), s8[1048576]{0:T(1024)(128)(4,1)S(1)}, s32[]{:S(2)}) async-start(s8[5242880]{0:T(1024)(128)(4,1)} %bitcast.4), calls=%async_computation.3 | async-start | bytes 2097152
  193.4 4.8 %copy-start.8 = (bf16[512,1280]{1,0:T(8,128)(2,1)S(1)}, bf16[512,1280]{1,0:T(8,128)(2,1)}, u32[]{:S(2)}) copy-start(bf16[512,1280]{1,0:T(8,128)(2,1)} %all-gather.7.cloned.1.call-done) | copy-start | bytes 3932164
  197.7 11.9 %copy-start.5 = (bf16[512,4096]{1,0:T(8,128)(2,1)}, bf16[512,4096]{1,0:T(8,128)(2,1)S(1)}, u32[]{:S(2)}) copy-start(bf16[512,4096]{1,0:T(8,128)(2,1)S(1)} %scale_rows.2.refs_0_) | copy-start | bytes 12582916
  197.7 8.1 %copy-start.16 = (bf16[768,640]{1,0:T(8,128)(2,1)S(1)}, bf16[768,640]{1,0:T(8,128)(2,1)}, u32[]{:S(2)}) copy-start(bf16[768,640]{1,0:T(8,128)(2,1)} %copy-done.15) | copy-start | bytes 2949124
  197.8 8.1 %copy-start.19 = (bf16[768,640]{1,0:T(8,128)(2,1)S(1)}, bf16[768,640]{1,0:T(8,128)(2,1)}, u32[]{:S(2)}) copy-start(bf16[768,640]{1,0:T(8,128)(2,1)} %copy-done.17) | copy-start | bytes 2949124
  204.4 5.2 %copy-start.23 = (bf16[768,256]{1,0:T(8,128)(2,1)S(1)}, bf16[768,256]{1,0:T(8,128)(2,1)}, u32[]{:S(2)}) copy-start(bf16[768,256]{1,0:T(8,128)(2,1)} %copy-done.22) | copy-start | bytes 1179652
  204.4 28.5 %collective-permute-start.20 = (f16[512,384]{1,0:T(8,128)(2,1)}, f16[512,384]{1,0:T(8,128)(2,1)}, u32[]{:S(2)}, u32[]{:S(2)}) collective-permute-start(f16[512,384]{1,0:T(8,128)(2,1)} %convert_element_type.17), channel_id=1, source_target_pairs={{0,8},{1,9},{2,10},{3,11},{4,12},{5,13},{6,14},{7,15},{8,0},{9,1},... | collective-permute-start | bytes 1179656 | tf_op jit(solution)/shard_map/ppermute | solution.py:81
  217.1 23.3 %collective-permute-start.25 = (bf16[512,256]{1,0:T(8,128)(2,1)S(1)}, bf16[512,256]{1,0:T(8,128)(2,1)}, u32[]{:S(2)}, u32[]{:S(2)}) collective-permute-start(bf16[512,256]{1,0:T(8,128)(2,1)S(1)} %attend.3), channel_id=1, source_target_pairs={{1,4},{3,6},{4,1},{6,3},{9,12},{11,14},{12,9},{14,11},{17,20},{19,... | collective-permute-start | bytes 786440 | tf_op jit(solution)/shard_map/ppermute | solution.py:81
  222.3 19.2 %collective-permute-start.18 = (bf16[512,384]{1,0:T(8,128)(2,1)S(1)}, bf16[512,384]{1,0:T(8,128)(2,1)}, u32[]{:S(2)}, u32[]{:S(2)}) collective-permute-start(bf16[512,384]{1,0:T(8,128)(2,1)S(1)} %get-tuple-element.62), channel_id=1, source_target_pairs={{1,4},{3,6},{4,1},{6,3},{9,12},{11,14},{12,9},{14,11},{17,20},{19,... | collective-permute-start | bytes 1179656 | tf_op jit(solution)/shard_map/ppermute | solution.py:81
  229.1 4.9 %copy-start.12 = (f32[512,128]{1,0:T(8,128)S(1)}, f32[512,128]{1,0:T(8,128)}, u32[]{:S(2)}) copy-start(f32[512,128]{1,0:T(8,128)} %copy-done.11) | copy-start | bytes 786436
  229.1 4.9 %copy-start.14 = (f32[512,128]{1,0:T(8,128)S(1)}, f32[512,128]{1,0:T(8,128)}, u32[]{:S(2)}) copy-start(f32[512,128]{1,0:T(8,128)} %copy-done.13) | copy-start | bytes 786436
  236.8 9.1 %collective-permute-start.21 = (bf16[512,384]{1,0:T(8,128)(2,1)S(1)}, bf16[512,384]{1,0:T(8,128)(2,1)S(1)}, u32[]{:S(2)}, u32[]{:S(2)}) collective-permute-start(bf16[512,384]{1,0:T(8,128)(2,1)S(1)} %attend.2), channel_id=1, source_target_pairs={{1,4},{3,6},{4,1},{6,3},{9,12},{11,14},{12,9},{14,11},{17,20},{19,... | collective-permute-start | bytes 1179656 | tf_op jit(solution)/shard_map/ppermute | solution.py:81
  (17 other events, 24.4 us)
Sparse Core Ops, SparseCore 0:
  52.5 11.0 all-gather.6
  65.2 17.4 all-gather.4

commit v3 on v2

--- a/solution.py
+++ b/solution.py
@@ -105,7 +105,7 @@
     return z ^ 2, x, y, c
 
 
-CHUNKS = ((0, 5), (5, 8), (8, 10))
+CHUNKS = ((0, 2), (2, 5), (5, 8), (8, 10))
 VMEM = 16 * 2**20
 
 
@@ -141,12 +141,12 @@
         out[:, 2 * HD :] = q_ref[:, pl.ds(pl.multiple_of(group * q_cols, HD), q_cols)]
 
 
-def rest_kernel(own_ref, a_ref, b_ref, c_ref, all_ref, *outs):
+def rest_kernel(own_ref, a_ref, b_ref, c_ref, far_ref, all_ref, *outs):
     own = a_ref.shape[0]
-    for i, ref in enumerate((own_ref, a_ref, b_ref, c_ref)):
+    for i, ref in enumerate((own_ref, a_ref, b_ref, c_ref, far_ref)):
         all_ref[i * own : (i + 1) * own, :] = ref[...]
         for out, (lo, hi) in zip(outs, CHUNKS):
-            if i > 0:
+            if 0 < i < 4:
                 out[(i - 1) * own : i * own, :] = ref[:, lo * HD : hi * HD]
 
 
@@ -175,16 +175,23 @@
 def scale_kernel(here, by_x, by_y, by_xy, out):
     z, x, y, c = place()
     rows, feats = out.shape[0], here.shape[1]
-    at = jnp.where(y == z >> 1, 0, feats)
+    own = feats // 8
+    near = y == z >> 1
 
     def fill(same, other):
         tiles = [ref[rows:, :].astype(jnp.float32) for ref in (same, other)]
         total = sum(tile[1:2, i * rows : (i + 1) * rows] for tile in tiles for i in range(3))
         scale = lax.rsqrt(total / (4 * feats) + 1e-05)
         scale = jnp.transpose(jnp.broadcast_to(scale, (HD, rows)))[:, :1]
-        for ref, tile, to in ((same, tiles[0], at), (other, tiles[1], feats - at)):
+        for ref, tile, is_near in ((same, tiles[0], near), (other, tiles[1], jnp.logical_not(near))):
             value = ref[:rows, :].astype(jnp.float32) * scale * tile[:1, :]
-            out[:, pl.ds(pl.multiple_of(to, feats), feats)] = value.astype(jnp.bfloat16)
+            value = value.astype(jnp.bfloat16)
+            for i in range(8):
+                core = (i & 1) ^ c
+                piece = (i >> 2 ^ x) + 2 * (i >> 1 & 1 ^ y)
+                at_far = jnp.where(piece == 0, 5 * core + 4, 9 + 3 * core + piece)
+                at = jnp.where(is_near, 5 * core + piece, at_far)
+                out[:, pl.ds(pl.multiple_of(at * own, own), own)] = value[:, i * own : (i + 1) * own]
 
     @pl.when(c == x)
     def _():
@@ -195,49 +202,43 @@
         fill(by_x, by_xy)
 
 
-def product_kernel(lo, hi, lhs, near_both, mine_both, rest, rest_core, out, near, far):
-    _, x, y, c = place()
-    own = mine_both.shape[1]
-    depth = near.shape[0]
-    span = slice(lo * HD, hi * HD)
-    for core, others in ((c, rest), (1 - c, rest_core)):
-        for i in range(4):
-            px = x if i % 2 == 0 else 1 - x
-            py = y if i < 2 else 1 - y
-            at = pl.ds(pl.multiple_of((4 * px + 2 * py + core) * own, own), own)
-            near[at, :] = near_both[core, i * own : (i + 1) * own, span]
-            far[at, :] = mine_both[core, :, span] if i == 0 else others[(i - 1) * own : i * own, :]
-    out[...] = jnp.dot(lhs[:, :depth], near[...], preferred_element_type=jnp.float32) + jnp.dot(
-        lhs[:, depth:], far[...], preferred_element_type=jnp.float32
-    )
+def dot(a, b):
+    return jnp.dot(a, b, preferred_element_type=jnp.float32)
+
+
+def early_kernel(lhs, mine, other, out):
+    depth = mine.shape[0]
+    out[...] = dot(lhs[:, :depth], mine[...]) + dot(lhs[:, depth : 2 * depth], other[...])
+
+
+def late_kernel(lo, hi, lhs, early, rest, rest_core, out):
+    depth = rest.shape[0]
+    start = lhs.shape[1] - 2 * depth
+    got = dot(lhs[:, start : start + depth], rest[...]) + dot(lhs[:, start + depth :], rest_core[...])
+    out[...] = got + early[:, lo * HD : hi * HD]
 
 
 def turn(value, cosine, sine):
     return (value * cosine + pltpu.roll(value, HD // 2, 1) * sine).astype(jnp.bfloat16)
 
 
-def attend_kernel(with_kv, *refs):
-    if with_kv:
-        near_ref, got_ref, cos_ref, sin_ref, out_ref, k_ref, v_ref = refs
-    else:
-        near_ref, got_ref, cos_ref, sin_ref, k_ref, v_ref, out_ref = refs
+def keys_kernel(near_ref, got_ref, cos_ref, sin_ref, k_ref, v_ref):
+    lin = near_ref[...] + got_ref[...]
+    k_ref[...] = turn(lin[:, :HD], cos_ref[...], sin_ref[...])
+    v_ref[...] = lin[:, HD:].astype(jnp.bfloat16)
+
+
+def attend_kernel(near_ref, got_ref, cos_ref, sin_ref, k_ref, v_ref, out_ref):
     rows = near_ref.shape[0]
     cosine, sine = cos_ref[...], sin_ref[...]
-
-    def head(h):
-        return near_ref[:, h * HD : (h + 1) * HD] + got_ref[:, h * HD : (h + 1) * HD]
-
-    if with_kv:
-        k_ref[...] = turn(head(0), cosine, sine)
-        v_ref[...] = head(1).astype(jnp.bfloat16)
-    skip = 2 if with_kv else 0
     half = rows // 2
     scale = 1.0 / (HD**0.5)
     above = lax.broadcasted_iota(jnp.int32, (half, half), 1) > lax.broadcasted_iota(
         jnp.int32, (half, half), 0
     )
     for h in range(out_ref.shape[1] // HD):
-        q = turn(head(h + skip), cosine, sine)
+        span = slice(h * HD, (h + 1) * HD)
+        q = turn(near_ref[:, span] + got_ref[:, span], cosine, sine)
         for block in range(2):
             mine = q[block * half : (block + 1) * half]
             parts = []
@@ -254,7 +255,7 @@
             got = jnp.dot(
                 probs, v_ref[: (block + 1) * half, :], preferred_element_type=jnp.float32
             )
-            out_ref[block * half : (block + 1) * half, h * HD : (h + 1) * HD] = got.astype(
+            out_ref[block * half : (block + 1) * half, span] = got.astype(
                 jnp.bfloat16
             )
 
@@ -284,98 +285,87 @@
         hidden_in, norm_gain[None, :], squares, move(squares, swap_c)
     )
     here_far = move(stamped, to_other_plane)
+    here_near = move(stamped, to_core)
+    for_xy, here_near = lax.optimization_barrier((for_xy, here_near))
+    here_near = jnp.where(home, stamped, here_near)
     far_mine = move(mine, swap_far)
     pieces = (move(for_x, swap_x), move(for_y, swap_y), move(for_xy, swap_xy))
-    mine, far_mine, pieces, here_far, later = lax.optimization_barrier(
-        (mine, far_mine, pieces, here_far, stamped)
+    mine, far_mine, pieces, here_near = lax.optimization_barrier(
+        (mine, far_mine, pieces, here_near)
     )
 
     widths = [(hi - lo) * HD for lo, hi in CHUNKS]
-    near_all, *rest = call(
+    mine_all, *rest = call(
         rest_kernel,
-        [jax.ShapeDtypeStruct((4 * own, cols), bf16)]
+        [jax.ShapeDtypeStruct((5 * own, cols), bf16)]
         + [jax.ShapeDtypeStruct((3 * own, n), bf16) for n in widths],
         name="rest",
-    )(mine, *pieces)
+    )(mine, *pieces, far_mine)
 
     def give(dx, dy):
         return lambda z, x, y, c: (z, x ^ dx, y ^ dy, c) if c == x else None
 
     def spread(block):
         return (block, move(block, give(1, 0)), move(block, give(0, 1)), move(block, give(1, 1)))
-
-    far_rest = [move(rest[0], swap_far)]
-    far_rows = spread(here_far)
-    here_near = jnp.where(home, later, move(later, to_core))
 
     def normed(blocks):
         shape = jax.ShapeDtypeStruct((rows, 2 * feats), bf16)
         return call(scale_kernel, shape, name="scale_rows")(*blocks)
 
-    far_rows, here_near, far_rest[0], rest[1] = lax.optimization_barrier(
-        (far_rows, here_near, far_rest[0], rest[1])
-    )
+    far_rest = [move(rest[0], swap_far)]
+    rest[1], far_rest[0] = lax.optimization_barrier((rest[1], far_rest[0]))
     far_rest.append(move(rest[1], swap_far))
+    far_rows = spread(here_far)
+    other_all = move(mine_all, swap_c)
+
+    far_rows, here_near, other_all, far_rest[0], far_rest[1], rest[2] = lax.optimization_barrier(
+        (far_rows, here_near, other_all, far_rest[0], far_rest[1], rest[2])
+    )
+    far_rest.append(move(rest[2], swap_far))
     near_rows = spread(here_near)
-    rest[2], far_rest[1], far_rows = lax.optimization_barrier((rest[2], far_rest[1], far_rows))
-    far_rest.append(move(rest[2], swap_far))
-    far_rows = normed(far_rows)
-    near_rows = normed(near_rows)
-
-    cores = [[0, 1], [2, 3]]
-    near_both = lax.all_gather(near_all, "tensor", axis_index_groups=cores)
-    far_mine_both = lax.all_gather(far_mine, "tensor", axis_index_groups=cores)
+
+    def start(blocks):
+        block = normed(blocks)
+        shape = jax.ShapeDtypeStruct((rows, cols), jnp.float32)
+        return block, call(early_kernel, shape, name="early")(block, mine_all, other_all)
+
+    def finish(block, early, j):
+        shape = jax.ShapeDtypeStruct((rows, widths[j]), jnp.float32)
+        return call(lambda *refs: late_kernel(*CHUNKS[j], *refs), shape, name="late")(
+            block, early, far_rest[j], rest_core[j]
+        )
+
+    def exchange(j):
+        part = finish(*far_part, j)
+        if j == 0:
+            return move(part, swap_near)
+        return move(part.astype(jnp.float16), swap_near).astype(jnp.float32)
+
+    rest_core = [move(part, swap_c) for part in far_rest[:2]]
+    far_part = start(far_rows)
+    first = finish(*far_part, 1)
+    rest[3], far_rest[2], first = lax.optimization_barrier((rest[3], far_rest[2], first))
+    far_rest.append(move(rest[3], swap_far))
+    rest_core += [move(part, swap_c) for part in far_rest[2:]]
+    sums = [exchange(0), move(first.astype(jnp.float16), swap_near).astype(jnp.float32)]
+    sums += [exchange(2), exchange(3)]
 
     cosine, sine = rotary_tables(rows, HD)
     cosine = jnp.concatenate([cosine, cosine], axis=1)
     sine = jnp.concatenate([-sine, sine], axis=1)
 
-    weights = [
-        (near_both, far_mine_both, far_rest[j], move(far_rest[j], swap_c))
-        for j in range(len(CHUNKS))
-    ]
-
-    def product(block, j):
-        lo, hi = CHUNKS[j]
-        n = (hi - lo) * HD
-        return call(
-            lambda *refs: product_kernel(lo, hi, *refs),
-            jax.ShapeDtypeStruct((rows, n), jnp.float32),
-            scratch=[pltpu.VMEM((feats, n), bf16)] * 2,
-            name="product",
-        )(block, *weights[j])
-
     def to_owner(z, x, y, c):
         return None if x == c else (z, c, y, x)
 
-    sums = []
-    for j, (lo, hi) in enumerate(CHUNKS):
-        sent = product(far_rows, j)
-        if lo == 0:
-            v_got = move(sent[:, HD : 2 * HD], swap_near)
-            sent = jnp.concatenate([sent[:, :HD], sent[:, 2 * HD :]], axis=1)
-        got = move(sent.astype(jnp.float16), swap_near).astype(jnp.float32)
-        if lo == 0:
-            got = jnp.concatenate([got[:, :HD], v_got, got[:, HD:]], axis=1)
-        sums.append(got)
-
+    near_part = start(near_rows)
     results = []
-    k_rot = v_val = None
-    for j, (lo, hi) in enumerate(CHUNKS):
-        args = (product(near_rows, j), sums[j], cosine, sine)
-        if lo == 0:
-            out, k_rot, v_val = call(
-                lambda *refs: attend_kernel(True, *refs),
-                [jax.ShapeDtypeStruct((rows, (hi - lo - 2) * HD), bf16)]
-                + [jax.ShapeDtypeStruct((rows, HD), bf16)] * 2,
-                name="attend_first",
-            )(*args)
-        else:
-            out = call(
-                lambda *refs: attend_kernel(False, *refs),
-                jax.ShapeDtypeStruct((rows, (hi - lo) * HD), bf16),
-                name="attend",
-            )(*args, k_rot, v_val)
+    k_rot, v_val = call(
+        keys_kernel, [jax.ShapeDtypeStruct((rows, HD), bf16)] * 2, name="keys"
+    )(finish(*near_part, 0), sums[0], cosine, sine)
+    for j in range(1, len(CHUNKS)):
+        out = call(attend_kernel, jax.ShapeDtypeStruct((rows, widths[j]), bf16), name="attend")(
+            finish(*near_part, j), sums[j], cosine, sine, k_rot, v_val
+        )
         results.append(jnp.where(direct, out, move(out, to_owner)))
     return jnp.concatenate(results, axis=1)
 

time: 255 us -> 215 us (0.84)
  waiting for transfers between devices: 97.2 us -> 126 us
  starting transfers between devices: 68.8 us -> 40.4 us
  local copies, waits for them, and re-layouts: 25.9 us -> 8.15 us
  between operations: 14 us -> 0.46 us
  Pallas kernels: 39.2 us -> 30.7 us
    ppermute x26 -> x29, waiting for transfers between devices: 97.2 us -> 126 us  [move(): return lax.ppermute(value, AXES, pairs)]
    ppermute x26 -> x29, starting transfers between devices: 68.8 us -> 40.4 us  [move(): return lax.ppermute(value, AXES, pairs)]
    unnamed x74 -> x30, local copies, waits for them, and re-layouts: 24.8 us -> 7.31 us
    pallas_call x10 -> x15, Pallas kernels: 29.3 us -> 23.4 us  [the longest x3 8.06 us: split_plan(): call(attend_kernel, jax.ShapeDtypeStruct((rows, widths[j]), bf16), name='...]
    pallas_call x2, Pallas kernels: 8.98 us -> 5.24 us  [normed(): return call(scale_kernel, shape, name='scale_rows')(*blocks)]
  transfers between devices with their start and end apart: 28 -> 29, of which waited for: 9 -> 14; matrix products, arithmetic and copies ran while one was open for 3% -> 4% of each run, Pallas kernels for 15% -> 14%
where the time goes in v3:
time: 215 us; the launch traced here: 214 us
  waiting for transfers between devices  126 us (59%)
  starting transfers between devices  40.4 us (19%)
  Pallas kernels  30.7 us (14%)
  other arithmetic  8.28 us (4%)
  local copies, waits for them, and re-layouts  8.15 us (4%)
    ppermute x29, waiting for transfers between devices, move(): return lax.ppermute(value, AXES, pairs)  126 us
    ppermute x29, starting transfers between devices, move(): return lax.ppermute(value, AXES, pairs)  40.4 us
    pallas_call x3, Pallas kernels, split_plan(): call(attend_kernel, jax.ShapeDtypeStruct((rows, widths[j]), bf16), name='...  8.06 us
    unnamed x30, local copies, waits for them, and re-layouts  7.31 us
    pallas_call x2, Pallas kernels, start(): call(early_kernel, shape, name='early')(block, mine_all, other_all)  7.1 us
    pallas_call x8, Pallas kernels, finish(): call(lambda *refs: late_kernel(*CHUNKS[j], *refs), shape, name='late')  6.22 us
    pallas_call x2, Pallas kernels, normed(): return call(scale_kernel, shape, name='scale_rows')(*blocks)  5.24 us
  transfers between devices with their start and end apart: 29, of which 14 were waited for; matrix products, arithmetic and copies ran while one was open for 4% of the time, Pallas kernels for 14%

profile of v3, /device:TPU:1, one launch (start us, length us, event | category | flops | bytes accessed | tf_op | source)
XLA Modules:
  0.0 214.0 jit_solution(13629648682789557713)
XLA Ops:
  0.0 1.6 copy-done.2
  4.3 6.4 %collective-permute-start.1 = (bf16[528,2048]{1,0:T(8,128)(2,1)S(1)}, bf16[528,2048]{1,0:T(8,128)(2,1)}, u32[]{:S(2)}, u32[]{:S(2)}) collective-permute-start(bf16[528,2048]{1,0:T(8,128)(2,1)S(1)} %stamp.1), channel_id=1, source_target_pairs={{1,8},{3,10},{5,13},{7,15},{8,0},{10,2},{12,5},{14,7},{17,24},{19,... | collective-permute-start | bytes 6488072 | tf_op jit(solution)/shard_map/ppermute | solution.py:81
  10.8 1.5 pack.1
  12.3 2.3 %collective-permute-start.5 = (bf16[256,1280]{1,0:T(8,128)(2,1)S(1)}, bf16[256,1280]{1,0:T(8,128)(2,1)S(1)}, u32[]{:S(2)}, u32[]{:S(2)}) collective-permute-start(bf16[256,1280]{1,0:T(8,128)(2,1)S(1)} %get-tuple-element.45.own_ref), channel_id=1, source_target_pairs={{0,16},{1,17},{2,18},{3,19},{4,20},{5,21},{6,22},{7,23},{8,24},{9,... | collective-permute-start | bytes 1966088 | tf_op jit(solution)/shard_map/ppermute | solution.py:81
  14.6 1.2 collective-permute-start.7
  15.8 1.4 copy-done.14
  17.2 1.4 collective-permute-start.9
  18.6 1.8 broadcast_select_fusion.here
  20.4 26.7 %collective-permute-done.5.far_ref = bf16[256,1280]{1,0:T(8,128)(2,1)S(1)} collective-permute-done((bf16[256,1280]{1,0:T(8,128)(2,1)S(1)}, bf16[256,1280]{1,0:T(8,128)(2,1)S(1)}, u32[]{:S(2)}, u32[]{:S(2)}) %collective-permute-start.5) | collective-permute-done | bytes 655392 | tf_op jit(solution)/shard_map/ppermute | solution.py:81
  47.1 1.8 rest.1
  49.1 1.3 collective-permute-start.2
  51.2 1.3 collective-permute-start.4
  52.5 2.9 %collective-permute-start.11 = (bf16[768,256]{1,0:T(8,128)(2,1)S(1)}, bf16[768,256]{1,0:T(8,128)(2,1)S(1)}, u32[]{:S(2)}, u32[]{:S(2)}) collective-permute-start(bf16[768,256]{1,0:T(8,128)(2,1)S(1)} %get-tuple-element.52), channel_id=1, source_target_pairs={{0,16},{1,17},{2,18},{3,19},{4,20},{5,21},{6,22},{7,23},{8,24},{9,... | collective-permute-start | bytes 1179656 | tf_op jit(solution)/shard_map/ppermute | solution.py:81
  55.4 15.0 %collective-permute-done.11.refs_2_ = bf16[768,256]{1,0:T(8,128)(2,1)S(1)} collective-permute-done((bf16[768,256]{1,0:T(8,128)(2,1)S(1)}, bf16[768,256]{1,0:T(8,128)(2,1)S(1)}, u32[]{:S(2)}, u32[]{:S(2)}) %collective-permute-start.11) | collective-permute-done | bytes 393248 | tf_op jit(solution)/shard_map/ppermute | solution.py:81
  70.3 12.2 %collective-permute-done.12.refs_2_ = bf16[768,384]{1,0:T(8,128)(2,1)S(1)} collective-permute-done((bf16[768,384]{1,0:T(8,128)(2,1)S(1)}, bf16[768,384]{1,0:T(8,128)(2,1)S(1)}, u32[]{:S(2)}, u32[]{:S(2)}) %collective-permute-start.12) | collective-permute-done | bytes 589856 | tf_op jit(solution)/shard_map/ppermute | solution.py:81
  82.5 18.5 %collective-permute-done.4.by_xy = bf16[528,2048]{1,0:T(8,128)(2,1)S(1)} collective-permute-done((bf16[528,2048]{1,0:T(8,128)(2,1)}, bf16[528,2048]{1,0:T(8,128)(2,1)S(1)}, u32[]{:S(2)}, u32[]{:S(2)}) %collective-permute-start.4) | collective-permute-done | bytes 2162720 | tf_op jit(solution)/shard_map/ppermute | solution.py:81
  101.0 1.3 collective-permute-start.13
  102.3 3.6 %collective-permute-start.16 = (bf16[768,384]{1,0:T(8,128)(2,1)S(1)}, bf16[768,384]{1,0:T(8,128)(2,1)S(1)}, u32[]{:S(2)}, u32[]{:S(2)}) collective-permute-start(bf16[768,384]{1,0:T(8,128)(2,1)S(1)} %collective-permute-done.12.refs_2_), channel_id=1, source_target_pairs={{0,1},{1,0},{2,3},{3,2},{4,5},{5,4},{6,7},{7,6},{8,9},{9,8},{10,11... | collective-permute-start | bytes 1769480 | tf_op jit(solution)/shard_map/ppermute | solution.py:81
  105.9 2.8 %collective-permute-start.17 = (bf16[768,384]{1,0:T(8,128)(2,1)S(1)}, bf16[768,384]{1,0:T(8,128)(2,1)S(1)}, u32[]{:S(2)}, u32[]{:S(2)}) collective-permute-start(bf16[768,384]{1,0:T(8,128)(2,1)S(1)} %get-tuple-element.60), channel_id=1, source_target_pairs={{0,16},{1,17},{2,18},{3,19},{4,20},{5,21},{6,22},{7,23},{8,24},{9,... | collective-permute-start | bytes 1769480 | tf_op jit(solution)/shard_map/ppermute | solution.py:81
  109.5 1.3 collective-permute-start.15
  110.8 3.4 %scale_rows.3.lhs.refs_0_ = bf16[512,4096]{1,0:T(8,128)(2,1)S(1)} custom-call(bf16[528,2048]{1,0:T(8,128)(2,1)} %collective-permute-done.1.here, bf16[528,2048]{1,0:T(8,128)(2,1)S(1)} %collective-permute-done.2.by_x, bf16[528,2048]{1,0:T(8,128)(2,1)S(1)} %collective-permute-done.3.by_y, bf16[528,2048]{1,0:T(8,128)(2,1)S(1)} %collective-permute-done.4.by_xy), custom_call_target="tpu_custom_call" | custom-call | bytes 8388608 | tf_op jit(solution)/shard_map/scale_rows/pallas_call | solution.py:313
  114.2 3.5 %early.3.refs_1_ = f32[512,1280]{1,0:T(8,128)S(1)} custom-call(bf16[512,4096]{1,0:T(8,128)(2,1)S(1)} %scale_rows.3.lhs.refs_0_, bf16[1280,1280]{1,0:T(8,128)(2,1)S(1)} %get-tuple-element.50.mine, bf16[1280,1280]{1,0:T(8,128)(2,1)S(1)} %collective-permute-done.10.other), custom_call_target="tpu_custom_call" | custom-call | bytes 5242880 | tf_op jit(solution)/shard_map/early/pallas_call | solution.py:330
  118.8 16.2 %collective-permute-done.17.refs_2_ = bf16[768,384]{1,0:T(8,128)(2,1)S(1)} collective-permute-done((bf16[768,384]{1,0:T(8,128)(2,1)S(1)}, bf16[768,384]{1,0:T(8,128)(2,1)S(1)}, u32[]{:S(2)}, u32[]{:S(2)}) %collective-permute-start.17) | collective-permute-done | bytes 589856 | tf_op jit(solution)/shard_map/ppermute | solution.py:81
  135.0 19.4 %collective-permute-done.25.refs_2_ = bf16[768,256]{1,0:T(8,128)(2,1)S(1)} collective-permute-done((bf16[768,256]{1,0:T(8,128)(2,1)S(1)}, bf16[768,256]{1,0:T(8,128)(2,1)S(1)}, u32[]{:S(2)}, u32[]{:S(2)}) %collective-permute-start.25) | collective-permute-done | bytes 393248 | tf_op jit(solution)/shard_map/ppermute | solution.py:81
  154.4 1.4 collective-permute-start.26
  155.8 1.3 collective-permute-done.26.refs_3_
  159.5 1.5 collective-permute-start.20
  162.9 3.5 %collective-permute-done.27 = f16[512,256]{1,0:T(8,128)(2,1)S(1)} collective-permute-done((f16[512,256]{1,0:T(8,128)(2,1)S(1)}, f16[512,256]{1,0:T(8,128)(2,1)S(1)}, u32[]{:S(2)}, u32[]{:S(2)}) %collective-permute-start.27) | collective-permute-done | bytes 262176 | tf_op jit(solution)/shard_map/ppermute | solution.py:81
  166.7 1.1 collective-permute-start.23
  169.2 1.8 scale_rows.2.lhs.refs_0_
  171.0 3.5 %early.2.refs_1_ = f32[512,1280]{1,0:T(8,128)S(1)} custom-call(bf16[512,4096]{1,0:T(8,128)(2,1)S(1)} %scale_rows.2.lhs.refs_0_, bf16[1280,1280]{1,0:T(8,128)(2,1)S(1)} %get-tuple-element.50.mine, bf16[1280,1280]{1,0:T(8,128)(2,1)S(1)} %collective-permute-done.10.other), custom_call_target="tpu_custom_call" | custom-call | bytes 5242880 | tf_op jit(solution)/shard_map/early/pallas_call | solution.py:330
  175.7 1.9 collective-permute-done.20.got_ref
  177.8 2.6 %attend.5 = bf16[512,256]{1,0:T(8,128)(2,1)} custom-call(f32[512,256]{1,0:T(8,128)S(1)} %late.14.near_ref, f32[512,256]{1,0:T(8,128)S(1)} %convert_element_type.23.got_ref, f32[512,128]{1,0:T(8,128)S(1)} %get-tuple-element.74.cos_ref, f32[512,128]{1,0:T(8,128)S(1)} %get-tuple-element.75.sin_ref, bf16[512,128]{1,0:T(8,128)(2,1)S(1)} %get-tuple-element.67.k_ref, ...), custom_call_target="tpu_custom_call" | custom-call | bytes 524288 | tf_op jit(solution)/shard_map/attend/pallas_call | solution.py:366
  180.4 2.6 %collective-permute-start.28 = (bf16[512,256]{1,0:T(8,128)(2,1)}, bf16[512,256]{1,0:T(8,128)(2,1)}, u32[]{:S(2)}, u32[]{:S(2)}) collective-permute-start(bf16[512,256]{1,0:T(8,128)(2,1)} %attend.5), channel_id=1, source_target_pairs={{1,4},{3,6},{4,1},{6,3},{9,12},{11,14},{12,9},{14,11},{17,20},{19,... | collective-permute-start | bytes 786440 | tf_op jit(solution)/shard_map/ppermute | solution.py:81
  183.1 3.0 %collective-permute-done.18 = f16[512,384]{1,0:T(8,128)(2,1)S(1)} collective-permute-done((f16[512,384]{1,0:T(8,128)(2,1)S(1)}, f16[512,384]{1,0:T(8,128)(2,1)S(1)}, u32[]{:S(2)}, u32[]{:S(2)}) %collective-permute-start.18) | collective-permute-done | bytes 393248 | tf_op jit(solution)/shard_map/ppermute | solution.py:81
  187.2 2.7 %attend.3 = bf16[512,384]{1,0:T(8,128)(2,1)S(1)} custom-call(f32[512,384]{1,0:T(8,128)S(1)} %late.8.near_ref, f32[512,384]{1,0:T(8,128)S(1)} %convert_element_type.19.got_ref, f32[512,128]{1,0:T(8,128)S(1)} %get-tuple-element.74.cos_ref, f32[512,128]{1,0:T(8,128)S(1)} %get-tuple-element.75.sin_ref, bf16[512,128]{1,0:T(8,128)(2,1)S(1)} %get-tuple-element.67.k_ref, ...), custom_call_target="tpu_custom_call" | custom-call | bytes 786432 | tf_op jit(solution)/shard_map/attend/pallas_call | solution.py:366
  189.9 2.7 %collective-permute-start.21 = (bf16[512,384]{1,0:T(8,128)(2,1)S(1)}, bf16[512,384]{1,0:T(8,128)(2,1)}, u32[]{:S(2)}, u32[]{:S(2)}) collective-permute-start(bf16[512,384]{1,0:T(8,128)(2,1)S(1)} %attend.3), channel_id=1, source_target_pairs={{1,4},{3,6},{4,1},{6,3},{9,12},{11,14},{12,9},{14,11},{17,20},{19,... | collective-permute-start | bytes 1179656 | tf_op jit(solution)/shard_map/ppermute | solution.py:81
  192.6 2.0 collective-permute-done.23
  194.6 1.0 convert_element_type.21.got_ref
  195.7 2.2 %copy-done.1 = bf16[512,4096]{1,0:T(8,128)(2,1)S(1)} copy-done((bf16[512,4096]{1,0:T(8,128)(2,1)S(1)}, bf16[512,4096]{1,0:T(8,128)(2,1)}, u32[]{:S(2)}) %copy-start.1) | copy-done | bytes 4194328
  197.9 1.1 copy-done.4
  198.9 1.1 copy-done.6
  201.0 2.7 %attend.4 = bf16[512,384]{1,0:T(8,128)(2,1)S(1)} custom-call(f32[512,384]{1,0:T(8,128)S(1)} %late.12.near_ref, f32[512,384]{1,0:T(8,128)S(1)} %convert_element_type.21.got_ref, f32[512,128]{1,0:T(8,128)S(1)} %get-tuple-element.74.cos_ref, f32[512,128]{1,0:T(8,128)S(1)} %get-tuple-element.75.sin_ref, bf16[512,128]{1,0:T(8,128)(2,1)S(1)} %copy-done.9, ...), custom_call_target="tpu_custom_call" | custom-call | bytes 786432 | tf_op jit(solution)/shard_map/attend/pallas_call | solution.py:366
  203.7 1.9 collective-permute-start.24
  205.7 1.0 broadcast_select_fusion.3
  206.7 1.1 broadcast_select_fusion.2
  207.7 5.1 %collective-permute-done.24 = bf16[512,384]{1,0:T(8,128)(2,1)S(1)} collective-permute-done((bf16[512,384]{1,0:T(8,128)(2,1)S(1)}, bf16[512,384]{1,0:T(8,128)(2,1)S(1)}, u32[]{:S(2)}, u32[]{:S(2)}) %collective-permute-start.24) | collective-permute-done | bytes 393248 | tf_op jit(solution)/shard_map/ppermute | solution.py:81
  212.9 1.1 pad_maximum_fusion
  (75 shorter events, 14.5 us)
Async XLA Ops:
  0.0 1.6 copy-start.2
  2.1 8.7 %copy-start.7 = (bf16[256,4096]{1,0:T(8,128)(2,1)S(1)}, bf16[256,4096]{1,0:T(8,128)(2,1)}, u32[]{:S(2)}) copy-start(bf16[256,4096]{1,0:T(8,128)(2,1)} %q_ref.1) | copy-start | bytes 6291460
  2.1 8.7 %copy-start.12 = (bf16[256,512]{1,0:T(8,128)(2,1)S(1)}, bf16[256,512]{1,0:T(8,128)(2,1)}, u32[]{:S(2)}) copy-start(bf16[256,512]{1,0:T(8,128)(2,1)} %k_ref.1) | copy-start | bytes 786436
  2.1 8.7 %copy-start.13 = (bf16[256,512]{1,0:T(8,128)(2,1)S(1)}, bf16[256,512]{1,0:T(8,128)(2,1)}, u32[]{:S(2)}) copy-start(bf16[256,512]{1,0:T(8,128)(2,1)} %v_ref.1) | copy-start | bytes 786436
  2.1 1.2 collective-permute-start
  3.5 12.3 %collective-permute-start.8 = (bf16[528,2048]{1,0:T(8,128)(2,1)S(1)}, bf16[528,2048]{1,0:T(8,128)(2,1)S(1)}, u32[]{:S(2)}, u32[]{:S(2)}) collective-permute-start(bf16[528,2048]{1,0:T(8,128)(2,1)S(1)} %stamp.1), channel_id=1, source_target_pairs={{4,5},{6,7},{9,8},{11,10},{20,21},{22,23},{25,24},{27,26}} | collective-permute-start | bytes 6488072 | tf_op jit(solution)/shard_map/ppermute | solution.py:81
  4.3 44.7 %collective-permute-start.1 = (bf16[528,2048]{1,0:T(8,128)(2,1)S(1)}, bf16[528,2048]{1,0:T(8,128)(2,1)}, u32[]{:S(2)}, u32[]{:S(2)}) collective-permute-start(bf16[528,2048]{1,0:T(8,128)(2,1)S(1)} %stamp.1), channel_id=1, source_target_pairs={{1,8},{3,10},{5,13},{7,15},{8,0},{10,2},{12,5},{14,7},{17,24},{19,... | collective-permute-start | bytes 6488072 | tf_op jit(solution)/shard_map/ppermute | solution.py:81
  12.3 34.9 %collective-permute-start.5 = (bf16[256,1280]{1,0:T(8,128)(2,1)S(1)}, bf16[256,1280]{1,0:T(8,128)(2,1)S(1)}, u32[]{:S(2)}, u32[]{:S(2)}) collective-permute-start(bf16[256,1280]{1,0:T(8,128)(2,1)S(1)} %get-tuple-element.45.own_ref), channel_id=1, source_target_pairs={{0,16},{1,17},{2,18},{3,19},{4,20},{5,21},{6,22},{7,23},{8,24},{9,... | collective-permute-start | bytes 1966088 | tf_op jit(solution)/shard_map/ppermute | solution.py:81
  14.6 32.6 %collective-permute-start.6 = (bf16[256,1280]{1,0:T(8,128)(2,1)}, bf16[256,1280]{1,0:T(8,128)(2,1)}, u32[]{:S(2)}, u32[]{:S(2)}) collective-permute-start(bf16[256,1280]{1,0:T(8,128)(2,1)} %get-tuple-element.39), channel_id=1, source_target_pairs={{0,4},{1,5},{2,6},{3,7},{4,0},{5,1},{6,2},{7,3},{8,12},{9,13},{10,... | collective-permute-start | bytes 1966088 | tf_op jit(solution)/shard_map/ppermute | solution.py:81
  14.6 32.6 %collective-permute-start.7 = (bf16[256,1280]{1,0:T(8,128)(2,1)}, bf16[256,1280]{1,0:T(8,128)(2,1)}, u32[]{:S(2)}, u32[]{:S(2)}) collective-permute-start(bf16[256,1280]{1,0:T(8,128)(2,1)} %get-tuple-element.40), channel_id=1, source_target_pairs={{0,2},{1,3},{2,0},{3,1},{4,6},{5,7},{6,4},{7,5},{8,10},{9,11},{10,... | collective-permute-start | bytes 1966088 | tf_op jit(solution)/shard_map/ppermute | solution.py:81
  15.8 1.4 copy-start.14
  17.2 30.0 %collective-permute-start.9 = (bf16[256,1280]{1,0:T(8,128)(2,1)}, bf16[256,1280]{1,0:T(8,128)(2,1)}, u32[]{:S(2)}, u32[]{:S(2)}) collective-permute-start(bf16[256,1280]{1,0:T(8,128)(2,1)} %get-tuple-element.42), channel_id=1, source_target_pairs={{0,6},{1,7},{2,4},{3,5},{4,2},{5,3},{6,0},{7,1},{8,14},{9,15},{10,... | collective-permute-start | bytes 1966088 | tf_op jit(solution)/shard_map/ppermute | solution.py:81
  49.0 52.0 %collective-permute-start.10 = (bf16[1280,1280]{1,0:T(8,128)(2,1)S(1)}, bf16[1280,1280]{1,0:T(8,128)(2,1)S(1)}, u32[]{:S(2)}, u32[]{:S(2)}) collective-permute-start(bf16[1280,1280]{1,0:T(8,128)(2,1)S(1)} %get-tuple-element.50.mine), channel_id=1, source_target_pairs={{0,1},{1,0},{2,3},{3,2},{4,5},{5,4},{6,7},{7,6},{8,9},{9,8},{10,11... | collective-permute-start | bytes 9830408 | tf_op jit(solution)/shard_map/ppermute | solution.py:81
  49.1 33.4 %collective-permute-start.2 = (bf16[528,2048]{1,0:T(8,128)(2,1)}, bf16[528,2048]{1,0:T(8,128)(2,1)S(1)}, u32[]{:S(2)}, u32[]{:S(2)}) collective-permute-start(bf16[528,2048]{1,0:T(8,128)(2,1)} %collective-permute-done.1.here), channel_id=1, source_target_pairs={{0,4},{2,6},{5,1},{7,3},{8,12},{10,14},{13,9},{15,11},{16,20},{18,... | collective-permute-start | bytes 6488072 | tf_op jit(solution)/shard_map/ppermute | solution.py:81
  50.4 32.1 %collective-permute-start.3 = (bf16[528,2048]{1,0:T(8,128)(2,1)}, bf16[528,2048]{1,0:T(8,128)(2,1)S(1)}, u32[]{:S(2)}, u32[]{:S(2)}) collective-permute-start(bf16[528,2048]{1,0:T(8,128)(2,1)} %collective-permute-done.1.here), channel_id=1, source_target_pairs={{0,2},{2,0},{5,7},{7,5},{8,10},{10,8},{13,15},{15,13},{16,18},{18,... | collective-permute-start | bytes 6488072 | tf_op jit(solution)/shard_map/ppermute | solution.py:81
  51.2 49.8 %collective-permute-start.4 = (bf16[528,2048]{1,0:T(8,128)(2,1)}, bf16[528,2048]{1,0:T(8,128)(2,1)S(1)}, u32[]{:S(2)}, u32[]{:S(2)}) collective-permute-start(bf16[528,2048]{1,0:T(8,128)(2,1)} %collective-permute-done.1.here), channel_id=1, source_target_pairs={{0,6},{2,4},{5,3},{7,1},{8,14},{10,12},{13,11},{15,9},{16,22},{18,... | collective-permute-start | bytes 6488072 | tf_op jit(solution)/shard_map/ppermute | solution.py:81
  52.5 17.8 %collective-permute-start.11 = (bf16[768,256]{1,0:T(8,128)(2,1)S(1)}, bf16[768,256]{1,0:T(8,128)(2,1)S(1)}, u32[]{:S(2)}, u32[]{:S(2)}) collective-permute-start(bf16[768,256]{1,0:T(8,128)(2,1)S(1)} %get-tuple-element.52), channel_id=1, source_target_pairs={{0,16},{1,17},{2,18},{3,19},{4,20},{5,21},{6,22},{7,23},{8,24},{9,... | collective-permute-start | bytes 1179656 | tf_op jit(solution)/shard_map/ppermute | solution.py:81
  70.3 12.2 %collective-permute-start.12 = (bf16[768,384]{1,0:T(8,128)(2,1)S(1)}, bf16[768,384]{1,0:T(8,128)(2,1)S(1)}, u32[]{:S(2)}, u32[]{:S(2)}) collective-permute-start(bf16[768,384]{1,0:T(8,128)(2,1)S(1)} %get-tuple-element.54), channel_id=1, source_target_pairs={{0,16},{1,17},{2,18},{3,19},{4,20},{5,21},{6,22},{7,23},{8,24},{9,... | collective-permute-start | bytes 1769480 | tf_op jit(solution)/shard_map/ppermute | solution.py:81
  101.0 65.7 %collective-permute-start.13 = (bf16[528,2048]{1,0:T(8,128)(2,1)S(1)}, bf16[528,2048]{1,0:T(8,128)(2,1)S(1)}, u32[]{:S(2)}, u32[]{:S(2)}) collective-permute-start(bf16[528,2048]{1,0:T(8,128)(2,1)S(1)} %broadcast_select_fusion.here), channel_id=1, source_target_pairs={{0,4},{2,6},{5,1},{7,3},{8,12},{10,14},{13,9},{15,11},{16,20},{18,... | collective-permute-start | bytes 6488072 | tf_op jit(solution)/shard_map/ppermute | solution.py:81
  102.3 15.5 %collective-permute-start.16 = (bf16[768,384]{1,0:T(8,128)(2,1)S(1)}, bf16[768,384]{1,0:T(8,128)(2,1)S(1)}, u32[]{:S(2)}, u32[]{:S(2)}) collective-permute-start(bf16[768,384]{1,0:T(8,128)(2,1)S(1)} %collective-permute-done.12.refs_2_), channel_id=1, source_target_pairs={{0,1},{1,0},{2,3},{3,2},{4,5},{5,4},{6,7},{7,6},{8,9},{9,8},{10,11... | collective-permute-start | bytes 1769480 | tf_op jit(solution)/shard_map/ppermute | solution.py:81
  105.9 29.1 %collective-permute-start.17 = (bf16[768,384]{1,0:T(8,128)(2,1)S(1)}, bf16[768,384]{1,0:T(8,128)(2,1)S(1)}, u32[]{:S(2)}, u32[]{:S(2)}) collective-permute-start(bf16[768,384]{1,0:T(8,128)(2,1)S(1)} %get-tuple-element.60), channel_id=1, source_target_pairs={{0,16},{1,17},{2,18},{3,19},{4,20},{5,21},{6,22},{7,23},{8,24},{9,... | collective-permute-start | bytes 1769480 | tf_op jit(solution)/shard_map/ppermute | solution.py:81
  108.7 60.4 %collective-permute-start.14 = (bf16[528,2048]{1,0:T(8,128)(2,1)S(1)}, bf16[528,2048]{1,0:T(8,128)(2,1)S(1)}, u32[]{:S(2)}, u32[]{:S(2)}) collective-permute-start(bf16[528,2048]{1,0:T(8,128)(2,1)S(1)} %broadcast_select_fusion.here), channel_id=1, source_target_pairs={{0,2},{2,0},{5,7},{7,5},{8,10},{10,8},{13,15},{15,13},{16,18},{18,... | collective-permute-start | bytes 6488072 | tf_op jit(solution)/shard_map/ppermute | solution.py:81
  109.5 59.6 %collective-permute-start.15 = (bf16[528,2048]{1,0:T(8,128)(2,1)S(1)}, bf16[528,2048]{1,0:T(8,128)(2,1)S(1)}, u32[]{:S(2)}, u32[]{:S(2)}) collective-permute-start(bf16[528,2048]{1,0:T(8,128)(2,1)S(1)} %broadcast_select_fusion.here), channel_id=1, source_target_pairs={{0,6},{2,4},{5,3},{7,1},{8,14},{10,12},{13,11},{15,9},{16,22},{18,... | collective-permute-start | bytes 6488072 | tf_op jit(solution)/shard_map/ppermute | solution.py:81
  135.0 26.1 %copy-start.3 = (bf16[768,384]{1,0:T(8,128)(2,1)}, bf16[768,384]{1,0:T(8,128)(2,1)S(1)}, u32[]{:S(2)}) copy-start(bf16[768,384]{1,0:T(8,128)(2,1)S(1)} %collective-permute-done.17.refs_2_) | copy-start | bytes 1769476
  135.0 19.4 %collective-permute-start.25 = (bf16[768,256]{1,0:T(8,128)(2,1)S(1)}, bf16[768,256]{1,0:T(8,128)(2,1)S(1)}, u32[]{:S(2)}, u32[]{:S(2)}) collective-permute-start(bf16[768,256]{1,0:T(8,128)(2,1)S(1)} %get-tuple-element.70), channel_id=1, source_target_pairs={{0,16},{1,17},{2,18},{3,19},{4,20},{5,21},{6,22},{7,23},{8,24},{9,... | collective-permute-start | bytes 1179656 | tf_op jit(solution)/shard_map/ppermute | solution.py:81
  154.4 2.8 %collective-permute-start.26 = (bf16[768,256]{1,0:T(8,128)(2,1)S(1)}, bf16[768,256]{1,0:T(8,128)(2,1)S(1)}, u32[]{:S(2)}, u32[]{:S(2)}) collective-permute-start(bf16[768,256]{1,0:T(8,128)(2,1)S(1)} %collective-permute-done.25.refs_2_), channel_id=1, source_target_pairs={{0,1},{1,0},{2,3},{3,2},{4,5},{5,4},{6,7},{7,6},{8,9},{9,8},{10,11... | collective-permute-start | bytes 1179656 | tf_op jit(solution)/shard_map/ppermute | solution.py:81
  155.8 3.7 %collective-permute-start.22 = (bf16[768,384]{1,0:T(8,128)(2,1)S(1)}, bf16[768,384]{1,0:T(8,128)(2,1)S(1)}, u32[]{:S(2)}, u32[]{:S(2)}) collective-permute-start(bf16[768,384]{1,0:T(8,128)(2,1)S(1)} %collective-permute-done.17.refs_2_), channel_id=1, source_target_pairs={{0,1},{1,0},{2,3},{3,2},{4,5},{5,4},{6,7},{7,6},{8,9},{9,8},{10,11... | collective-permute-start | bytes 1769480 | tf_op jit(solution)/shard_map/ppermute | solution.py:81
  157.2 1.7 collective-permute-start.19
  158.9 7.5 %collective-permute-start.27 = (f16[512,256]{1,0:T(8,128)(2,1)S(1)}, f16[512,256]{1,0:T(8,128)(2,1)S(1)}, u32[]{:S(2)}, u32[]{:S(2)}) collective-permute-start(f16[512,256]{1,0:T(8,128)(2,1)S(1)} %convert_element_type.22), channel_id=1, source_target_pairs={{0,8},{1,9},{2,10},{3,11},{4,12},{5,13},{6,14},{7,15},{8,0},{9,1},... | collective-permute-start | bytes 786440 | tf_op jit(solution)/shard_map/ppermute | solution.py:81
  159.5 2.6 %copy-start.5 = (bf16[768,384]{1,0:T(8,128)(2,1)}, bf16[768,384]{1,0:T(8,128)(2,1)S(1)}, u32[]{:S(2)}) copy-start(bf16[768,384]{1,0:T(8,128)(2,1)S(1)} %collective-permute-done.22.refs_3_) | copy-start | bytes 1769476
  159.5 18.2 %collective-permute-start.20 = (f32[512,256]{1,0:T(8,128)S(1)}, f32[512,256]{1,0:T(8,128)S(1)}, u32[]{:S(2)}, u32[]{:S(2)}) collective-permute-start(f32[512,256]{1,0:T(8,128)S(1)} %late.11), channel_id=1, source_target_pairs={{0,8},{1,9},{2,10},{3,11},{4,12},{5,13},{6,14},{7,15},{8,0},{9,1},... | collective-permute-start | bytes 1572872 | tf_op jit(solution)/shard_map/ppermute | solution.py:81
  166.4 19.7 %collective-permute-start.18 = (f16[512,384]{1,0:T(8,128)(2,1)S(1)}, f16[512,384]{1,0:T(8,128)(2,1)S(1)}, u32[]{:S(2)}, u32[]{:S(2)}) collective-permute-start(f16[512,384]{1,0:T(8,128)(2,1)S(1)} %convert_element_type.18), channel_id=1, source_target_pairs={{0,8},{1,9},{2,10},{3,11},{4,12},{5,13},{6,14},{7,15},{8,0},{9,1},... | collective-permute-start | bytes 1179656 | tf_op jit(solution)/shard_map/ppermute | solution.py:81
  166.7 27.9 %collective-permute-start.23 = (f16[512,384]{1,0:T(8,128)(2,1)}, f16[512,384]{1,0:T(8,128)(2,1)}, u32[]{:S(2)}, u32[]{:S(2)}) collective-permute-start(f16[512,384]{1,0:T(8,128)(2,1)} %convert_element_type.20), channel_id=1, source_target_pairs={{0,8},{1,9},{2,10},{3,11},{4,12},{5,13},{6,14},{7,15},{8,0},{9,1},... | collective-permute-start | bytes 1179656 | tf_op jit(solution)/shard_map/ppermute | solution.py:81
  171.0 15.1 %copy-start = (bf16[512,4096]{1,0:T(8,128)(2,1)}, bf16[512,4096]{1,0:T(8,128)(2,1)S(1)}, u32[]{:S(2)}) copy-start(bf16[512,4096]{1,0:T(8,128)(2,1)S(1)} %scale_rows.2.lhs.refs_0_) | copy-start | bytes 12582916
  177.8 9.3 %copy-start.8 = (bf16[512,128]{1,0:T(8,128)(2,1)}, bf16[512,128]{1,0:T(8,128)(2,1)S(1)}, u32[]{:S(2)}) copy-start(bf16[512,128]{1,0:T(8,128)(2,1)S(1)} %get-tuple-element.67.k_ref) | copy-start | bytes 393220
  177.8 9.3 %copy-start.10 = (bf16[512,128]{1,0:T(8,128)(2,1)}, bf16[512,128]{1,0:T(8,128)(2,1)S(1)}, u32[]{:S(2)}) copy-start(bf16[512,128]{1,0:T(8,128)(2,1)S(1)} %get-tuple-element.68.v_ref) | copy-start | bytes 393220
  180.4 25.3 %collective-permute-start.28 = (bf16[512,256]{1,0:T(8,128)(2,1)}, bf16[512,256]{1,0:T(8,128)(2,1)}, u32[]{:S(2)}, u32[]{:S(2)}) collective-permute-start(bf16[512,256]{1,0:T(8,128)(2,1)} %attend.5), channel_id=1, source_target_pairs={{1,4},{3,6},{4,1},{6,3},{9,12},{11,14},{12,9},{14,11},{17,20},{19,... | collective-permute-start | bytes 786440 | tf_op jit(solution)/shard_map/ppermute | solution.py:81
  189.9 16.8 %collective-permute-start.21 = (bf16[512,384]{1,0:T(8,128)(2,1)S(1)}, bf16[512,384]{1,0:T(8,128)(2,1)}, u32[]{:S(2)}, u32[]{:S(2)}) collective-permute-start(bf16[512,384]{1,0:T(8,128)(2,1)S(1)} %attend.3), channel_id=1, source_target_pairs={{1,4},{3,6},{4,1},{6,3},{9,12},{11,14},{12,9},{14,11},{17,20},{19,... | collective-permute-start | bytes 1179656 | tf_op jit(solution)/shard_map/ppermute | solution.py:81
  195.7 2.2 %copy-start.1 = (bf16[512,4096]{1,0:T(8,128)(2,1)S(1)}, bf16[512,4096]{1,0:T(8,128)(2,1)}, u32[]{:S(2)}) copy-start(bf16[512,4096]{1,0:T(8,128)(2,1)} %copy-done) | copy-start | bytes 12582916
  197.8 1.1 copy-start.4
  198.9 1.1 copy-start.6
  200.0 1.0 copy-start.9
  200.0 1.0 copy-start.11
  203.7 9.1 %collective-permute-start.24 = (bf16[512,384]{1,0:T(8,128)(2,1)S(1)}, bf16[512,384]{1,0:T(8,128)(2,1)S(1)}, u32[]{:S(2)}, u32[]{:S(2)}) collective-permute-start(bf16[512,384]{1,0:T(8,128)(2,1)S(1)} %attend.4), channel_id=1, source_target_pairs={{1,4},{3,6},{4,1},{6,3},{9,12},{11,14},{12,9},{14,11},{17,20},{19,... | collective-permute-start | bytes 1179656 | tf_op jit(solution)/shard_map/ppermute | solution.py:81

commit v4 on v3

--- a/solution.py
+++ b/solution.py
@@ -105,8 +105,16 @@
     return z ^ 2, x, y, c
 
 
-CHUNKS = ((0, 2), (2, 5), (5, 8), (8, 10))
-VMEM = 16 * 2**20
+CHUNKS = ((0, 3), (3, 5), (5, 8), (8, 10))
+PARTS = (
+    ((0, 1), ((1, 0), (1, 1), (0, 0), (0, 1), (0, 2))),
+    ((2,), ((0, 0), (0, 1), (0, 2))),
+    ((3,), ((0, 0), (0, 1))),
+)
+VMEM = {
+    "pack": 8, "squares": 6, "stamp": 6, "rest": 10, "scale_rows": 16, "early": 15,
+    "late": 14, "whole": 18, "keys": 4, "attend": 6, "place": 5,
+}
 
 
 def place():
@@ -118,14 +126,13 @@
     return lax.dynamic_index_in_dim(pair, index, 0, keepdims=False)
 
 
-def call(kernel, out_shape, scratch=(), flops=0, name=None):
+def call(kernel, out_shape, name=None, flops=0):
     shapes = out_shape if isinstance(out_shape, (list, tuple)) else (out_shape,)
     size = sum(2 * s.size * s.dtype.itemsize for s in shapes)
     return pl.pallas_call(
         kernel,
         out_shape=out_shape,
-        scratch_shapes=scratch,
-        compiler_params=pltpu.CompilerParams(vmem_limit_bytes=VMEM),
+        compiler_params=pltpu.CompilerParams(vmem_limit_bytes=VMEM[name] * 2**20),
         cost_estimate=pl.CostEstimate(flops=flops, bytes_accessed=size, transcendentals=0),
         name=name,
     )
@@ -172,30 +179,40 @@
     out[rows:, :] = jnp.concatenate([tile, tile], axis=0).astype(jnp.bfloat16)
 
 
-def scale_kernel(here, by_x, by_y, by_xy, out):
+def scale_kernel(here, by_x, by_y, by_xy, *refs):
     z, x, y, c = place()
+    out = refs[-1]
     rows, feats = out.shape[0], here.shape[1]
     own = feats // 8
     near = y == z >> 1
+    home = jnp.logical_and(len(refs) > 1, c == z & 1)
+    kept = refs[0] if len(refs) > 1 else here
 
     def fill(same, other):
         tiles = [ref[rows:, :].astype(jnp.float32) for ref in (same, other)]
         total = sum(tile[1:2, i * rows : (i + 1) * rows] for tile in tiles for i in range(3))
         scale = lax.rsqrt(total / (4 * feats) + 1e-05)
         scale = jnp.transpose(jnp.broadcast_to(scale, (HD, rows)))[:, :1]
-        for ref, tile, is_near in ((same, tiles[0], near), (other, tiles[1], jnp.logical_not(near))):
-            value = ref[:rows, :].astype(jnp.float32) * scale * tile[:1, :]
-            value = value.astype(jnp.bfloat16)
+        for ref, tile, is_near in (
+            (same, tiles[0], near), (other, tiles[1], jnp.logical_not(near))
+        ):
             for i in range(8):
+                span = slice(i * own, (i + 1) * own)
                 core = (i & 1) ^ c
                 piece = (i >> 2 ^ x) + 2 * (i >> 1 & 1 ^ y)
                 at_far = jnp.where(piece == 0, 5 * core + 4, 9 + 3 * core + piece)
                 at = jnp.where(is_near, 5 * core + piece, at_far)
-                out[:, pl.ds(pl.multiple_of(at * own, own), own)] = value[:, i * own : (i + 1) * own]
-
-    @pl.when(c == x)
+                to = pl.ds(pl.multiple_of(at * own, own), own)
+                value = ref[:rows, span].astype(jnp.float32) * scale * tile[:1, span]
+                out[:, to] = value.astype(jnp.bfloat16)
+
+    @pl.when(jnp.logical_and(c == x, jnp.logical_not(home)))
     def _():
         fill(here, by_y)
+
+    @pl.when(jnp.logical_and(c == x, home))
+    def _():
+        fill(kept, by_y)
 
     @pl.when(c != x)
     def _():
@@ -206,16 +223,66 @@
     return jnp.dot(a, b, preferred_element_type=jnp.float32)
 
 
-def early_kernel(lhs, mine, other, out):
+def early_kernel(lhs, *refs):
+    total, at = 0.0, 0
+    for ref in refs[:-1]:
+        total = total + dot(lhs[:, at : at + ref.shape[0]], ref[...])
+        at += ref.shape[0]
+    refs[-1][...] = total
+
+
+def late_kernel(chunks, places, lhs, early, *refs):
+    count = len(chunks)
+    outs = refs[2 * count :]
+    places = iter(places)
+    for j, rest, rest_core in zip(chunks, refs[:count], refs[count : 2 * count]):
+        depth = rest.shape[0]
+        start = lhs.shape[1] - 2 * depth
+        lo, hi = CHUNKS[j]
+        got = dot(lhs[:, start : start + depth], rest[...])
+        got = got + dot(lhs[:, start + depth :], rest_core[...]) + early[:, lo * HD : hi * HD]
+        for h in range(hi - lo):
+            i, at = next(places)
+            outs[i][:, at * HD : (at + 1) * HD] = got[:, h * HD : (h + 1) * HD]
+
+
+def whole_kernel(lhs, mine, other, *refs):
+    count = len(CHUNKS)
+    rest, rest_core, outs = refs[:count], refs[count : 2 * count], list(refs[2 * count :])
     depth = mine.shape[0]
-    out[...] = dot(lhs[:, :depth], mine[...]) + dot(lhs[:, depth : 2 * depth], other[...])
-
-
-def late_kernel(lo, hi, lhs, early, rest, rest_core, out):
-    depth = rest.shape[0]
-    start = lhs.shape[1] - 2 * depth
-    got = dot(lhs[:, start : start + depth], rest[...]) + dot(lhs[:, start + depth :], rest_core[...])
-    out[...] = got + early[:, lo * HD : hi * HD]
+    for chunks, places in PARTS:
+        parts = [outs.pop(0) for _ in range(1 + max(i for i, _ in places))]
+        places = iter(places)
+        for j in chunks:
+            lo, hi = CHUNKS[j]
+            span = slice(lo * HD, hi * HD)
+            got, at = 0.0, 0
+            for weight in (mine[:, span], other[:, span], rest[j][...], rest_core[j][...]):
+                got = got + dot(lhs[:, at : at + weight.shape[0]], weight)
+                at += weight.shape[0]
+            for h in range(hi - lo):
+                i, to = next(places)
+                parts[i][:, to * HD : (to + 1) * HD] = got[:, h * HD : (h + 1) * HD]
+
+
+def place_kernel(*refs):
+    _, x, _, c = place()
+    out = refs[-1]
+    count = len(refs) // 2
+
+    def fill(parts):
+        at = 0
+        for ref in parts:
+            out[:, at : at + ref.shape[1]] = ref[...]
+            at += ref.shape[1]
+
+    @pl.when(c == x)
+    def _():
+        fill(refs[:count])
+
+    @pl.when(c != x)
+    def _():
+        fill(refs[count:-1])
 
 
 def turn(value, cosine, sine):
@@ -285,89 +352,104 @@
         hidden_in, norm_gain[None, :], squares, move(squares, swap_c)
     )
     here_far = move(stamped, to_other_plane)
-    here_near = move(stamped, to_core)
-    for_xy, here_near = lax.optimization_barrier((for_xy, here_near))
-    here_near = jnp.where(home, stamped, here_near)
     far_mine = move(mine, swap_far)
     pieces = (move(for_x, swap_x), move(for_y, swap_y), move(for_xy, swap_xy))
-    mine, far_mine, pieces, here_near = lax.optimization_barrier(
-        (mine, far_mine, pieces, here_near)
-    )
-
-    widths = [(hi - lo) * HD for lo, hi in CHUNKS]
+    mine, far_mine, pieces = lax.optimization_barrier((mine, far_mine, pieces))
     mine_all, *rest = call(
         rest_kernel,
         [jax.ShapeDtypeStruct((5 * own, cols), bf16)]
-        + [jax.ShapeDtypeStruct((3 * own, n), bf16) for n in widths],
+        + [jax.ShapeDtypeStruct((3 * own, (hi - lo) * HD), bf16) for lo, hi in CHUNKS],
         name="rest",
     )(mine, *pieces, far_mine)
 
-    def give(dx, dy):
+    def give_far(dx, dy):
         return lambda z, x, y, c: (z, x ^ dx, y ^ dy, c) if c == x else None
 
-    def spread(block):
-        return (block, move(block, give(1, 0)), move(block, give(0, 1)), move(block, give(1, 1)))
+    def give_near(dx, dy):
+        return lambda z, x, y, c: (z, x ^ dx, y ^ dy, x) if c == z & 1 else None
+
+    def spread(block, give):
+        return [move(block, give(1, 0)), move(block, give(0, 1)), move(block, give(1, 1))]
 
     def normed(blocks):
         shape = jax.ShapeDtypeStruct((rows, 2 * feats), bf16)
-        return call(scale_kernel, shape, name="scale_rows")(*blocks)
-
+        return call(scale_kernel, shape, name="scale_rows", flops=2 * 10**10)(*blocks)
+
+    here_far, rest, mine_all = lax.optimization_barrier((here_far, rest, mine_all))
+    far_rows = [here_far, *spread(here_far, give_far)]
     far_rest = [move(rest[0], swap_far)]
     rest[1], far_rest[0] = lax.optimization_barrier((rest[1], far_rest[0]))
     far_rest.append(move(rest[1], swap_far))
-    far_rows = spread(here_far)
-    other_all = move(mine_all, swap_c)
-
-    far_rows, here_near, other_all, far_rest[0], far_rest[1], rest[2] = lax.optimization_barrier(
-        (far_rows, here_near, other_all, far_rest[0], far_rest[1], rest[2])
-    )
-    far_rest.append(move(rest[2], swap_far))
-    near_rows = spread(here_near)
-
-    def start(blocks):
-        block = normed(blocks)
-        shape = jax.ShapeDtypeStruct((rows, cols), jnp.float32)
-        return block, call(early_kernel, shape, name="early")(block, mine_all, other_all)
-
-    def finish(block, early, j):
-        shape = jax.ShapeDtypeStruct((rows, widths[j]), jnp.float32)
-        return call(lambda *refs: late_kernel(*CHUNKS[j], *refs), shape, name="late")(
-            block, early, far_rest[j], rest_core[j]
-        )
-
-    def exchange(j):
-        part = finish(*far_part, j)
-        if j == 0:
-            return move(part, swap_near)
-        return move(part.astype(jnp.float16), swap_near).astype(jnp.float32)
-
-    rest_core = [move(part, swap_c) for part in far_rest[:2]]
-    far_part = start(far_rows)
-    first = finish(*far_part, 1)
-    rest[3], far_rest[2], first = lax.optimization_barrier((rest[3], far_rest[2], first))
-    far_rest.append(move(rest[3], swap_far))
-    rest_core += [move(part, swap_c) for part in far_rest[2:]]
-    sums = [exchange(0), move(first.astype(jnp.float16), swap_near).astype(jnp.float32)]
-    sums += [exchange(2), exchange(3)]
-
     cosine, sine = rotary_tables(rows, HD)
     cosine = jnp.concatenate([cosine, cosine], axis=1)
     sine = jnp.concatenate([-sine, sine], axis=1)
+    other_all, here_near = move(mine_all, swap_c), move(stamped, to_core)
+    rest_core = [move(far_rest[0], swap_c)]
+    far_block = normed(far_rows)
+    far_block, far_rest, rest_core, stamped, here_near, other_all, rest[2], cosine, sine = (
+        lax.optimization_barrier(
+            (far_block, far_rest, rest_core, stamped, here_near, other_all, rest[2], cosine, sine)
+        )
+    )
+
+    near_rows = spread(stamped, give_near)
+    far_rest.append(move(rest[2], swap_far))
+    rest_core.append(move(far_rest[1], swap_c))
+    rest[3], far_rest[2] = lax.optimization_barrier((rest[3], far_rest[2]))
+    far_rest.append(move(rest[3], swap_far))
+    rest_core.append(move(far_rest[2], swap_c))
+
+    def start(block):
+        shape = jax.ShapeDtypeStruct((rows, cols), jnp.float32)
+        return block, call(early_kernel, shape, name="early")(block, mine_all, other_all)
+
+    def finish(block, early, i):
+        chunks, places = PARTS[i]
+        widths = [HD * sum(out == j for out, _ in places) for j in range(2)]
+        shapes = [jax.ShapeDtypeStruct((rows, n), jnp.float32) for n in widths if n > 0]
+        return call(lambda *refs: late_kernel(chunks, places, *refs), shapes, name="late")(
+            block, early, *[far_rest[j] for j in chunks], *[rest_core[j] for j in chunks]
+        )
+
+    def send(part):
+        return move(part.astype(jnp.float16), swap_near)
+
+    far_part = start(far_block)
+    part, kv_part = finish(*far_part, 0)
+    kv_sum, sums = move(kv_part, swap_near), [send(part)]
+    near_block = normed((here_near, *near_rows, stamped))
+    near_block, far_rest, rest_core, kv_sum, sums = lax.optimization_barrier(
+        (near_block, far_rest, rest_core, kv_sum, sums)
+    )
+    sums.append(send(finish(*far_part, 1)[0]))
+    rest_core.append(move(far_rest[3], swap_c))
+    part = finish(*far_part, 2)[0]
+    sums.append(send(part))
+    near_block, part = lax.optimization_barrier((near_block, part))
 
     def to_owner(z, x, y, c):
         return None if x == c else (z, c, y, x)
 
-    near_part = start(near_rows)
-    results = []
+    widths = [[HD * sum(i == j for i, _ in places) for j in range(2)] for _, places in PARTS]
+    part, kv_part, *parts = call(
+        whole_kernel,
+        [jax.ShapeDtypeStruct((rows, n), jnp.float32) for ns in widths for n in ns if n > 0],
+        name="whole",
+    )(near_block, mine_all, other_all, *far_rest, *rest_core)
+    parts = [part, *parts]
     k_rot, v_val = call(
         keys_kernel, [jax.ShapeDtypeStruct((rows, HD), bf16)] * 2, name="keys"
-    )(finish(*near_part, 0), sums[0], cosine, sine)
-    for j in range(1, len(CHUNKS)):
-        out = call(attend_kernel, jax.ShapeDtypeStruct((rows, widths[j]), bf16), name="attend")(
-            finish(*near_part, j), sums[j], cosine, sine, k_rot, v_val
+    )(kv_part, kv_sum, cosine, sine)
+    outs = [
+        call(attend_kernel, jax.ShapeDtypeStruct(part.shape, bf16), name="attend")(
+            part, got.astype(jnp.float32), cosine, sine, k_rot, v_val
         )
-        results.append(jnp.where(direct, out, move(out, to_owner)))
-    return jnp.concatenate(results, axis=1)
+        for part, got in zip(parts, sums)
+    ]
+    came = [move(out, to_owner) for out in outs]
+    return call(place_kernel, jax.ShapeDtypeStruct((rows, q_weight.shape[1] // 4), bf16), name="place")(
+        *outs, *came
+    )
 
 
 def solution(mesh):

time: 215 us -> 194 us (0.902)
  waiting for transfers between devices: 126 us -> 86.9 us
  starting transfers between devices: 40.4 us -> 75.9 us
  other arithmetic: 8.28 us -> 1.49 us
  local copies, waits for them, and re-layouts: 8.15 us -> 2.46 us
  Pallas kernels: 30.7 us -> 26.5 us
    ppermute x29, waiting for transfers between devices: 126 us -> 86.9 us  [move(): return lax.ppermute(value, AXES, pairs)]
    ppermute x29, starting transfers between devices: 40.4 us -> 75.9 us  [move(): return lax.ppermute(value, AXES, pairs)]
    unnamed x30 -> x10, local copies, waits for them, and re-layouts: 7.31 us -> 1.61 us
    select_n x4 -> x0, other arithmetic: 3.93 us -> none  [the longest x3 2.1 us: split_plan(): results.append(jnp.where(direct, out, move(out, to_owner)))]
    pallas_call x2 -> x1, Pallas kernels: 7.1 us -> 3.55 us  [start(): call(early_kernel, shape, name='early')(block, mine_all, other_all)]
    pallas_call x13 -> x10, Pallas kernels: 19.5 us -> 21.5 us  [the longest x3 7.38 us: split_plan(): call(attend_kernel, jax.ShapeDtypeStruct(part.shape, bf16), name='attend')]
  transfers between devices with their start and end apart: 29 -> 29, of which waited for: 14 -> 8; matrix products, arithmetic and copies ran while one was open for 4% -> 1% of each run, Pallas kernels for 14% -> 13%
where the time goes in v4:
time: 194 us
  waiting for transfers between devices  86.9 us (45%)
  starting transfers between devices  75.9 us (39%)
  Pallas kernels  26.5 us (14%)
  local copies, waits for them, and re-layouts  2.46 us (1%)
    ppermute x29, waiting for transfers between devices, move(): return lax.ppermute(value, AXES, pairs)  86.9 us
    ppermute x29, starting transfers between devices, move(): return lax.ppermute(value, AXES, pairs)  75.9 us
    pallas_call x3, Pallas kernels, split_plan(): call(attend_kernel, jax.ShapeDtypeStruct(part.shape, bf16), name='attend')  7.38 us
    pallas_call x1, Pallas kernels, split_plan(): call(whole_kernel, [jax.ShapeDtypeStruct((rows, n), jnp.float32) for ns i...  6.65 us
  transfers between devices with their start and end apart: 29, of which 8 were waited for; matrix products, arithmetic and copies ran while one was open for 1% of the time, Pallas kernels for 13%

profile of v4, /device:TPU:1, one launch (start us, length us, event | category | flops | bytes accessed | tf_op | source)
XLA Modules:
  0.0 193.7 jit_solution(1684265527966000364)
XLA Ops:
  0.0 1.6 copy-done
  1.6 0.5 squares.1.own_ref
  2.2 0.9 broadcast_in_dim.2.gain_ref
  3.1 0.3 collective-permute-done.got_ref
  3.5 4.7 %collective-permute-start.1 = (bf16[528,2048]{1,0:T(8,128)(2,1)S(1)}, bf16[528,2048]{1,0:T(8,128)(2,1)S(1)}, u32[]{:S(2)}, u32[]{:S(2)}) collective-permute-start(bf16[528,2048]{1,0:T(8,128)(2,1)S(1)} %stamp.1.refs_0_), channel_id=1, source_target_pairs={{1,8},{3,10},{5,13},{7,15},{8,0},{10,2},{12,5},{14,7},{17,24},{19,... | collective-permute-start | bytes 6488072 | tf_op jit(solution)/shard_map/ppermute | solution.py:81
  8.3 0.2 pack.1
  8.5 2.4 %collective-permute-start.2 = (bf16[256,1280]{1,0:T(8,128)(2,1)S(1)}, bf16[256,1280]{1,0:T(8,128)(2,1)S(1)}, u32[]{:S(2)}, u32[]{:S(2)}) collective-permute-start(bf16[256,1280]{1,0:T(8,128)(2,1)S(1)} %get-tuple-element.62.own_ref), channel_id=1, source_target_pairs={{0,16},{1,17},{2,18},{3,19},{4,20},{5,21},{6,22},{7,23},{8,24},{9,... | collective-permute-start | bytes 1966088 | tf_op jit(solution)/shard_map/ppermute | solution.py:81
  10.9 0.9 collective-permute-start.3
  11.8 1.2 collective-permute-start.4
  13.0 0.5 collective-permute-start.5
  13.6 32.3 %collective-permute-done.2.far_ref = bf16[256,1280]{1,0:T(8,128)(2,1)S(1)} collective-permute-done((bf16[256,1280]{1,0:T(8,128)(2,1)S(1)}, bf16[256,1280]{1,0:T(8,128)(2,1)S(1)}, u32[]{:S(2)}, u32[]{:S(2)}) %collective-permute-start.2) | collective-permute-done | bytes 655392 | tf_op jit(solution)/shard_map/ppermute | solution.py:81
  45.9 0.4 rest.1
  46.2 1.3 collective-permute-start.6
  47.5 0.8 collective-permute-start.7
  48.3 1.3 collective-permute-start.8
  49.6 4.4 %collective-permute-start.13 = (bf16[1280,1280]{1,0:T(8,128)(2,1)S(1)}, bf16[1280,1280]{1,0:T(8,128)(2,1)S(1)}, u32[]{:S(2)}, u32[]{:S(2)}) collective-permute-start(bf16[1280,1280]{1,0:T(8,128)(2,1)S(1)} %get-tuple-element.77.refs_0_.mine), channel_id=1, source_target_pairs={{0,1},{1,0},{2,3},{3,2},{4,5},{5,4},{6,7},{7,6},{8,9},{9,8},{10,11... | collective-permute-start | bytes 9830408 | tf_op jit(solution)/shard_map/ppermute | solution.py:81
  54.1 28.4 %collective-permute-done.9.refs_2_.refs_0_ = bf16[768,384]{1,0:T(8,128)(2,1)S(1)} collective-permute-done((bf16[768,384]{1,0:T(8,128)(2,1)S(1)}, bf16[768,384]{1,0:T(8,128)(2,1)S(1)}, u32[]{:S(2)}, u32[]{:S(2)}) %collective-permute-start.9) | collective-permute-done | bytes 589856 | tf_op jit(solution)/shard_map/ppermute | solution.py:81
  82.5 0.8 collective-permute-start.12
  83.3 1.0 fusion.2
  84.3 0.2 pad_maximum_fusion
  84.6 15.9 %collective-permute-start.11 = (bf16[768,384]{1,0:T(8,128)(2,1)S(1)}, bf16[768,384]{1,0:T(8,128)(2,1)S(1)}, u32[]{:S(2)}, u32[]{:S(2)}) collective-permute-start(bf16[768,384]{1,0:T(8,128)(2,1)S(1)} %collective-permute-done.9.refs_2_.refs_0_), channel_id=1, source_target_pairs={{0,1},{1,0},{2,3},{3,2},{4,5},{5,4},{6,7},{7,6},{8,9},{9,8},{10,11... | collective-permute-start | bytes 1769480 | tf_op jit(solution)/shard_map/ppermute | solution.py:81
  100.5 1.6 scale_rows.2.lhs.refs_0_
  102.1 2.8 %collective-permute-done.10.refs_3_.refs_1_ = bf16[768,256]{1,0:T(8,128)(2,1)S(1)} collective-permute-done((bf16[768,256]{1,0:T(8,128)(2,1)S(1)}, bf16[768,256]{1,0:T(8,128)(2,1)S(1)}, u32[]{:S(2)}, u32[]{:S(2)}) %collective-permute-start.10) | collective-permute-done | bytes 393248 | tf_op jit(solution)/shard_map/ppermute | solution.py:81
  104.9 1.3 collective-permute-start.14
  106.2 0.8 collective-permute-start.15
  107.0 1.5 collective-permute-start.16
  108.6 4.5 %collective-permute-start.19 = (bf16[768,256]{1,0:T(8,128)(2,1)S(1)}, bf16[768,256]{1,0:T(8,128)(2,1)S(1)}, u32[]{:S(2)}, u32[]{:S(2)}) collective-permute-start(bf16[768,256]{1,0:T(8,128)(2,1)S(1)} %collective-permute-done.10.refs_3_.refs_1_), channel_id=1, source_target_pairs={{0,1},{1,0},{2,3},{3,2},{4,5},{5,4},{6,7},{7,6},{8,9},{9,8},{10,11... | collective-permute-start | bytes 1179656 | tf_op jit(solution)/shard_map/ppermute | solution.py:81
  113.1 3.5 %early.1.refs_1_ = f32[512,1280]{1,0:T(8,128)S(1)} custom-call(bf16[512,4096]{1,0:T(8,128)(2,1)S(1)} %scale_rows.2.lhs.refs_0_, bf16[1280,1280]{1,0:T(8,128)(2,1)S(1)} %get-tuple-element.77.refs_0_.mine, bf16[1280,1280]{1,0:T(8,128)(2,1)S(1)} %collective-permute-done.13.refs_1_.other), custom_call_target="tpu_custom_call" | custom-call | bytes 5242880 | tf_op jit(solution)/shard_map/early/pallas_call | solution.py:404
  116.7 1.4 late.3
  118.1 0.4 collective-permute-start.21
  118.5 17.4 %collective-permute-done.17.refs_2_ = bf16[768,384]{1,0:T(8,128)(2,1)S(1)} collective-permute-done((bf16[768,384]{1,0:T(8,128)(2,1)S(1)}, bf16[768,384]{1,0:T(8,128)(2,1)S(1)}, u32[]{:S(2)}, u32[]{:S(2)}) %collective-permute-start.17) | collective-permute-done | bytes 589856 | tf_op jit(solution)/shard_map/ppermute | solution.py:81
  135.9 2.6 %collective-permute-start.18 = (bf16[768,256]{1,0:T(8,128)(2,1)S(1)}, bf16[768,256]{1,0:T(8,128)(2,1)S(1)}, u32[]{:S(2)}, u32[]{:S(2)}) collective-permute-start(bf16[768,256]{1,0:T(8,128)(2,1)S(1)} %get-tuple-element.86), channel_id=1, source_target_pairs={{0,16},{1,17},{2,18},{3,19},{4,20},{5,21},{6,22},{7,23},{8,24},{9,... | collective-permute-start | bytes 1179656 | tf_op jit(solution)/shard_map/ppermute | solution.py:81
  138.6 21.1 %collective-permute-start.20 = (bf16[768,384]{1,0:T(8,128)(2,1)S(1)}, bf16[768,384]{1,0:T(8,128)(2,1)S(1)}, u32[]{:S(2)}, u32[]{:S(2)}) collective-permute-start(bf16[768,384]{1,0:T(8,128)(2,1)S(1)} %collective-permute-done.17.refs_2_), channel_id=1, source_target_pairs={{0,1},{1,0},{2,3},{3,2},{4,5},{5,4},{6,7},{7,6},{8,9},{9,8},{10,11... | collective-permute-start | bytes 1769480 | tf_op jit(solution)/shard_map/ppermute | solution.py:81
  159.6 1.8 scale_rows.3.lhs
  161.6 1.0 late.5
  162.8 0.5 collective-permute-done.23.refs_3_.refs_7_
  163.3 0.6 late.4
  163.9 1.0 collective-permute-start.25
  165.0 6.6 %whole.1 = (f32[512,384]{1,0:T(8,128)S(1)}, f32[512,256]{1,0:T(8,128)S(1)}, f32[512,384]{1,0:T(8,128)S(1)}, f32[512,256]{1,0:T(8,128)S(1)}) custom-call(bf16[512,4096]{1,0:T(8,128)(2,1)S(1)} %scale_rows.3.lhs, bf16[1280,1280]{1,0:T(8,128)(2,1)S(1)} %get-tuple-element.77.refs_0_.mine, bf16[1280,1280]{1,0:T(8,128)(2,1)S(1)} %collective-permute-done.13.refs_1_.other, ...), custom_call_target="tpu_custom_call" | custom-call | bytes 5242880 | tf_op jit(solution)/shard_map/whole/pallas_call | solution.py:434
  171.8 2.7 %attend.3.refs_0_ = bf16[512,384]{1,0:T(8,128)(2,1)S(1)} custom-call(f32[512,384]{1,0:T(8,128)S(1)} %get-tuple-element.101.near_ref, f32[512,384]{1,0:T(8,128)S(1)} %convert_element_type.19.got_ref, f32[512,128]{1,0:T(8,128)S(1)} %get-tuple-element.103.cos_ref, f32[512,128]{1,0:T(8,128)S(1)} %get-tuple-element.104.sin_ref, ...), custom_call_target="tpu_custom_call" | custom-call | bytes 786432 | tf_op jit(solution)/shard_map/attend/pallas_call | solution.py:444
  174.5 2.5 %collective-permute-start.26 = (bf16[512,384]{1,0:T(8,128)(2,1)S(1)}, bf16[512,384]{1,0:T(8,128)(2,1)S(1)}, u32[]{:S(2)}, u32[]{:S(2)}) collective-permute-start(bf16[512,384]{1,0:T(8,128)(2,1)S(1)} %attend.3.refs_0_), channel_id=1, source_target_pairs={{1,4},{3,6},{4,1},{6,3},{9,12},{11,14},{12,9},{14,11},{17,20},{19,... | collective-permute-start | bytes 1179656 | tf_op jit(solution)/shard_map/ppermute | solution.py:81
  177.1 2.8 %attend.4.refs_1_ = bf16[512,384]{1,0:T(8,128)(2,1)S(1)} custom-call(f32[512,384]{1,0:T(8,128)S(1)} %get-tuple-element.109.near_ref, f32[512,384]{1,0:T(8,128)S(1)} %convert_element_type.21.got_ref, f32[512,128]{1,0:T(8,128)S(1)} %get-tuple-element.103.cos_ref, f32[512,128]{1,0:T(8,128)S(1)} %get-tuple-element.104.sin_ref, ...), custom_call_target="tpu_custom_call" | custom-call | bytes 786432 | tf_op jit(solution)/shard_map/attend/pallas_call | solution.py:444
  179.9 3.1 %collective-permute-start.27 = (bf16[512,384]{1,0:T(8,128)(2,1)S(1)}, bf16[512,384]{1,0:T(8,128)(2,1)S(1)}, u32[]{:S(2)}, u32[]{:S(2)}) collective-permute-start(bf16[512,384]{1,0:T(8,128)(2,1)S(1)} %attend.4.refs_1_), channel_id=1, source_target_pairs={{1,4},{3,6},{4,1},{6,3},{9,12},{11,14},{12,9},{14,11},{17,20},{19,... | collective-permute-start | bytes 1179656 | tf_op jit(solution)/shard_map/ppermute | solution.py:81
  183.0 1.9 attend.5.refs_2_
  184.9 2.5 %collective-permute-start.28 = (bf16[512,256]{1,0:T(8,128)(2,1)S(1)}, bf16[512,256]{1,0:T(8,128)(2,1)S(1)}, u32[]{:S(2)}, u32[]{:S(2)}) collective-permute-start(bf16[512,256]{1,0:T(8,128)(2,1)S(1)} %attend.5.refs_2_), channel_id=1, source_target_pairs={{1,4},{3,6},{4,1},{6,3},{9,12},{11,14},{12,9},{14,11},{17,20},{19,... | collective-permute-start | bytes 786440 | tf_op jit(solution)/shard_map/ppermute | solution.py:81
  187.4 1.6 collective-permute-done.27.refs_4_
  189.0 3.6 %collective-permute-done.28.refs_5_ = bf16[512,256]{1,0:T(8,128)(2,1)S(1)} collective-permute-done((bf16[512,256]{1,0:T(8,128)(2,1)S(1)}, bf16[512,256]{1,0:T(8,128)(2,1)S(1)}, u32[]{:S(2)}, u32[]{:S(2)}) %collective-permute-start.28) | collective-permute-done | bytes 262176 | tf_op jit(solution)/shard_map/ppermute | solution.py:81
  192.6 1.1 place.1
  (46 shorter events, 1.1 us)
Async XLA Ops:
  0.0 1.6 copy-start
  1.6 1.8 copy-start.1
  2.1 6.2 %copy-start.2 = (bf16[256,4096]{1,0:T(8,128)(2,1)S(1)}, bf16[256,4096]{1,0:T(8,128)(2,1)}, u32[]{:S(2)}) copy-start(bf16[256,4096]{1,0:T(8,128)(2,1)} %q_ref.1) | copy-start | bytes 6291460
  2.1 6.2 %copy-start.3 = (bf16[256,512]{1,0:T(8,128)(2,1)S(1)}, bf16[256,512]{1,0:T(8,128)(2,1)}, u32[]{:S(2)}) copy-start(bf16[256,512]{1,0:T(8,128)(2,1)} %k_ref.1) | copy-start | bytes 786436
  2.1 6.2 %copy-start.4 = (bf16[256,512]{1,0:T(8,128)(2,1)S(1)}, bf16[256,512]{1,0:T(8,128)(2,1)}, u32[]{:S(2)}) copy-start(bf16[256,512]{1,0:T(8,128)(2,1)} %v_ref.1) | copy-start | bytes 786436
  2.1 1.2 collective-permute-start
  3.5 42.7 %collective-permute-start.1 = (bf16[528,2048]{1,0:T(8,128)(2,1)S(1)}, bf16[528,2048]{1,0:T(8,128)(2,1)S(1)}, u32[]{:S(2)}, u32[]{:S(2)}) collective-permute-start(bf16[528,2048]{1,0:T(8,128)(2,1)S(1)} %stamp.1.refs_0_), channel_id=1, source_target_pairs={{1,8},{3,10},{5,13},{7,15},{8,0},{10,2},{12,5},{14,7},{17,24},{19,... | collective-permute-start | bytes 6488072 | tf_op jit(solution)/shard_map/ppermute | solution.py:81
  8.5 37.3 %collective-permute-start.2 = (bf16[256,1280]{1,0:T(8,128)(2,1)S(1)}, bf16[256,1280]{1,0:T(8,128)(2,1)S(1)}, u32[]{:S(2)}, u32[]{:S(2)}) collective-permute-start(bf16[256,1280]{1,0:T(8,128)(2,1)S(1)} %get-tuple-element.62.own_ref), channel_id=1, source_target_pairs={{0,16},{1,17},{2,18},{3,19},{4,20},{5,21},{6,22},{7,23},{8,24},{9,... | collective-permute-start | bytes 1966088 | tf_op jit(solution)/shard_map/ppermute | solution.py:81
  10.9 34.9 %collective-permute-start.3 = (bf16[256,1280]{1,0:T(8,128)(2,1)S(1)}, bf16[256,1280]{1,0:T(8,128)(2,1)S(1)}, u32[]{:S(2)}, u32[]{:S(2)}) collective-permute-start(bf16[256,1280]{1,0:T(8,128)(2,1)S(1)} %get-tuple-element.59), channel_id=1, source_target_pairs={{0,4},{1,5},{2,6},{3,7},{4,0},{5,1},{6,2},{7,3},{8,12},{9,13},{10,... | collective-permute-start | bytes 1966088 | tf_op jit(solution)/shard_map/ppermute | solution.py:81
  11.8 34.1 %collective-permute-start.4 = (bf16[256,1280]{1,0:T(8,128)(2,1)S(1)}, bf16[256,1280]{1,0:T(8,128)(2,1)S(1)}, u32[]{:S(2)}, u32[]{:S(2)}) collective-permute-start(bf16[256,1280]{1,0:T(8,128)(2,1)S(1)} %get-tuple-element.60), channel_id=1, source_target_pairs={{0,2},{1,3},{2,0},{3,1},{4,6},{5,7},{6,4},{7,5},{8,10},{9,11},{10,... | collective-permute-start | bytes 1966088 | tf_op jit(solution)/shard_map/ppermute | solution.py:81
  13.0 32.8 %collective-permute-start.5 = (bf16[256,1280]{1,0:T(8,128)(2,1)S(1)}, bf16[256,1280]{1,0:T(8,128)(2,1)S(1)}, u32[]{:S(2)}, u32[]{:S(2)}) collective-permute-start(bf16[256,1280]{1,0:T(8,128)(2,1)S(1)} %get-tuple-element.61), channel_id=1, source_target_pairs={{0,6},{1,7},{2,4},{3,5},{4,2},{5,3},{6,0},{7,1},{8,14},{9,15},{10,... | collective-permute-start | bytes 1966088 | tf_op jit(solution)/shard_map/ppermute | solution.py:81
  46.2 38.3 %collective-permute-start.6 = (bf16[528,2048]{1,0:T(8,128)(2,1)S(1)}, bf16[528,2048]{1,0:T(8,128)(2,1)S(1)}, u32[]{:S(2)}, u32[]{:S(2)}) collective-permute-start(bf16[528,2048]{1,0:T(8,128)(2,1)S(1)} %collective-permute-done.1.here), channel_id=1, source_target_pairs={{0,4},{2,6},{5,1},{7,3},{8,12},{10,14},{13,9},{15,11},{16,20},{18,... | collective-permute-start | bytes 6488072 | tf_op jit(solution)/shard_map/ppermute | solution.py:81
  47.5 37.1 %collective-permute-start.7 = (bf16[528,2048]{1,0:T(8,128)(2,1)S(1)}, bf16[528,2048]{1,0:T(8,128)(2,1)S(1)}, u32[]{:S(2)}, u32[]{:S(2)}) collective-permute-start(bf16[528,2048]{1,0:T(8,128)(2,1)S(1)} %collective-permute-done.1.here), channel_id=1, source_target_pairs={{0,2},{2,0},{5,7},{7,5},{8,10},{10,8},{13,15},{15,13},{16,18},{18,... | collective-permute-start | bytes 6488072 | tf_op jit(solution)/shard_map/ppermute | solution.py:81
  48.3 52.2 %collective-permute-start.8 = (bf16[528,2048]{1,0:T(8,128)(2,1)S(1)}, bf16[528,2048]{1,0:T(8,128)(2,1)S(1)}, u32[]{:S(2)}, u32[]{:S(2)}) collective-permute-start(bf16[528,2048]{1,0:T(8,128)(2,1)S(1)} %collective-permute-done.1.here), channel_id=1, source_target_pairs={{0,6},{2,4},{5,3},{7,1},{8,14},{10,12},{13,11},{15,9},{16,22},{18,... | collective-permute-start | bytes 6488072 | tf_op jit(solution)/shard_map/ppermute | solution.py:81
  49.6 55.3 %collective-permute-start.13 = (bf16[1280,1280]{1,0:T(8,128)(2,1)S(1)}, bf16[1280,1280]{1,0:T(8,128)(2,1)S(1)}, u32[]{:S(2)}, u32[]{:S(2)}) collective-permute-start(bf16[1280,1280]{1,0:T(8,128)(2,1)S(1)} %get-tuple-element.77.refs_0_.mine), channel_id=1, source_target_pairs={{0,1},{1,0},{2,3},{3,2},{4,5},{5,4},{6,7},{7,6},{8,9},{9,8},{10,11... | collective-permute-start | bytes 9830408 | tf_op jit(solution)/shard_map/ppermute | solution.py:81
  54.1 28.4 %collective-permute-start.9 = (bf16[768,384]{1,0:T(8,128)(2,1)S(1)}, bf16[768,384]{1,0:T(8,128)(2,1)S(1)}, u32[]{:S(2)}, u32[]{:S(2)}) collective-permute-start(bf16[768,384]{1,0:T(8,128)(2,1)S(1)} %get-tuple-element.74), channel_id=1, source_target_pairs={{0,16},{1,17},{2,18},{3,19},{4,20},{5,21},{6,22},{7,23},{8,24},{9,... | collective-permute-start | bytes 1769480 | tf_op jit(solution)/shard_map/ppermute | solution.py:81
  82.5 19.6 %collective-permute-start.12 = (bf16[528,2048]{1,0:T(8,128)(2,1)S(1)}, bf16[528,2048]{1,0:T(8,128)(2,1)S(1)}, u32[]{:S(2)}, u32[]{:S(2)}) collective-permute-start(bf16[528,2048]{1,0:T(8,128)(2,1)S(1)} %stamp.1.refs_0_), channel_id=1, source_target_pairs={{4,5},{6,7},{9,8},{11,10},{20,21},{22,23},{25,24},{27,26}} | collective-permute-start | bytes 6488072 | tf_op jit(solution)/shard_map/ppermute | solution.py:81
  84.5 20.4 %collective-permute-start.10 = (bf16[768,256]{1,0:T(8,128)(2,1)S(1)}, bf16[768,256]{1,0:T(8,128)(2,1)S(1)}, u32[]{:S(2)}, u32[]{:S(2)}) collective-permute-start(bf16[768,256]{1,0:T(8,128)(2,1)S(1)} %get-tuple-element.76), channel_id=1, source_target_pairs={{0,16},{1,17},{2,18},{3,19},{4,20},{5,21},{6,22},{7,23},{8,24},{9,... | collective-permute-start | bytes 1179656 | tf_op jit(solution)/shard_map/ppermute | solution.py:81
  84.6 20.3 %collective-permute-start.11 = (bf16[768,384]{1,0:T(8,128)(2,1)S(1)}, bf16[768,384]{1,0:T(8,128)(2,1)S(1)}, u32[]{:S(2)}, u32[]{:S(2)}) collective-permute-start(bf16[768,384]{1,0:T(8,128)(2,1)S(1)} %collective-permute-done.9.refs_2_.refs_0_), channel_id=1, source_target_pairs={{0,1},{1,0},{2,3},{3,2},{4,5},{5,4},{6,7},{7,6},{8,9},{9,8},{10,11... | collective-permute-start | bytes 1769480 | tf_op jit(solution)/shard_map/ppermute | solution.py:81
  104.9 31.0 %collective-permute-start.14 = (bf16[528,2048]{1,0:T(8,128)(2,1)S(1)}, bf16[528,2048]{1,0:T(8,128)(2,1)S(1)}, u32[]{:S(2)}, u32[]{:S(2)}) collective-permute-start(bf16[528,2048]{1,0:T(8,128)(2,1)S(1)} %stamp.1.refs_0_), channel_id=1, source_target_pairs={{0,4},{2,6},{4,1},{6,3},{9,12},{11,14},{13,9},{15,11},{16,20},{18,... | collective-permute-start | bytes 6488072 | tf_op jit(solution)/shard_map/ppermute | solution.py:81
  106.2 32.4 %collective-permute-start.15 = (bf16[528,2048]{1,0:T(8,128)(2,1)S(1)}, bf16[528,2048]{1,0:T(8,128)(2,1)S(1)}, u32[]{:S(2)}, u32[]{:S(2)}) collective-permute-start(bf16[528,2048]{1,0:T(8,128)(2,1)S(1)} %stamp.1.refs_0_), channel_id=1, source_target_pairs={{0,2},{2,0},{4,7},{6,5},{9,10},{11,8},{13,15},{15,13},{16,18},{18,... | collective-permute-start | bytes 6488072 | tf_op jit(solution)/shard_map/ppermute | solution.py:81
  107.0 52.6 %collective-permute-start.16 = (bf16[528,2048]{1,0:T(8,128)(2,1)S(1)}, bf16[528,2048]{1,0:T(8,128)(2,1)S(1)}, u32[]{:S(2)}, u32[]{:S(2)}) collective-permute-start(bf16[528,2048]{1,0:T(8,128)(2,1)S(1)} %stamp.1.refs_0_), channel_id=1, source_target_pairs={{0,6},{2,4},{4,3},{6,1},{9,14},{11,12},{13,11},{15,9},{16,22},{18,... | collective-permute-start | bytes 6488072 | tf_op jit(solution)/shard_map/ppermute | solution.py:81
  108.5 27.4 %collective-permute-start.17 = (bf16[768,384]{1,0:T(8,128)(2,1)S(1)}, bf16[768,384]{1,0:T(8,128)(2,1)S(1)}, u32[]{:S(2)}, u32[]{:S(2)}) collective-permute-start(bf16[768,384]{1,0:T(8,128)(2,1)S(1)} %get-tuple-element.84), channel_id=1, source_target_pairs={{0,16},{1,17},{2,18},{3,19},{4,20},{5,21},{6,22},{7,23},{8,24},{9,... | collective-permute-start | bytes 1769480 | tf_op jit(solution)/shard_map/ppermute | solution.py:81
  108.6 8.1 %collective-permute-start.19 = (bf16[768,256]{1,0:T(8,128)(2,1)S(1)}, bf16[768,256]{1,0:T(8,128)(2,1)S(1)}, u32[]{:S(2)}, u32[]{:S(2)}) collective-permute-start(bf16[768,256]{1,0:T(8,128)(2,1)S(1)} %collective-permute-done.10.refs_3_.refs_1_), channel_id=1, source_target_pairs={{0,1},{1,0},{2,3},{3,2},{4,5},{5,4},{6,7},{7,6},{8,9},{9,8},{10,11... | collective-permute-start | bytes 1179656 | tf_op jit(solution)/shard_map/ppermute | solution.py:81
  118.1 43.4 %collective-permute-start.21 = (f32[512,256]{1,0:T(8,128)S(1)}, f32[512,256]{1,0:T(8,128)S(1)}, u32[]{:S(2)}, u32[]{:S(2)}) collective-permute-start(f32[512,256]{1,0:T(8,128)S(1)} %get-tuple-element.90), channel_id=1, source_target_pairs={{0,8},{1,9},{2,10},{3,11},{4,12},{5,13},{6,14},{7,15},{8,0},{9,1},... | collective-permute-start | bytes 1572872 | tf_op jit(solution)/shard_map/ppermute | solution.py:81
  135.9 25.6 %collective-permute-start.22 = (f16[512,384]{1,0:T(8,128)(2,1)S(1)}, f16[512,384]{1,0:T(8,128)(2,1)S(1)}, u32[]{:S(2)}, u32[]{:S(2)}) collective-permute-start(f16[512,384]{1,0:T(8,128)(2,1)S(1)} %convert_element_type.18), channel_id=1, source_target_pairs={{0,8},{1,9},{2,10},{3,11},{4,12},{5,13},{6,14},{7,15},{8,0},{9,1},... | collective-permute-start | bytes 1179656 | tf_op jit(solution)/shard_map/ppermute | solution.py:81
  135.9 25.6 %collective-permute-start.18 = (bf16[768,256]{1,0:T(8,128)(2,1)S(1)}, bf16[768,256]{1,0:T(8,128)(2,1)S(1)}, u32[]{:S(2)}, u32[]{:S(2)}) collective-permute-start(bf16[768,256]{1,0:T(8,128)(2,1)S(1)} %get-tuple-element.86), channel_id=1, source_target_pairs={{0,16},{1,17},{2,18},{3,19},{4,20},{5,21},{6,22},{7,23},{8,24},{9,... | collective-permute-start | bytes 1179656 | tf_op jit(solution)/shard_map/ppermute | solution.py:81
  138.6 22.9 %collective-permute-start.20 = (bf16[768,384]{1,0:T(8,128)(2,1)S(1)}, bf16[768,384]{1,0:T(8,128)(2,1)S(1)}, u32[]{:S(2)}, u32[]{:S(2)}) collective-permute-start(bf16[768,384]{1,0:T(8,128)(2,1)S(1)} %collective-permute-done.17.refs_2_), channel_id=1, source_target_pairs={{0,1},{1,0},{2,3},{3,2},{4,5},{5,4},{6,7},{7,6},{8,9},{9,8},{10,11... | collective-permute-start | bytes 1769480 | tf_op jit(solution)/shard_map/ppermute | solution.py:81
  161.5 1.8 collective-permute-start.23
  162.7 14.3 %collective-permute-start.24 = (f16[512,384]{1,0:T(8,128)(2,1)S(1)}, f16[512,384]{1,0:T(8,128)(2,1)S(1)}, u32[]{:S(2)}, u32[]{:S(2)}) collective-permute-start(f16[512,384]{1,0:T(8,128)(2,1)S(1)} %convert_element_type.20), channel_id=1, source_target_pairs={{0,8},{1,9},{2,10},{3,11},{4,12},{5,13},{6,14},{7,15},{8,0},{9,1},... | collective-permute-start | bytes 1179656 | tf_op jit(solution)/shard_map/ppermute | solution.py:81
  163.9 19.0 %collective-permute-start.25 = (f16[512,256]{1,0:T(8,128)(2,1)S(1)}, f16[512,256]{1,0:T(8,128)(2,1)S(1)}, u32[]{:S(2)}, u32[]{:S(2)}) collective-permute-start(f16[512,256]{1,0:T(8,128)(2,1)S(1)} %convert_element_type.22), channel_id=1, source_target_pairs={{0,8},{1,9},{2,10},{3,11},{4,12},{5,13},{6,14},{7,15},{8,0},{9,1},... | collective-permute-start | bytes 786440 | tf_op jit(solution)/shard_map/ppermute | solution.py:81
  174.5 12.9 %collective-permute-start.26 = (bf16[512,384]{1,0:T(8,128)(2,1)S(1)}, bf16[512,384]{1,0:T(8,128)(2,1)S(1)}, u32[]{:S(2)}, u32[]{:S(2)}) collective-permute-start(bf16[512,384]{1,0:T(8,128)(2,1)S(1)} %attend.3.refs_0_), channel_id=1, source_target_pairs={{1,4},{3,6},{4,1},{6,3},{9,12},{11,14},{12,9},{14,11},{17,20},{19,... | collective-permute-start | bytes 1179656 | tf_op jit(solution)/shard_map/ppermute | solution.py:81
  179.9 9.1 %collective-permute-start.27 = (bf16[512,384]{1,0:T(8,128)(2,1)S(1)}, bf16[512,384]{1,0:T(8,128)(2,1)S(1)}, u32[]{:S(2)}, u32[]{:S(2)}) collective-permute-start(bf16[512,384]{1,0:T(8,128)(2,1)S(1)} %attend.4.refs_1_), channel_id=1, source_target_pairs={{1,4},{3,6},{4,1},{6,3},{9,12},{11,14},{12,9},{14,11},{17,20},{19,... | collective-permute-start | bytes 1179656 | tf_op jit(solution)/shard_map/ppermute | solution.py:81
  184.9 7.7 %collective-permute-start.28 = (bf16[512,256]{1,0:T(8,128)(2,1)S(1)}, bf16[512,256]{1,0:T(8,128)(2,1)S(1)}, u32[]{:S(2)}, u32[]{:S(2)}) collective-permute-start(bf16[512,256]{1,0:T(8,128)(2,1)S(1)} %attend.5.refs_2_), channel_id=1, source_target_pairs={{1,4},{3,6},{4,1},{6,3},{9,12},{11,14},{12,9},{14,11},{17,20},{19,... | collective-permute-start | bytes 786440 | tf_op jit(solution)/shard_map/ppermute | solution.py:81

commit v5 on v4

--- a/solution.py
+++ b/solution.py
@@ -113,7 +113,7 @@
 )
 VMEM = {
     "pack": 8, "squares": 6, "stamp": 6, "rest": 10, "scale_rows": 16, "early": 15,
-    "late": 14, "whole": 18, "keys": 4, "attend": 6, "place": 5,
+    "late": 14, "whole": 20, "keys": 4, "attend": 10, "place": 5,
 }
 
 
@@ -250,16 +250,16 @@
     count = len(CHUNKS)
     rest, rest_core, outs = refs[:count], refs[count : 2 * count], list(refs[2 * count :])
     depth = mine.shape[0]
+    near = dot(lhs[:, :depth], mine[...]) + dot(lhs[:, depth : 2 * depth], other[...])
     for chunks, places in PARTS:
         parts = [outs.pop(0) for _ in range(1 + max(i for i, _ in places))]
         places = iter(places)
         for j in chunks:
             lo, hi = CHUNKS[j]
-            span = slice(lo * HD, hi * HD)
-            got, at = 0.0, 0
-            for weight in (mine[:, span], other[:, span], rest[j][...], rest_core[j][...]):
-                got = got + dot(lhs[:, at : at + weight.shape[0]], weight)
-                at += weight.shape[0]
+            got, at = near[:, lo * HD : hi * HD], 2 * depth
+            for ref in (rest[j], rest_core[j]):
+                got = got + dot(lhs[:, at : at + ref.shape[0]], ref[...])
+                at += ref.shape[0]
             for h in range(hi - lo):
                 i, to = next(places)
                 parts[i][:, to * HD : (to + 1) * HD] = got[:, h * HD : (h + 1) * HD]
@@ -296,35 +296,28 @@
 
 
 def attend_kernel(near_ref, got_ref, cos_ref, sin_ref, k_ref, v_ref, out_ref):
-    rows = near_ref.shape[0]
+    rows, width = out_ref.shape
+    half = rows // 2
     cosine, sine = cos_ref[...], sin_ref[...]
-    half = rows // 2
-    scale = 1.0 / (HD**0.5)
-    above = lax.broadcasted_iota(jnp.int32, (half, half), 1) > lax.broadcasted_iota(
-        jnp.int32, (half, half), 0
-    )
-    for h in range(out_ref.shape[1] // HD):
-        span = slice(h * HD, (h + 1) * HD)
-        q = turn(near_ref[:, span] + got_ref[:, span], cosine, sine)
-        for block in range(2):
-            mine = q[block * half : (block + 1) * half]
-            parts = []
-            for other in range(block + 1):
-                keys = k_ref[other * half : (other + 1) * half, :]
-                s = lax.dot_general(
-                    mine, keys, (((1,), (1,)), ((), ())), preferred_element_type=jnp.float32
-                )
-                s = s * scale
-                parts.append(jnp.where(above, -1e30, s) if other == block else s)
-            s = parts[0] if block == 0 else jnp.concatenate(parts, axis=1)
-            expo = jnp.exp(s - jnp.max(s, axis=1, keepdims=True))
-            probs = (expo / jnp.sum(expo, axis=1, keepdims=True)).astype(jnp.bfloat16)
-            got = jnp.dot(
-                probs, v_ref[: (block + 1) * half, :], preferred_element_type=jnp.float32
-            )
-            out_ref[block * half : (block + 1) * half, span] = got.astype(
-                jnp.bfloat16
-            )
+    spans = [slice(h, h + HD) for h in range(0, width, HD)]
+    queries = [turn(near_ref[:, span] + got_ref[:, span], cosine, sine) for span in spans]
+    scale = 1.4426950408889634 / HD**0.5
+    for lo, hi in ((0, half), (half, rows)):
+        mine = jnp.concatenate([q[lo:hi] for q in queries], axis=0)
+        scores = lax.dot_general(
+            mine, k_ref[:hi, :], (((1,), (1,)), ((), ())), preferred_element_type=jnp.float32
+        )
+        row = lax.broadcasted_iota(jnp.int32, (half, hi), 0) + lo
+        later = lax.broadcasted_iota(jnp.int32, (half, hi), 1) > row
+        probs = []
+        for h in range(len(spans)):
+            s = jnp.where(later, -1e30, scores[h * half : (h + 1) * half])
+            expo = jnp.exp2((s - jnp.max(s, axis=1, keepdims=True)) * scale)
+            inverse = 1.0 / jnp.sum(expo, axis=1, keepdims=True)
+            probs.append((expo * inverse).astype(jnp.bfloat16))
+        got = dot(jnp.concatenate(probs, axis=0), v_ref[:hi, :]).astype(jnp.bfloat16)
+        for h, span in enumerate(spans):
+            out_ref[lo:hi, span] = got[h * half : (h + 1) * half]
 
 
 def split_plan(hidden_in, norm_gain, q_weight, k_weight, v_weight):

time: 194 us -> 191 us (0.985)
  Pallas kernels: 26.5 us -> 23.9 us
  transfers between devices with their start and end apart: 29 -> 29, of which waited for: 8 -> 8; matrix products, arithmetic and copies ran while one was open for 1% -> 1% of each run, Pallas kernels for 13% -> 12%
where the time goes in v5:
time: 191 us
  waiting for transfers between devices  86.9 us (45%)
  starting transfers between devices  75.9 us (40%)
  Pallas kernels  23.9 us (13%)
  local copies, waits for them, and re-layouts  2.46 us (1%)
    ppermute x29, waiting for transfers between devices, move(): return lax.ppermute(value, AXES, pairs)  86.9 us
    ppermute x29, starting transfers between devices, move(): return lax.ppermute(value, AXES, pairs)  75.9 us
    pallas_call x1, Pallas kernels, split_plan(): call(whole_kernel, [jax.ShapeDtypeStruct((rows, n), jnp.float32) for ns i...  6 us
    pallas_call x3, Pallas kernels, split_plan(): call(attend_kernel, jax.ShapeDtypeStruct(part.shape, bf16), name='attend')  5.49 us
  transfers between devices with their start and end apart: 29, of which 8 were waited for; matrix products, arithmetic and copies ran while one was open for 1% of the time, Pallas kernels for 12%

profile of v5, /device:TPU:1, one launch (start us, length us, event | category | flops | bytes accessed | tf_op | source)
XLA Modules:
  0.0 191.1 jit_solution(5549042420486427748)
XLA Ops:
  0.0 1.6 copy-done
  1.6 0.5 squares.1.own_ref
  2.2 0.9 broadcast_in_dim.2.gain_ref
  3.1 0.3 collective-permute-done.got_ref
  3.5 4.7 %collective-permute-start.1 = (bf16[528,2048]{1,0:T(8,128)(2,1)S(1)}, bf16[528,2048]{1,0:T(8,128)(2,1)S(1)}, u32[]{:S(2)}, u32[]{:S(2)}) collective-permute-start(bf16[528,2048]{1,0:T(8,128)(2,1)S(1)} %stamp.1.refs_0_), channel_id=1, source_target_pairs={{1,8},{3,10},{5,13},{7,15},{8,0},{10,2},{12,5},{14,7},{17,24},{19,... | collective-permute-start | bytes 6488072 | tf_op jit(solution)/shard_map/ppermute | solution.py:81
  8.3 0.2 pack.1
  8.5 2.4 %collective-permute-start.2 = (bf16[256,1280]{1,0:T(8,128)(2,1)S(1)}, bf16[256,1280]{1,0:T(8,128)(2,1)S(1)}, u32[]{:S(2)}, u32[]{:S(2)}) collective-permute-start(bf16[256,1280]{1,0:T(8,128)(2,1)S(1)} %get-tuple-element.62.own_ref), channel_id=1, source_target_pairs={{0,16},{1,17},{2,18},{3,19},{4,20},{5,21},{6,22},{7,23},{8,24},{9,... | collective-permute-start | bytes 1966088 | tf_op jit(solution)/shard_map/ppermute | solution.py:81
  10.9 0.9 collective-permute-start.3
  11.8 1.2 collective-permute-start.4
  13.0 0.5 collective-permute-start.5
  13.6 32.3 %collective-permute-done.2.far_ref = bf16[256,1280]{1,0:T(8,128)(2,1)S(1)} collective-permute-done((bf16[256,1280]{1,0:T(8,128)(2,1)S(1)}, bf16[256,1280]{1,0:T(8,128)(2,1)S(1)}, u32[]{:S(2)}, u32[]{:S(2)}) %collective-permute-start.2) | collective-permute-done | bytes 655392 | tf_op jit(solution)/shard_map/ppermute | solution.py:81
  45.9 0.4 rest.1
  46.2 1.3 collective-permute-start.6
  47.5 0.8 collective-permute-start.7
  48.3 1.3 collective-permute-start.8
  49.6 4.4 %collective-permute-start.13 = (bf16[1280,1280]{1,0:T(8,128)(2,1)S(1)}, bf16[1280,1280]{1,0:T(8,128)(2,1)S(1)}, u32[]{:S(2)}, u32[]{:S(2)}) collective-permute-start(bf16[1280,1280]{1,0:T(8,128)(2,1)S(1)} %get-tuple-element.77.refs_0_.mine), channel_id=1, source_target_pairs={{0,1},{1,0},{2,3},{3,2},{4,5},{5,4},{6,7},{7,6},{8,9},{9,8},{10,11... | collective-permute-start | bytes 9830408 | tf_op jit(solution)/shard_map/ppermute | solution.py:81
  54.1 28.4 %collective-permute-done.9.refs_2_.refs_0_ = bf16[768,384]{1,0:T(8,128)(2,1)S(1)} collective-permute-done((bf16[768,384]{1,0:T(8,128)(2,1)S(1)}, bf16[768,384]{1,0:T(8,128)(2,1)S(1)}, u32[]{:S(2)}, u32[]{:S(2)}) %collective-permute-start.9) | collective-permute-done | bytes 589856 | tf_op jit(solution)/shard_map/ppermute | solution.py:81
  82.5 0.8 collective-permute-start.12
  83.3 1.0 fusion.2
  84.3 0.2 pad_maximum_fusion
  84.6 15.9 %collective-permute-start.11 = (bf16[768,384]{1,0:T(8,128)(2,1)S(1)}, bf16[768,384]{1,0:T(8,128)(2,1)S(1)}, u32[]{:S(2)}, u32[]{:S(2)}) collective-permute-start(bf16[768,384]{1,0:T(8,128)(2,1)S(1)} %collective-permute-done.9.refs_2_.refs_0_), channel_id=1, source_target_pairs={{0,1},{1,0},{2,3},{3,2},{4,5},{5,4},{6,7},{7,6},{8,9},{9,8},{10,11... | collective-permute-start | bytes 1769480 | tf_op jit(solution)/shard_map/ppermute | solution.py:81
  100.5 1.6 scale_rows.2.lhs.refs_0_
  102.1 2.8 %collective-permute-done.10.refs_3_.refs_1_ = bf16[768,256]{1,0:T(8,128)(2,1)S(1)} collective-permute-done((bf16[768,256]{1,0:T(8,128)(2,1)S(1)}, bf16[768,256]{1,0:T(8,128)(2,1)S(1)}, u32[]{:S(2)}, u32[]{:S(2)}) %collective-permute-start.10) | collective-permute-done | bytes 393248 | tf_op jit(solution)/shard_map/ppermute | solution.py:81
  104.9 1.3 collective-permute-start.14
  106.2 0.8 collective-permute-start.15
  107.0 1.5 collective-permute-start.16
  108.6 4.5 %collective-permute-start.19 = (bf16[768,256]{1,0:T(8,128)(2,1)S(1)}, bf16[768,256]{1,0:T(8,128)(2,1)S(1)}, u32[]{:S(2)}, u32[]{:S(2)}) collective-permute-start(bf16[768,256]{1,0:T(8,128)(2,1)S(1)} %collective-permute-done.10.refs_3_.refs_1_), channel_id=1, source_target_pairs={{0,1},{1,0},{2,3},{3,2},{4,5},{5,4},{6,7},{7,6},{8,9},{9,8},{10,11... | collective-permute-start | bytes 1179656 | tf_op jit(solution)/shard_map/ppermute | solution.py:81
  113.1 3.5 %early.1.refs_1_ = f32[512,1280]{1,0:T(8,128)S(1)} custom-call(bf16[512,4096]{1,0:T(8,128)(2,1)S(1)} %scale_rows.2.lhs.refs_0_, bf16[1280,1280]{1,0:T(8,128)(2,1)S(1)} %get-tuple-element.77.refs_0_.mine, bf16[1280,1280]{1,0:T(8,128)(2,1)S(1)} %collective-permute-done.13.refs_1_.other), custom_call_target="tpu_custom_call" | custom-call | bytes 5242880 | tf_op jit(solution)/shard_map/early/pallas_call | solution.py:397
  116.7 1.4 late.3
  118.1 0.4 collective-permute-start.21
  118.5 17.4 %collective-permute-done.17.refs_2_ = bf16[768,384]{1,0:T(8,128)(2,1)S(1)} collective-permute-done((bf16[768,384]{1,0:T(8,128)(2,1)S(1)}, bf16[768,384]{1,0:T(8,128)(2,1)S(1)}, u32[]{:S(2)}, u32[]{:S(2)}) %collective-permute-start.17) | collective-permute-done | bytes 589856 | tf_op jit(solution)/shard_map/ppermute | solution.py:81
  135.9 2.6 %collective-permute-start.18 = (bf16[768,256]{1,0:T(8,128)(2,1)S(1)}, bf16[768,256]{1,0:T(8,128)(2,1)S(1)}, u32[]{:S(2)}, u32[]{:S(2)}) collective-permute-start(bf16[768,256]{1,0:T(8,128)(2,1)S(1)} %get-tuple-element.86), channel_id=1, source_target_pairs={{0,16},{1,17},{2,18},{3,19},{4,20},{5,21},{6,22},{7,23},{8,24},{9,... | collective-permute-start | bytes 1179656 | tf_op jit(solution)/shard_map/ppermute | solution.py:81
  138.6 21.1 %collective-permute-start.20 = (bf16[768,384]{1,0:T(8,128)(2,1)S(1)}, bf16[768,384]{1,0:T(8,128)(2,1)S(1)}, u32[]{:S(2)}, u32[]{:S(2)}) collective-permute-start(bf16[768,384]{1,0:T(8,128)(2,1)S(1)} %collective-permute-done.17.refs_2_), channel_id=1, source_target_pairs={{0,1},{1,0},{2,3},{3,2},{4,5},{5,4},{6,7},{7,6},{8,9},{9,8},{10,11... | collective-permute-start | bytes 1769480 | tf_op jit(solution)/shard_map/ppermute | solution.py:81
  159.6 1.8 scale_rows.3.lhs
  161.6 1.0 late.5
  162.8 0.5 collective-permute-done.23.refs_3_.refs_7_
  163.3 0.6 late.4
  163.9 1.0 collective-permute-start.25
  165.0 6.0 %whole.1 = (f32[512,384]{1,0:T(8,128)S(1)}, f32[512,256]{1,0:T(8,128)S(1)}, f32[512,384]{1,0:T(8,128)S(1)}, f32[512,256]{1,0:T(8,128)S(1)}) custom-call(bf16[512,4096]{1,0:T(8,128)(2,1)S(1)} %scale_rows.3.lhs, bf16[1280,1280]{1,0:T(8,128)(2,1)S(1)} %get-tuple-element.77.refs_0_.mine, bf16[1280,1280]{1,0:T(8,128)(2,1)S(1)} %collective-permute-done.13.refs_1_.other, ...), custom_call_target="tpu_custom_call" | custom-call | bytes 5242880 | tf_op jit(solution)/shard_map/whole/pallas_call | solution.py:427
  171.1 2.1 %attend.3.refs_0_ = bf16[512,384]{1,0:T(8,128)(2,1)S(1)} custom-call(f32[512,384]{1,0:T(8,128)S(1)} %get-tuple-element.101.near_ref, f32[512,384]{1,0:T(8,128)S(1)} %convert_element_type.19.got_ref, f32[512,128]{1,0:T(8,128)S(1)} %get-tuple-element.103.cos_ref, f32[512,128]{1,0:T(8,128)S(1)} %get-tuple-element.104.sin_ref, ...), custom_call_target="tpu_custom_call" | custom-call | bytes 786432 | tf_op jit(solution)/shard_map/attend/pallas_call | solution.py:437
  173.2 2.5 %collective-permute-start.26 = (bf16[512,384]{1,0:T(8,128)(2,1)S(1)}, bf16[512,384]{1,0:T(8,128)(2,1)S(1)}, u32[]{:S(2)}, u32[]{:S(2)}) collective-permute-start(bf16[512,384]{1,0:T(8,128)(2,1)S(1)} %attend.3.refs_0_), channel_id=1, source_target_pairs={{1,4},{3,6},{4,1},{6,3},{9,12},{11,14},{12,9},{14,11},{17,20},{19,... | collective-permute-start | bytes 1179656 | tf_op jit(solution)/shard_map/ppermute | solution.py:81
  175.8 2.1 %attend.4.refs_1_ = bf16[512,384]{1,0:T(8,128)(2,1)S(1)} custom-call(f32[512,384]{1,0:T(8,128)S(1)} %get-tuple-element.109.near_ref, f32[512,384]{1,0:T(8,128)S(1)} %convert_element_type.21.got_ref, f32[512,128]{1,0:T(8,128)S(1)} %get-tuple-element.103.cos_ref, f32[512,128]{1,0:T(8,128)S(1)} %get-tuple-element.104.sin_ref, ...), custom_call_target="tpu_custom_call" | custom-call | bytes 786432 | tf_op jit(solution)/shard_map/attend/pallas_call | solution.py:437
  177.9 3.1 %collective-permute-start.27 = (bf16[512,384]{1,0:T(8,128)(2,1)S(1)}, bf16[512,384]{1,0:T(8,128)(2,1)S(1)}, u32[]{:S(2)}, u32[]{:S(2)}) collective-permute-start(bf16[512,384]{1,0:T(8,128)(2,1)S(1)} %attend.4.refs_1_), channel_id=1, source_target_pairs={{1,4},{3,6},{4,1},{6,3},{9,12},{11,14},{12,9},{14,11},{17,20},{19,... | collective-permute-start | bytes 1179656 | tf_op jit(solution)/shard_map/ppermute | solution.py:81
  181.0 1.4 attend.5.refs_2_
  182.4 2.5 %collective-permute-start.28 = (bf16[512,256]{1,0:T(8,128)(2,1)S(1)}, bf16[512,256]{1,0:T(8,128)(2,1)S(1)}, u32[]{:S(2)}, u32[]{:S(2)}) collective-permute-start(bf16[512,256]{1,0:T(8,128)(2,1)S(1)} %attend.5.refs_2_), channel_id=1, source_target_pairs={{1,4},{3,6},{4,1},{6,3},{9,12},{11,14},{12,9},{14,11},{17,20},{19,... | collective-permute-start | bytes 786440 | tf_op jit(solution)/shard_map/ppermute | solution.py:81
  184.9 2.1 %collective-permute-done.27.refs_4_ = bf16[512,384]{1,0:T(8,128)(2,1)S(1)} collective-permute-done((bf16[512,384]{1,0:T(8,128)(2,1)S(1)}, bf16[512,384]{1,0:T(8,128)(2,1)S(1)}, u32[]{:S(2)}, u32[]{:S(2)}) %collective-permute-start.27) | collective-permute-done | bytes 393248 | tf_op jit(solution)/shard_map/ppermute | solution.py:81
  186.9 3.1 %collective-permute-done.28.refs_5_ = bf16[512,256]{1,0:T(8,128)(2,1)S(1)} collective-permute-done((bf16[512,256]{1,0:T(8,128)(2,1)S(1)}, bf16[512,256]{1,0:T(8,128)(2,1)S(1)}, u32[]{:S(2)}, u32[]{:S(2)}) %collective-permute-start.28) | collective-permute-done | bytes 262176 | tf_op jit(solution)/shard_map/ppermute | solution.py:81
  190.0 1.1 place.1
  (46 shorter events, 1.1 us)
Async XLA Ops:
  0.0 1.6 copy-start
  1.6 1.8 copy-start.1
  2.1 6.2 %copy-start.2 = (bf16[256,4096]{1,0:T(8,128)(2,1)S(1)}, bf16[256,4096]{1,0:T(8,128)(2,1)}, u32[]{:S(2)}) copy-start(bf16[256,4096]{1,0:T(8,128)(2,1)} %q_ref.1) | copy-start | bytes 6291460
  2.1 6.2 %copy-start.3 = (bf16[256,512]{1,0:T(8,128)(2,1)S(1)}, bf16[256,512]{1,0:T(8,128)(2,1)}, u32[]{:S(2)}) copy-start(bf16[256,512]{1,0:T(8,128)(2,1)} %k_ref.1) | copy-start | bytes 786436
  2.1 6.2 %copy-start.4 = (bf16[256,512]{1,0:T(8,128)(2,1)S(1)}, bf16[256,512]{1,0:T(8,128)(2,1)}, u32[]{:S(2)}) copy-start(bf16[256,512]{1,0:T(8,128)(2,1)} %v_ref.1) | copy-start | bytes 786436
  2.1 1.2 collective-permute-start
  3.5 42.7 %collective-permute-start.1 = (bf16[528,2048]{1,0:T(8,128)(2,1)S(1)}, bf16[528,2048]{1,0:T(8,128)(2,1)S(1)}, u32[]{:S(2)}, u32[]{:S(2)}) collective-permute-start(bf16[528,2048]{1,0:T(8,128)(2,1)S(1)} %stamp.1.refs_0_), channel_id=1, source_target_pairs={{1,8},{3,10},{5,13},{7,15},{8,0},{10,2},{12,5},{14,7},{17,24},{19,... | collective-permute-start | bytes 6488072 | tf_op jit(solution)/shard_map/ppermute | solution.py:81
  8.5 37.3 %collective-permute-start.2 = (bf16[256,1280]{1,0:T(8,128)(2,1)S(1)}, bf16[256,1280]{1,0:T(8,128)(2,1)S(1)}, u32[]{:S(2)}, u32[]{:S(2)}) collective-permute-start(bf16[256,1280]{1,0:T(8,128)(2,1)S(1)} %get-tuple-element.62.own_ref), channel_id=1, source_target_pairs={{0,16},{1,17},{2,18},{3,19},{4,20},{5,21},{6,22},{7,23},{8,24},{9,... | collective-permute-start | bytes 1966088 | tf_op jit(solution)/shard_map/ppermute | solution.py:81
  10.9 34.9 %collective-permute-start.3 = (bf16[256,1280]{1,0:T(8,128)(2,1)S(1)}, bf16[256,1280]{1,0:T(8,128)(2,1)S(1)}, u32[]{:S(2)}, u32[]{:S(2)}) collective-permute-start(bf16[256,1280]{1,0:T(8,128)(2,1)S(1)} %get-tuple-element.59), channel_id=1, source_target_pairs={{0,4},{1,5},{2,6},{3,7},{4,0},{5,1},{6,2},{7,3},{8,12},{9,13},{10,... | collective-permute-start | bytes 1966088 | tf_op jit(solution)/shard_map/ppermute | solution.py:81
  11.8 34.1 %collective-permute-start.4 = (bf16[256,1280]{1,0:T(8,128)(2,1)S(1)}, bf16[256,1280]{1,0:T(8,128)(2,1)S(1)}, u32[]{:S(2)}, u32[]{:S(2)}) collective-permute-start(bf16[256,1280]{1,0:T(8,128)(2,1)S(1)} %get-tuple-element.60), channel_id=1, source_target_pairs={{0,2},{1,3},{2,0},{3,1},{4,6},{5,7},{6,4},{7,5},{8,10},{9,11},{10,... | collective-permute-start | bytes 1966088 | tf_op jit(solution)/shard_map/ppermute | solution.py:81
  13.0 32.8 %collective-permute-start.5 = (bf16[256,1280]{1,0:T(8,128)(2,1)S(1)}, bf16[256,1280]{1,0:T(8,128)(2,1)S(1)}, u32[]{:S(2)}, u32[]{:S(2)}) collective-permute-start(bf16[256,1280]{1,0:T(8,128)(2,1)S(1)} %get-tuple-element.61), channel_id=1, source_target_pairs={{0,6},{1,7},{2,4},{3,5},{4,2},{5,3},{6,0},{7,1},{8,14},{9,15},{10,... | collective-permute-start | bytes 1966088 | tf_op jit(solution)/shard_map/ppermute | solution.py:81
  46.2 38.3 %collective-permute-start.6 = (bf16[528,2048]{1,0:T(8,128)(2,1)S(1)}, bf16[528,2048]{1,0:T(8,128)(2,1)S(1)}, u32[]{:S(2)}, u32[]{:S(2)}) collective-permute-start(bf16[528,2048]{1,0:T(8,128)(2,1)S(1)} %collective-permute-done.1.here), channel_id=1, source_target_pairs={{0,4},{2,6},{5,1},{7,3},{8,12},{10,14},{13,9},{15,11},{16,20},{18,... | collective-permute-start | bytes 6488072 | tf_op jit(solution)/shard_map/ppermute | solution.py:81
  47.5 37.1 %collective-permute-start.7 = (bf16[528,2048]{1,0:T(8,128)(2,1)S(1)}, bf16[528,2048]{1,0:T(8,128)(2,1)S(1)}, u32[]{:S(2)}, u32[]{:S(2)}) collective-permute-start(bf16[528,2048]{1,0:T(8,128)(2,1)S(1)} %collective-permute-done.1.here), channel_id=1, source_target_pairs={{0,2},{2,0},{5,7},{7,5},{8,10},{10,8},{13,15},{15,13},{16,18},{18,... | collective-permute-start | bytes 6488072 | tf_op jit(solution)/shard_map/ppermute | solution.py:81
  48.3 52.2 %collective-permute-start.8 = (bf16[528,2048]{1,0:T(8,128)(2,1)S(1)}, bf16[528,2048]{1,0:T(8,128)(2,1)S(1)}, u32[]{:S(2)}, u32[]{:S(2)}) collective-permute-start(bf16[528,2048]{1,0:T(8,128)(2,1)S(1)} %collective-permute-done.1.here), channel_id=1, source_target_pairs={{0,6},{2,4},{5,3},{7,1},{8,14},{10,12},{13,11},{15,9},{16,22},{18,... | collective-permute-start | bytes 6488072 | tf_op jit(solution)/shard_map/ppermute | solution.py:81
  49.6 55.3 %collective-permute-start.13 = (bf16[1280,1280]{1,0:T(8,128)(2,1)S(1)}, bf16[1280,1280]{1,0:T(8,128)(2,1)S(1)}, u32[]{:S(2)}, u32[]{:S(2)}) collective-permute-start(bf16[1280,1280]{1,0:T(8,128)(2,1)S(1)} %get-tuple-element.77.refs_0_.mine), channel_id=1, source_target_pairs={{0,1},{1,0},{2,3},{3,2},{4,5},{5,4},{6,7},{7,6},{8,9},{9,8},{10,11... | collective-permute-start | bytes 9830408 | tf_op jit(solution)/shard_map/ppermute | solution.py:81
  54.1 28.4 %collective-permute-start.9 = (bf16[768,384]{1,0:T(8,128)(2,1)S(1)}, bf16[768,384]{1,0:T(8,128)(2,1)S(1)}, u32[]{:S(2)}, u32[]{:S(2)}) collective-permute-start(bf16[768,384]{1,0:T(8,128)(2,1)S(1)} %get-tuple-element.74), channel_id=1, source_target_pairs={{0,16},{1,17},{2,18},{3,19},{4,20},{5,21},{6,22},{7,23},{8,24},{9,... | collective-permute-start | bytes 1769480 | tf_op jit(solution)/shard_map/ppermute | solution.py:81
  82.5 19.6 %collective-permute-start.12 = (bf16[528,2048]{1,0:T(8,128)(2,1)S(1)}, bf16[528,2048]{1,0:T(8,128)(2,1)S(1)}, u32[]{:S(2)}, u32[]{:S(2)}) collective-permute-start(bf16[528,2048]{1,0:T(8,128)(2,1)S(1)} %stamp.1.refs_0_), channel_id=1, source_target_pairs={{4,5},{6,7},{9,8},{11,10},{20,21},{22,23},{25,24},{27,26}} | collective-permute-start | bytes 6488072 | tf_op jit(solution)/shard_map/ppermute | solution.py:81
  84.5 20.4 %collective-permute-start.10 = (bf16[768,256]{1,0:T(8,128)(2,1)S(1)}, bf16[768,256]{1,0:T(8,128)(2,1)S(1)}, u32[]{:S(2)}, u32[]{:S(2)}) collective-permute-start(bf16[768,256]{1,0:T(8,128)(2,1)S(1)} %get-tuple-element.76), channel_id=1, source_target_pairs={{0,16},{1,17},{2,18},{3,19},{4,20},{5,21},{6,22},{7,23},{8,24},{9,... | collective-permute-start | bytes 1179656 | tf_op jit(solution)/shard_map/ppermute | solution.py:81
  84.6 20.3 %collective-permute-start.11 = (bf16[768,384]{1,0:T(8,128)(2,1)S(1)}, bf16[768,384]{1,0:T(8,128)(2,1)S(1)}, u32[]{:S(2)}, u32[]{:S(2)}) collective-permute-start(bf16[768,384]{1,0:T(8,128)(2,1)S(1)} %collective-permute-done.9.refs_2_.refs_0_), channel_id=1, source_target_pairs={{0,1},{1,0},{2,3},{3,2},{4,5},{5,4},{6,7},{7,6},{8,9},{9,8},{10,11... | collective-permute-start | bytes 1769480 | tf_op jit(solution)/shard_map/ppermute | solution.py:81
  104.9 31.0 %collective-permute-start.14 = (bf16[528,2048]{1,0:T(8,128)(2,1)S(1)}, bf16[528,2048]{1,0:T(8,128)(2,1)S(1)}, u32[]{:S(2)}, u32[]{:S(2)}) collective-permute-start(bf16[528,2048]{1,0:T(8,128)(2,1)S(1)} %stamp.1.refs_0_), channel_id=1, source_target_pairs={{0,4},{2,6},{4,1},{6,3},{9,12},{11,14},{13,9},{15,11},{16,20},{18,... | collective-permute-start | bytes 6488072 | tf_op jit(solution)/shard_map/ppermute | solution.py:81
  106.2 32.4 %collective-permute-start.15 = (bf16[528,2048]{1,0:T(8,128)(2,1)S(1)}, bf16[528,2048]{1,0:T(8,128)(2,1)S(1)}, u32[]{:S(2)}, u32[]{:S(2)}) collective-permute-start(bf16[528,2048]{1,0:T(8,128)(2,1)S(1)} %stamp.1.refs_0_), channel_id=1, source_target_pairs={{0,2},{2,0},{4,7},{6,5},{9,10},{11,8},{13,15},{15,13},{16,18},{18,... | collective-permute-start | bytes 6488072 | tf_op jit(solution)/shard_map/ppermute | solution.py:81
  107.0 52.6 %collective-permute-start.16 = (bf16[528,2048]{1,0:T(8,128)(2,1)S(1)}, bf16[528,2048]{1,0:T(8,128)(2,1)S(1)}, u32[]{:S(2)}, u32[]{:S(2)}) collective-permute-start(bf16[528,2048]{1,0:T(8,128)(2,1)S(1)} %stamp.1.refs_0_), channel_id=1, source_target_pairs={{0,6},{2,4},{4,3},{6,1},{9,14},{11,12},{13,11},{15,9},{16,22},{18,... | collective-permute-start | bytes 6488072 | tf_op jit(solution)/shard_map/ppermute | solution.py:81
  108.5 27.4 %collective-permute-start.17 = (bf16[768,384]{1,0:T(8,128)(2,1)S(1)}, bf16[768,384]{1,0:T(8,128)(2,1)S(1)}, u32[]{:S(2)}, u32[]{:S(2)}) collective-permute-start(bf16[768,384]{1,0:T(8,128)(2,1)S(1)} %get-tuple-element.84), channel_id=1, source_target_pairs={{0,16},{1,17},{2,18},{3,19},{4,20},{5,21},{6,22},{7,23},{8,24},{9,... | collective-permute-start | bytes 1769480 | tf_op jit(solution)/shard_map/ppermute | solution.py:81
  108.6 8.1 %collective-permute-start.19 = (bf16[768,256]{1,0:T(8,128)(2,1)S(1)}, bf16[768,256]{1,0:T(8,128)(2,1)S(1)}, u32[]{:S(2)}, u32[]{:S(2)}) collective-permute-start(bf16[768,256]{1,0:T(8,128)(2,1)S(1)} %collective-permute-done.10.refs_3_.refs_1_), channel_id=1, source_target_pairs={{0,1},{1,0},{2,3},{3,2},{4,5},{5,4},{6,7},{7,6},{8,9},{9,8},{10,11... | collective-permute-start | bytes 1179656 | tf_op jit(solution)/shard_map/ppermute | solution.py:81
  118.1 43.4 %collective-permute-start.21 = (f32[512,256]{1,0:T(8,128)S(1)}, f32[512,256]{1,0:T(8,128)S(1)}, u32[]{:S(2)}, u32[]{:S(2)}) collective-permute-start(f32[512,256]{1,0:T(8,128)S(1)} %get-tuple-element.90), channel_id=1, source_target_pairs={{0,8},{1,9},{2,10},{3,11},{4,12},{5,13},{6,14},{7,15},{8,0},{9,1},... | collective-permute-start | bytes 1572872 | tf_op jit(solution)/shard_map/ppermute | solution.py:81
  135.9 25.6 %collective-permute-start.22 = (f16[512,384]{1,0:T(8,128)(2,1)S(1)}, f16[512,384]{1,0:T(8,128)(2,1)S(1)}, u32[]{:S(2)}, u32[]{:S(2)}) collective-permute-start(f16[512,384]{1,0:T(8,128)(2,1)S(1)} %convert_element_type.18), channel_id=1, source_target_pairs={{0,8},{1,9},{2,10},{3,11},{4,12},{5,13},{6,14},{7,15},{8,0},{9,1},... | collective-permute-start | bytes 1179656 | tf_op jit(solution)/shard_map/ppermute | solution.py:81
  135.9 25.6 %collective-permute-start.18 = (bf16[768,256]{1,0:T(8,128)(2,1)S(1)}, bf16[768,256]{1,0:T(8,128)(2,1)S(1)}, u32[]{:S(2)}, u32[]{:S(2)}) collective-permute-start(bf16[768,256]{1,0:T(8,128)(2,1)S(1)} %get-tuple-element.86), channel_id=1, source_target_pairs={{0,16},{1,17},{2,18},{3,19},{4,20},{5,21},{6,22},{7,23},{8,24},{9,... | collective-permute-start | bytes 1179656 | tf_op jit(solution)/shard_map/ppermute | solution.py:81
  138.6 22.9 %collective-permute-start.20 = (bf16[768,384]{1,0:T(8,128)(2,1)S(1)}, bf16[768,384]{1,0:T(8,128)(2,1)S(1)}, u32[]{:S(2)}, u32[]{:S(2)}) collective-permute-start(bf16[768,384]{1,0:T(8,128)(2,1)S(1)} %collective-permute-done.17.refs_2_), channel_id=1, source_target_pairs={{0,1},{1,0},{2,3},{3,2},{4,5},{5,4},{6,7},{7,6},{8,9},{9,8},{10,11... | collective-permute-start | bytes 1769480 | tf_op jit(solution)/shard_map/ppermute | solution.py:81
  161.5 1.8 collective-permute-start.23
  162.7 13.0 %collective-permute-start.24 = (f16[512,384]{1,0:T(8,128)(2,1)S(1)}, f16[512,384]{1,0:T(8,128)(2,1)S(1)}, u32[]{:S(2)}, u32[]{:S(2)}) collective-permute-start(f16[512,384]{1,0:T(8,128)(2,1)S(1)} %convert_element_type.20), channel_id=1, source_target_pairs={{0,8},{1,9},{2,10},{3,11},{4,12},{5,13},{6,14},{7,15},{8,0},{9,1},... | collective-permute-start | bytes 1179656 | tf_op jit(solution)/shard_map/ppermute | solution.py:81
  163.9 17.0 %collective-permute-start.25 = (f16[512,256]{1,0:T(8,128)(2,1)S(1)}, f16[512,256]{1,0:T(8,128)(2,1)S(1)}, u32[]{:S(2)}, u32[]{:S(2)}) collective-permute-start(f16[512,256]{1,0:T(8,128)(2,1)S(1)} %convert_element_type.22), channel_id=1, source_target_pairs={{0,8},{1,9},{2,10},{3,11},{4,12},{5,13},{6,14},{7,15},{8,0},{9,1},... | collective-permute-start | bytes 786440 | tf_op jit(solution)/shard_map/ppermute | solution.py:81
  173.2 11.6 %collective-permute-start.26 = (bf16[512,384]{1,0:T(8,128)(2,1)S(1)}, bf16[512,384]{1,0:T(8,128)(2,1)S(1)}, u32[]{:S(2)}, u32[]{:S(2)}) collective-permute-start(bf16[512,384]{1,0:T(8,128)(2,1)S(1)} %attend.3.refs_0_), channel_id=1, source_target_pairs={{1,4},{3,6},{4,1},{6,3},{9,12},{11,14},{12,9},{14,11},{17,20},{19,... | collective-permute-start | bytes 1179656 | tf_op jit(solution)/shard_map/ppermute | solution.py:81
  177.9 9.1 %collective-permute-start.27 = (bf16[512,384]{1,0:T(8,128)(2,1)S(1)}, bf16[512,384]{1,0:T(8,128)(2,1)S(1)}, u32[]{:S(2)}, u32[]{:S(2)}) collective-permute-start(bf16[512,384]{1,0:T(8,128)(2,1)S(1)} %attend.4.refs_1_), channel_id=1, source_target_pairs={{1,4},{3,6},{4,1},{6,3},{9,12},{11,14},{12,9},{14,11},{17,20},{19,... | collective-permute-start | bytes 1179656 | tf_op jit(solution)/shard_map/ppermute | solution.py:81
  182.4 7.7 %collective-permute-start.28 = (bf16[512,256]{1,0:T(8,128)(2,1)S(1)}, bf16[512,256]{1,0:T(8,128)(2,1)S(1)}, u32[]{:S(2)}, u32[]{:S(2)}) collective-permute-start(bf16[512,256]{1,0:T(8,128)(2,1)S(1)} %attend.5.refs_2_), channel_id=1, source_target_pairs={{1,4},{3,6},{4,1},{6,3},{9,12},{11,14},{12,9},{14,11},{17,20},{19,... | collective-permute-start | bytes 786440 | tf_op jit(solution)/shard_map/ppermute | solution.py:81

commit v6 on v5

--- a/solution.py
+++ b/solution.py
@@ -113,7 +113,7 @@
 )
 VMEM = {
     "pack": 8, "squares": 6, "stamp": 6, "rest": 10, "scale_rows": 16, "early": 15,
-    "late": 14, "whole": 20, "keys": 4, "attend": 10, "place": 5,
+    "late": 14, "whole": 22, "attend": 10, "place": 5,
 }
 
 
@@ -246,13 +246,13 @@
             outs[i][:, at * HD : (at + 1) * HD] = got[:, h * HD : (h + 1) * HD]
 
 
-def whole_kernel(lhs, mine, other, *refs):
+def whole_kernel(lhs, kv_sum, cos_ref, sin_ref, mine, other, *refs):
     count = len(CHUNKS)
     rest, rest_core, outs = refs[:count], refs[count : 2 * count], list(refs[2 * count :])
     depth = mine.shape[0]
     near = dot(lhs[:, :depth], mine[...]) + dot(lhs[:, depth : 2 * depth], other[...])
     for chunks, places in PARTS:
-        parts = [outs.pop(0) for _ in range(1 + max(i for i, _ in places))]
+        parts = [outs.pop(0) for _ in range(1 + 2 * max(i for i, _ in places))]
         places = iter(places)
         for j in chunks:
             lo, hi = CHUNKS[j]
@@ -262,7 +262,13 @@
                 at += ref.shape[0]
             for h in range(hi - lo):
                 i, to = next(places)
-                parts[i][:, to * HD : (to + 1) * HD] = got[:, h * HD : (h + 1) * HD]
+                head, at = got[:, h * HD : (h + 1) * HD], slice(to * HD, (to + 1) * HD)
+                if i == 0:
+                    parts[0][:, at] = head
+                elif to == 0:
+                    parts[1][...] = turn(head + kv_sum[:, at], cos_ref[...], sin_ref[...])
+                else:
+                    parts[2][...] = (head + kv_sum[:, at]).astype(jnp.bfloat16)
 
 
 def place_kernel(*refs):
@@ -287,12 +293,6 @@
 
 def turn(value, cosine, sine):
     return (value * cosine + pltpu.roll(value, HD // 2, 1) * sine).astype(jnp.bfloat16)
-
-
-def keys_kernel(near_ref, got_ref, cos_ref, sin_ref, k_ref, v_ref):
-    lin = near_ref[...] + got_ref[...]
-    k_ref[...] = turn(lin[:, :HD], cos_ref[...], sin_ref[...])
-    v_ref[...] = lin[:, HD:].astype(jnp.bfloat16)
 
 
 def attend_kernel(near_ref, got_ref, cos_ref, sin_ref, k_ref, v_ref, out_ref):
@@ -424,15 +424,12 @@
         return None if x == c else (z, c, y, x)
 
     widths = [[HD * sum(i == j for i, _ in places) for j in range(2)] for _, places in PARTS]
-    part, kv_part, *parts = call(
-        whole_kernel,
-        [jax.ShapeDtypeStruct((rows, n), jnp.float32) for ns in widths for n in ns if n > 0],
-        name="whole",
-    )(near_block, mine_all, other_all, *far_rest, *rest_core)
+    shapes = [jax.ShapeDtypeStruct((rows, ns[0]), jnp.float32) for ns in widths]
+    shapes[1:1] = [jax.ShapeDtypeStruct((rows, HD), bf16)] * 2
+    part, k_rot, v_val, *parts = call(whole_kernel, shapes, name="whole")(
+        near_block, kv_sum, cosine, sine, mine_all, other_all, *far_rest, *rest_core
+    )
     parts = [part, *parts]
-    k_rot, v_val = call(
-        keys_kernel, [jax.ShapeDtypeStruct((rows, HD), bf16)] * 2, name="keys"
-    )(kv_part, kv_sum, cosine, sine)
     outs = [
         call(attend_kernel, jax.ShapeDtypeStruct(part.shape, bf16), name="attend")(
             part, got.astype(jnp.float32), cosine, sine, k_rot, v_val

time: 191 us -> 191 us (level)
    pallas_call x2 -> x1, Pallas kernels: 6.16 us -> 6 us  [split_plan(): call(whole_kernel, shapes, name='whole')]
where the time goes in v6:
time: 191 us
  waiting for transfers between devices  87 us (46%)
  starting transfers between devices  75.9 us (40%)
  Pallas kernels  23.8 us (12%)
  local copies, waits for them, and re-layouts  2.46 us (1%)
    ppermute x29, waiting for transfers between devices, move(): return lax.ppermute(value, AXES, pairs)  87 us
    ppermute x29, starting transfers between devices, move(): return lax.ppermute(value, AXES, pairs)  75.9 us
    pallas_call x1, Pallas kernels, split_plan(): call(whole_kernel, shapes, name='whole')  6 us
    pallas_call x3, Pallas kernels, split_plan(): call(attend_kernel, jax.ShapeDtypeStruct(part.shape, bf16), name='attend')  5.49 us
  transfers between devices with their start and end apart: 29, of which 8 were waited for; matrix products, arithmetic and copies ran while one was open for 1% of the time, Pallas kernels for 12%

profile of v6, /device:TPU:1, one launch (start us, length us, event | category | flops | bytes accessed | tf_op | source)
XLA Modules:
  0.0 191.0 jit_solution(1633886067656473168)
XLA Ops:
  0.0 1.6 copy-done
  1.6 0.5 squares.1.own_ref
  2.2 0.9 broadcast_in_dim.2.gain_ref
  3.1 0.3 collective-permute-done.got_ref
  3.5 4.7 %collective-permute-start.1 = (bf16[528,2048]{1,0:T(8,128)(2,1)S(1)}, bf16[528,2048]{1,0:T(8,128)(2,1)S(1)}, u32[]{:S(2)}, u32[]{:S(2)}) collective-permute-start(bf16[528,2048]{1,0:T(8,128)(2,1)S(1)} %stamp.1.refs_0_), channel_id=1, source_target_pairs={{1,8},{3,10},{5,13},{7,15},{8,0},{10,2},{12,5},{14,7},{17,24},{19,... | collective-permute-start | bytes 6488072 | tf_op jit(solution)/shard_map/ppermute | solution.py:81
  8.3 0.2 pack.1
  8.5 2.4 %collective-permute-start.2 = (bf16[256,1280]{1,0:T(8,128)(2,1)S(1)}, bf16[256,1280]{1,0:T(8,128)(2,1)S(1)}, u32[]{:S(2)}, u32[]{:S(2)}) collective-permute-start(bf16[256,1280]{1,0:T(8,128)(2,1)S(1)} %get-tuple-element.61.own_ref), channel_id=1, source_target_pairs={{0,16},{1,17},{2,18},{3,19},{4,20},{5,21},{6,22},{7,23},{8,24},{9,... | collective-permute-start | bytes 1966088 | tf_op jit(solution)/shard_map/ppermute | solution.py:81
  10.9 0.9 collective-permute-start.3
  11.8 1.2 collective-permute-start.4
  13.0 0.5 collective-permute-start.5
  13.6 32.3 %collective-permute-done.2.far_ref = bf16[256,1280]{1,0:T(8,128)(2,1)S(1)} collective-permute-done((bf16[256,1280]{1,0:T(8,128)(2,1)S(1)}, bf16[256,1280]{1,0:T(8,128)(2,1)S(1)}, u32[]{:S(2)}, u32[]{:S(2)}) %collective-permute-start.2) | collective-permute-done | bytes 655392 | tf_op jit(solution)/shard_map/ppermute | solution.py:81
  45.9 0.4 rest.1
  46.2 1.3 collective-permute-start.6
  47.5 0.8 collective-permute-start.7
  48.3 1.3 collective-permute-start.8
  49.6 4.4 %collective-permute-start.13 = (bf16[1280,1280]{1,0:T(8,128)(2,1)S(1)}, bf16[1280,1280]{1,0:T(8,128)(2,1)S(1)}, u32[]{:S(2)}, u32[]{:S(2)}) collective-permute-start(bf16[1280,1280]{1,0:T(8,128)(2,1)S(1)} %get-tuple-element.76.refs_0_.mine), channel_id=1, source_target_pairs={{0,1},{1,0},{2,3},{3,2},{4,5},{5,4},{6,7},{7,6},{8,9},{9,8},{10,11... | collective-permute-start | bytes 9830408 | tf_op jit(solution)/shard_map/ppermute | solution.py:81
  54.1 28.4 %collective-permute-done.9.refs_2_.refs_0_ = bf16[768,384]{1,0:T(8,128)(2,1)S(1)} collective-permute-done((bf16[768,384]{1,0:T(8,128)(2,1)S(1)}, bf16[768,384]{1,0:T(8,128)(2,1)S(1)}, u32[]{:S(2)}, u32[]{:S(2)}) %collective-permute-start.9) | collective-permute-done | bytes 589856 | tf_op jit(solution)/shard_map/ppermute | solution.py:81
  82.5 0.8 collective-permute-start.12
  83.3 1.0 fusion.2
  84.3 0.2 pad_maximum_fusion
  84.6 15.9 %collective-permute-start.11 = (bf16[768,384]{1,0:T(8,128)(2,1)S(1)}, bf16[768,384]{1,0:T(8,128)(2,1)S(1)}, u32[]{:S(2)}, u32[]{:S(2)}) collective-permute-start(bf16[768,384]{1,0:T(8,128)(2,1)S(1)} %collective-permute-done.9.refs_2_.refs_0_), channel_id=1, source_target_pairs={{0,1},{1,0},{2,3},{3,2},{4,5},{5,4},{6,7},{7,6},{8,9},{9,8},{10,11... | collective-permute-start | bytes 1769480 | tf_op jit(solution)/shard_map/ppermute | solution.py:81
  100.5 1.6 scale_rows.2.lhs.refs_0_
  102.1 2.8 %collective-permute-done.10.refs_3_.refs_1_ = bf16[768,256]{1,0:T(8,128)(2,1)S(1)} collective-permute-done((bf16[768,256]{1,0:T(8,128)(2,1)S(1)}, bf16[768,256]{1,0:T(8,128)(2,1)S(1)}, u32[]{:S(2)}, u32[]{:S(2)}) %collective-permute-start.10) | collective-permute-done | bytes 393248 | tf_op jit(solution)/shard_map/ppermute | solution.py:81
  104.9 1.3 collective-permute-start.14
  106.2 0.8 collective-permute-start.15
  107.0 1.5 collective-permute-start.16
  108.6 4.5 %collective-permute-start.19 = (bf16[768,256]{1,0:T(8,128)(2,1)S(1)}, bf16[768,256]{1,0:T(8,128)(2,1)S(1)}, u32[]{:S(2)}, u32[]{:S(2)}) collective-permute-start(bf16[768,256]{1,0:T(8,128)(2,1)S(1)} %collective-permute-done.10.refs_3_.refs_1_), channel_id=1, source_target_pairs={{0,1},{1,0},{2,3},{3,2},{4,5},{5,4},{6,7},{7,6},{8,9},{9,8},{10,11... | collective-permute-start | bytes 1179656 | tf_op jit(solution)/shard_map/ppermute | solution.py:81
  113.1 3.5 %early.1.refs_1_ = f32[512,1280]{1,0:T(8,128)S(1)} custom-call(bf16[512,4096]{1,0:T(8,128)(2,1)S(1)} %scale_rows.2.lhs.refs_0_, bf16[1280,1280]{1,0:T(8,128)(2,1)S(1)} %get-tuple-element.76.refs_0_.mine, bf16[1280,1280]{1,0:T(8,128)(2,1)S(1)} %collective-permute-done.13.refs_1_.other), custom_call_target="tpu_custom_call" | custom-call | bytes 5242880 | tf_op jit(solution)/shard_map/early/pallas_call | solution.py:397
  116.7 1.4 late.3
  118.1 0.4 collective-permute-start.21
  118.5 17.4 %collective-permute-done.17.refs_2_ = bf16[768,384]{1,0:T(8,128)(2,1)S(1)} collective-permute-done((bf16[768,384]{1,0:T(8,128)(2,1)S(1)}, bf16[768,384]{1,0:T(8,128)(2,1)S(1)}, u32[]{:S(2)}, u32[]{:S(2)}) %collective-permute-start.17) | collective-permute-done | bytes 589856 | tf_op jit(solution)/shard_map/ppermute | solution.py:81
  135.9 2.6 %collective-permute-start.18 = (bf16[768,256]{1,0:T(8,128)(2,1)S(1)}, bf16[768,256]{1,0:T(8,128)(2,1)S(1)}, u32[]{:S(2)}, u32[]{:S(2)}) collective-permute-start(bf16[768,256]{1,0:T(8,128)(2,1)S(1)} %get-tuple-element.85), channel_id=1, source_target_pairs={{0,16},{1,17},{2,18},{3,19},{4,20},{5,21},{6,22},{7,23},{8,24},{9,... | collective-permute-start | bytes 1179656 | tf_op jit(solution)/shard_map/ppermute | solution.py:81
  138.6 21.1 %collective-permute-start.20 = (bf16[768,384]{1,0:T(8,128)(2,1)S(1)}, bf16[768,384]{1,0:T(8,128)(2,1)S(1)}, u32[]{:S(2)}, u32[]{:S(2)}) collective-permute-start(bf16[768,384]{1,0:T(8,128)(2,1)S(1)} %collective-permute-done.17.refs_2_), channel_id=1, source_target_pairs={{0,1},{1,0},{2,3},{3,2},{4,5},{5,4},{6,7},{7,6},{8,9},{9,8},{10,11... | collective-permute-start | bytes 1769480 | tf_op jit(solution)/shard_map/ppermute | solution.py:81
  159.6 1.8 scale_rows.3.lhs
  161.6 1.0 late.5
  162.8 0.5 collective-permute-done.23.refs_3_.refs_7_
  163.3 0.6 late.4
  163.9 1.0 collective-permute-start.25
  165.0 6.0 %whole.1 = (f32[512,384]{1,0:T(8,128)S(1)}, bf16[512,128]{1,0:T(8,128)(2,1)S(1)}, bf16[512,128]{1,0:T(8,128)(2,1)S(1)}, f32[512,384]{1,0:T(8,128)S(1)}, f32[512,256]{1,0:T(8,128)S(1)}) custom-call(bf16[512,4096]{1,0:T(8,128)(2,1)S(1)} %scale_rows.3.lhs, f32[512,256]{1,0:T(8,128)S(1)} %collective-permute-done.21.kv_sum, ...), custom_call_target="tpu_custom_call" | custom-call | bytes 4718592 | tf_op jit(solution)/shard_map/whole/pallas_call | solution.py:429
  171.0 2.1 %attend.3.refs_0_ = bf16[512,384]{1,0:T(8,128)(2,1)S(1)} custom-call(f32[512,384]{1,0:T(8,128)S(1)} %get-tuple-element.103.near_ref, f32[512,384]{1,0:T(8,128)S(1)} %convert_element_type.19.got_ref, f32[512,128]{1,0:T(8,128)S(1)} %get-tuple-element.95.cos_ref, f32[512,128]{1,0:T(8,128)S(1)} %get-tuple-element.96.sin_ref, ...), custom_call_target="tpu_custom_call" | custom-call | bytes 786432 | tf_op jit(solution)/shard_map/attend/pallas_call | solution.py:434
  173.1 2.5 %collective-permute-start.26 = (bf16[512,384]{1,0:T(8,128)(2,1)S(1)}, bf16[512,384]{1,0:T(8,128)(2,1)S(1)}, u32[]{:S(2)}, u32[]{:S(2)}) collective-permute-start(bf16[512,384]{1,0:T(8,128)(2,1)S(1)} %attend.3.refs_0_), channel_id=1, source_target_pairs={{1,4},{3,6},{4,1},{6,3},{9,12},{11,14},{12,9},{14,11},{17,20},{19,... | collective-permute-start | bytes 1179656 | tf_op jit(solution)/shard_map/ppermute | solution.py:81
  175.6 2.1 %attend.4.refs_1_ = bf16[512,384]{1,0:T(8,128)(2,1)S(1)} custom-call(f32[512,384]{1,0:T(8,128)S(1)} %get-tuple-element.107.near_ref, f32[512,384]{1,0:T(8,128)S(1)} %convert_element_type.21.got_ref, f32[512,128]{1,0:T(8,128)S(1)} %get-tuple-element.95.cos_ref, f32[512,128]{1,0:T(8,128)S(1)} %get-tuple-element.96.sin_ref, ...), custom_call_target="tpu_custom_call" | custom-call | bytes 786432 | tf_op jit(solution)/shard_map/attend/pallas_call | solution.py:434
  177.7 3.1 %collective-permute-start.27 = (bf16[512,384]{1,0:T(8,128)(2,1)S(1)}, bf16[512,384]{1,0:T(8,128)(2,1)S(1)}, u32[]{:S(2)}, u32[]{:S(2)}) collective-permute-start(bf16[512,384]{1,0:T(8,128)(2,1)S(1)} %attend.4.refs_1_), channel_id=1, source_target_pairs={{1,4},{3,6},{4,1},{6,3},{9,12},{11,14},{12,9},{14,11},{17,20},{19,... | collective-permute-start | bytes 1179656 | tf_op jit(solution)/shard_map/ppermute | solution.py:81
  180.8 1.4 attend.5.refs_2_
  182.2 2.5 %collective-permute-start.28 = (bf16[512,256]{1,0:T(8,128)(2,1)S(1)}, bf16[512,256]{1,0:T(8,128)(2,1)S(1)}, u32[]{:S(2)}, u32[]{:S(2)}) collective-permute-start(bf16[512,256]{1,0:T(8,128)(2,1)S(1)} %attend.5.refs_2_), channel_id=1, source_target_pairs={{1,4},{3,6},{4,1},{6,3},{9,12},{11,14},{12,9},{14,11},{17,20},{19,... | collective-permute-start | bytes 786440 | tf_op jit(solution)/shard_map/ppermute | solution.py:81
  184.7 2.1 %collective-permute-done.27.refs_4_ = bf16[512,384]{1,0:T(8,128)(2,1)S(1)} collective-permute-done((bf16[512,384]{1,0:T(8,128)(2,1)S(1)}, bf16[512,384]{1,0:T(8,128)(2,1)S(1)}, u32[]{:S(2)}, u32[]{:S(2)}) %collective-permute-start.27) | collective-permute-done | bytes 393248 | tf_op jit(solution)/shard_map/ppermute | solution.py:81
  186.8 3.1 %collective-permute-done.28.refs_5_ = bf16[512,256]{1,0:T(8,128)(2,1)S(1)} collective-permute-done((bf16[512,256]{1,0:T(8,128)(2,1)S(1)}, bf16[512,256]{1,0:T(8,128)(2,1)S(1)}, u32[]{:S(2)}, u32[]{:S(2)}) %collective-permute-start.28) | collective-permute-done | bytes 262176 | tf_op jit(solution)/shard_map/ppermute | solution.py:81
  189.9 1.1 place.1
  (45 shorter events, 1.0 us)
Async XLA Ops:
  0.0 1.6 copy-start
  1.6 1.8 copy-start.1
  2.1 6.2 %copy-start.2 = (bf16[256,4096]{1,0:T(8,128)(2,1)S(1)}, bf16[256,4096]{1,0:T(8,128)(2,1)}, u32[]{:S(2)}) copy-start(bf16[256,4096]{1,0:T(8,128)(2,1)} %q_ref.1) | copy-start | bytes 6291460
  2.1 6.2 %copy-start.3 = (bf16[256,512]{1,0:T(8,128)(2,1)S(1)}, bf16[256,512]{1,0:T(8,128)(2,1)}, u32[]{:S(2)}) copy-start(bf16[256,512]{1,0:T(8,128)(2,1)} %k_ref.1) | copy-start | bytes 786436
  2.1 6.2 %copy-start.4 = (bf16[256,512]{1,0:T(8,128)(2,1)S(1)}, bf16[256,512]{1,0:T(8,128)(2,1)}, u32[]{:S(2)}) copy-start(bf16[256,512]{1,0:T(8,128)(2,1)} %v_ref.1) | copy-start | bytes 786436
  2.1 1.2 collective-permute-start
  3.5 42.7 %collective-permute-start.1 = (bf16[528,2048]{1,0:T(8,128)(2,1)S(1)}, bf16[528,2048]{1,0:T(8,128)(2,1)S(1)}, u32[]{:S(2)}, u32[]{:S(2)}) collective-permute-start(bf16[528,2048]{1,0:T(8,128)(2,1)S(1)} %stamp.1.refs_0_), channel_id=1, source_target_pairs={{1,8},{3,10},{5,13},{7,15},{8,0},{10,2},{12,5},{14,7},{17,24},{19,... | collective-permute-start | bytes 6488072 | tf_op jit(solution)/shard_map/ppermute | solution.py:81
  8.5 37.3 %collective-permute-start.2 = (bf16[256,1280]{1,0:T(8,128)(2,1)S(1)}, bf16[256,1280]{1,0:T(8,128)(2,1)S(1)}, u32[]{:S(2)}, u32[]{:S(2)}) collective-permute-start(bf16[256,1280]{1,0:T(8,128)(2,1)S(1)} %get-tuple-element.61.own_ref), channel_id=1, source_target_pairs={{0,16},{1,17},{2,18},{3,19},{4,20},{5,21},{6,22},{7,23},{8,24},{9,... | collective-permute-start | bytes 1966088 | tf_op jit(solution)/shard_map/ppermute | solution.py:81
  10.9 34.9 %collective-permute-start.3 = (bf16[256,1280]{1,0:T(8,128)(2,1)S(1)}, bf16[256,1280]{1,0:T(8,128)(2,1)S(1)}, u32[]{:S(2)}, u32[]{:S(2)}) collective-permute-start(bf16[256,1280]{1,0:T(8,128)(2,1)S(1)} %get-tuple-element.58), channel_id=1, source_target_pairs={{0,4},{1,5},{2,6},{3,7},{4,0},{5,1},{6,2},{7,3},{8,12},{9,13},{10,... | collective-permute-start | bytes 1966088 | tf_op jit(solution)/shard_map/ppermute | solution.py:81
  11.8 34.1 %collective-permute-start.4 = (bf16[256,1280]{1,0:T(8,128)(2,1)S(1)}, bf16[256,1280]{1,0:T(8,128)(2,1)S(1)}, u32[]{:S(2)}, u32[]{:S(2)}) collective-permute-start(bf16[256,1280]{1,0:T(8,128)(2,1)S(1)} %get-tuple-element.59), channel_id=1, source_target_pairs={{0,2},{1,3},{2,0},{3,1},{4,6},{5,7},{6,4},{7,5},{8,10},{9,11},{10,... | collective-permute-start | bytes 1966088 | tf_op jit(solution)/shard_map/ppermute | solution.py:81
  13.0 32.8 %collective-permute-start.5 = (bf16[256,1280]{1,0:T(8,128)(2,1)S(1)}, bf16[256,1280]{1,0:T(8,128)(2,1)S(1)}, u32[]{:S(2)}, u32[]{:S(2)}) collective-permute-start(bf16[256,1280]{1,0:T(8,128)(2,1)S(1)} %get-tuple-element.60), channel_id=1, source_target_pairs={{0,6},{1,7},{2,4},{3,5},{4,2},{5,3},{6,0},{7,1},{8,14},{9,15},{10,... | collective-permute-start | bytes 1966088 | tf_op jit(solution)/shard_map/ppermute | solution.py:81
  46.2 38.3 %collective-permute-start.6 = (bf16[528,2048]{1,0:T(8,128)(2,1)S(1)}, bf16[528,2048]{1,0:T(8,128)(2,1)S(1)}, u32[]{:S(2)}, u32[]{:S(2)}) collective-permute-start(bf16[528,2048]{1,0:T(8,128)(2,1)S(1)} %collective-permute-done.1.here), channel_id=1, source_target_pairs={{0,4},{2,6},{5,1},{7,3},{8,12},{10,14},{13,9},{15,11},{16,20},{18,... | collective-permute-start | bytes 6488072 | tf_op jit(solution)/shard_map/ppermute | solution.py:81
  47.5 37.1 %collective-permute-start.7 = (bf16[528,2048]{1,0:T(8,128)(2,1)S(1)}, bf16[528,2048]{1,0:T(8,128)(2,1)S(1)}, u32[]{:S(2)}, u32[]{:S(2)}) collective-permute-start(bf16[528,2048]{1,0:T(8,128)(2,1)S(1)} %collective-permute-done.1.here), channel_id=1, source_target_pairs={{0,2},{2,0},{5,7},{7,5},{8,10},{10,8},{13,15},{15,13},{16,18},{18,... | collective-permute-start | bytes 6488072 | tf_op jit(solution)/shard_map/ppermute | solution.py:81
  48.3 52.2 %collective-permute-start.8 = (bf16[528,2048]{1,0:T(8,128)(2,1)S(1)}, bf16[528,2048]{1,0:T(8,128)(2,1)S(1)}, u32[]{:S(2)}, u32[]{:S(2)}) collective-permute-start(bf16[528,2048]{1,0:T(8,128)(2,1)S(1)} %collective-permute-done.1.here), channel_id=1, source_target_pairs={{0,6},{2,4},{5,3},{7,1},{8,14},{10,12},{13,11},{15,9},{16,22},{18,... | collective-permute-start | bytes 6488072 | tf_op jit(solution)/shard_map/ppermute | solution.py:81
  49.6 55.3 %collective-permute-start.13 = (bf16[1280,1280]{1,0:T(8,128)(2,1)S(1)}, bf16[1280,1280]{1,0:T(8,128)(2,1)S(1)}, u32[]{:S(2)}, u32[]{:S(2)}) collective-permute-start(bf16[1280,1280]{1,0:T(8,128)(2,1)S(1)} %get-tuple-element.76.refs_0_.mine), channel_id=1, source_target_pairs={{0,1},{1,0},{2,3},{3,2},{4,5},{5,4},{6,7},{7,6},{8,9},{9,8},{10,11... | collective-permute-start | bytes 9830408 | tf_op jit(solution)/shard_map/ppermute | solution.py:81
  54.1 28.4 %collective-permute-start.9 = (bf16[768,384]{1,0:T(8,128)(2,1)S(1)}, bf16[768,384]{1,0:T(8,128)(2,1)S(1)}, u32[]{:S(2)}, u32[]{:S(2)}) collective-permute-start(bf16[768,384]{1,0:T(8,128)(2,1)S(1)} %get-tuple-element.73), channel_id=1, source_target_pairs={{0,16},{1,17},{2,18},{3,19},{4,20},{5,21},{6,22},{7,23},{8,24},{9,... | collective-permute-start | bytes 1769480 | tf_op jit(solution)/shard_map/ppermute | solution.py:81
  82.5 19.6 %collective-permute-start.12 = (bf16[528,2048]{1,0:T(8,128)(2,1)S(1)}, bf16[528,2048]{1,0:T(8,128)(2,1)S(1)}, u32[]{:S(2)}, u32[]{:S(2)}) collective-permute-start(bf16[528,2048]{1,0:T(8,128)(2,1)S(1)} %stamp.1.refs_0_), channel_id=1, source_target_pairs={{4,5},{6,7},{9,8},{11,10},{20,21},{22,23},{25,24},{27,26}} | collective-permute-start | bytes 6488072 | tf_op jit(solution)/shard_map/ppermute | solution.py:81
  84.5 20.4 %collective-permute-start.10 = (bf16[768,256]{1,0:T(8,128)(2,1)S(1)}, bf16[768,256]{1,0:T(8,128)(2,1)S(1)}, u32[]{:S(2)}, u32[]{:S(2)}) collective-permute-start(bf16[768,256]{1,0:T(8,128)(2,1)S(1)} %get-tuple-element.75), channel_id=1, source_target_pairs={{0,16},{1,17},{2,18},{3,19},{4,20},{5,21},{6,22},{7,23},{8,24},{9,... | collective-permute-start | bytes 1179656 | tf_op jit(solution)/shard_map/ppermute | solution.py:81
  84.6 20.3 %collective-permute-start.11 = (bf16[768,384]{1,0:T(8,128)(2,1)S(1)}, bf16[768,384]{1,0:T(8,128)(2,1)S(1)}, u32[]{:S(2)}, u32[]{:S(2)}) collective-permute-start(bf16[768,384]{1,0:T(8,128)(2,1)S(1)} %collective-permute-done.9.refs_2_.refs_0_), channel_id=1, source_target_pairs={{0,1},{1,0},{2,3},{3,2},{4,5},{5,4},{6,7},{7,6},{8,9},{9,8},{10,11... | collective-permute-start | bytes 1769480 | tf_op jit(solution)/shard_map/ppermute | solution.py:81
  104.9 31.0 %collective-permute-start.14 = (bf16[528,2048]{1,0:T(8,128)(2,1)S(1)}, bf16[528,2048]{1,0:T(8,128)(2,1)S(1)}, u32[]{:S(2)}, u32[]{:S(2)}) collective-permute-start(bf16[528,2048]{1,0:T(8,128)(2,1)S(1)} %stamp.1.refs_0_), channel_id=1, source_target_pairs={{0,4},{2,6},{4,1},{6,3},{9,12},{11,14},{13,9},{15,11},{16,20},{18,... | collective-permute-start | bytes 6488072 | tf_op jit(solution)/shard_map/ppermute | solution.py:81
  106.2 32.4 %collective-permute-start.15 = (bf16[528,2048]{1,0:T(8,128)(2,1)S(1)}, bf16[528,2048]{1,0:T(8,128)(2,1)S(1)}, u32[]{:S(2)}, u32[]{:S(2)}) collective-permute-start(bf16[528,2048]{1,0:T(8,128)(2,1)S(1)} %stamp.1.refs_0_), channel_id=1, source_target_pairs={{0,2},{2,0},{4,7},{6,5},{9,10},{11,8},{13,15},{15,13},{16,18},{18,... | collective-permute-start | bytes 6488072 | tf_op jit(solution)/shard_map/ppermute | solution.py:81
  107.0 52.6 %collective-permute-start.16 = (bf16[528,2048]{1,0:T(8,128)(2,1)S(1)}, bf16[528,2048]{1,0:T(8,128)(2,1)S(1)}, u32[]{:S(2)}, u32[]{:S(2)}) collective-permute-start(bf16[528,2048]{1,0:T(8,128)(2,1)S(1)} %stamp.1.refs_0_), channel_id=1, source_target_pairs={{0,6},{2,4},{4,3},{6,1},{9,14},{11,12},{13,11},{15,9},{16,22},{18,... | collective-permute-start | bytes 6488072 | tf_op jit(solution)/shard_map/ppermute | solution.py:81
  108.5 27.4 %collective-permute-start.17 = (bf16[768,384]{1,0:T(8,128)(2,1)S(1)}, bf16[768,384]{1,0:T(8,128)(2,1)S(1)}, u32[]{:S(2)}, u32[]{:S(2)}) collective-permute-start(bf16[768,384]{1,0:T(8,128)(2,1)S(1)} %get-tuple-element.83), channel_id=1, source_target_pairs={{0,16},{1,17},{2,18},{3,19},{4,20},{5,21},{6,22},{7,23},{8,24},{9,... | collective-permute-start | bytes 1769480 | tf_op jit(solution)/shard_map/ppermute | solution.py:81
  108.6 8.1 %collective-permute-start.19 = (bf16[768,256]{1,0:T(8,128)(2,1)S(1)}, bf16[768,256]{1,0:T(8,128)(2,1)S(1)}, u32[]{:S(2)}, u32[]{:S(2)}) collective-permute-start(bf16[768,256]{1,0:T(8,128)(2,1)S(1)} %collective-permute-done.10.refs_3_.refs_1_), channel_id=1, source_target_pairs={{0,1},{1,0},{2,3},{3,2},{4,5},{5,4},{6,7},{7,6},{8,9},{9,8},{10,11... | collective-permute-start | bytes 1179656 | tf_op jit(solution)/shard_map/ppermute | solution.py:81
  118.1 43.4 %collective-permute-start.21 = (f32[512,256]{1,0:T(8,128)S(1)}, f32[512,256]{1,0:T(8,128)S(1)}, u32[]{:S(2)}, u32[]{:S(2)}) collective-permute-start(f32[512,256]{1,0:T(8,128)S(1)} %get-tuple-element.89), channel_id=1, source_target_pairs={{0,8},{1,9},{2,10},{3,11},{4,12},{5,13},{6,14},{7,15},{8,0},{9,1},... | collective-permute-start | bytes 1572872 | tf_op jit(solution)/shard_map/ppermute | solution.py:81
  135.9 25.6 %collective-permute-start.22 = (f16[512,384]{1,0:T(8,128)(2,1)S(1)}, f16[512,384]{1,0:T(8,128)(2,1)S(1)}, u32[]{:S(2)}, u32[]{:S(2)}) collective-permute-start(f16[512,384]{1,0:T(8,128)(2,1)S(1)} %convert_element_type.18), channel_id=1, source_target_pairs={{0,8},{1,9},{2,10},{3,11},{4,12},{5,13},{6,14},{7,15},{8,0},{9,1},... | collective-permute-start | bytes 1179656 | tf_op jit(solution)/shard_map/ppermute | solution.py:81
  135.9 25.6 %collective-permute-start.18 = (bf16[768,256]{1,0:T(8,128)(2,1)S(1)}, bf16[768,256]{1,0:T(8,128)(2,1)S(1)}, u32[]{:S(2)}, u32[]{:S(2)}) collective-permute-start(bf16[768,256]{1,0:T(8,128)(2,1)S(1)} %get-tuple-element.85), channel_id=1, source_target_pairs={{0,16},{1,17},{2,18},{3,19},{4,20},{5,21},{6,22},{7,23},{8,24},{9,... | collective-permute-start | bytes 1179656 | tf_op jit(solution)/shard_map/ppermute | solution.py:81
  138.6 22.9 %collective-permute-start.20 = (bf16[768,384]{1,0:T(8,128)(2,1)S(1)}, bf16[768,384]{1,0:T(8,128)(2,1)S(1)}, u32[]{:S(2)}, u32[]{:S(2)}) collective-permute-start(bf16[768,384]{1,0:T(8,128)(2,1)S(1)} %collective-permute-done.17.refs_2_), channel_id=1, source_target_pairs={{0,1},{1,0},{2,3},{3,2},{4,5},{5,4},{6,7},{7,6},{8,9},{9,8},{10,11... | collective-permute-start | bytes 1769480 | tf_op jit(solution)/shard_map/ppermute | solution.py:81
  161.5 1.8 collective-permute-start.23
  162.7 12.9 %collective-permute-start.24 = (f16[512,384]{1,0:T(8,128)(2,1)S(1)}, f16[512,384]{1,0:T(8,128)(2,1)S(1)}, u32[]{:S(2)}, u32[]{:S(2)}) collective-permute-start(f16[512,384]{1,0:T(8,128)(2,1)S(1)} %convert_element_type.20), channel_id=1, source_target_pairs={{0,8},{1,9},{2,10},{3,11},{4,12},{5,13},{6,14},{7,15},{8,0},{9,1},... | collective-permute-start | bytes 1179656 | tf_op jit(solution)/shard_map/ppermute | solution.py:81
  163.9 16.8 %collective-permute-start.25 = (f16[512,256]{1,0:T(8,128)(2,1)S(1)}, f16[512,256]{1,0:T(8,128)(2,1)S(1)}, u32[]{:S(2)}, u32[]{:S(2)}) collective-permute-start(f16[512,256]{1,0:T(8,128)(2,1)S(1)} %convert_element_type.22), channel_id=1, source_target_pairs={{0,8},{1,9},{2,10},{3,11},{4,12},{5,13},{6,14},{7,15},{8,0},{9,1},... | collective-permute-start | bytes 786440 | tf_op jit(solution)/shard_map/ppermute | solution.py:81
  173.1 11.6 %collective-permute-start.26 = (bf16[512,384]{1,0:T(8,128)(2,1)S(1)}, bf16[512,384]{1,0:T(8,128)(2,1)S(1)}, u32[]{:S(2)}, u32[]{:S(2)}) collective-permute-start(bf16[512,384]{1,0:T(8,128)(2,1)S(1)} %attend.3.refs_0_), channel_id=1, source_target_pairs={{1,4},{3,6},{4,1},{6,3},{9,12},{11,14},{12,9},{14,11},{17,20},{19,... | collective-permute-start | bytes 1179656 | tf_op jit(solution)/shard_map/ppermute | solution.py:81
  177.7 9.1 %collective-permute-start.27 = (bf16[512,384]{1,0:T(8,128)(2,1)S(1)}, bf16[512,384]{1,0:T(8,128)(2,1)S(1)}, u32[]{:S(2)}, u32[]{:S(2)}) collective-permute-start(bf16[512,384]{1,0:T(8,128)(2,1)S(1)} %attend.4.refs_1_), channel_id=1, source_target_pairs={{1,4},{3,6},{4,1},{6,3},{9,12},{11,14},{12,9},{14,11},{17,20},{19,... | collective-permute-start | bytes 1179656 | tf_op jit(solution)/shard_map/ppermute | solution.py:81
  182.2 7.7 %collective-permute-start.28 = (bf16[512,256]{1,0:T(8,128)(2,1)S(1)}, bf16[512,256]{1,0:T(8,128)(2,1)S(1)}, u32[]{:S(2)}, u32[]{:S(2)}) collective-permute-start(bf16[512,256]{1,0:T(8,128)(2,1)S(1)} %attend.5.refs_2_), channel_id=1, source_target_pairs={{1,4},{3,6},{4,1},{6,3},{9,12},{11,14},{12,9},{14,11},{17,20},{19,... | collective-permute-start | bytes 786440 | tf_op jit(solution)/shard_map/ppermute | solution.py:81
